TPU v7x, 256 devices: a whole 4x4x8 slice. The times are simulated.
256 devices in a mesh: ex: 16 (over z_lo, y), par: 16 (over z_hi, x, core).
Axes of the slice: x: 4, y: 4, z: 8 (z_hi: 2, z_lo: 4; z = z_hi * 4 + z_lo), core: 2. Of those that a mesh axis runs over, the one named last changes fastest.
Arguments:
- inputs: bfloat16 [8192, 4096], P('ex', 'par'), may hold values from -6 to 6
- w_gate: bfloat16 [4096, 11008], P(None, 'par'), may hold values from -0.09375 to 0.09375
- w_up: bfloat16 [4096, 11008], P(None, 'par'), may hold values from -0.09375 to 0.09375
- out_grads: bfloat16 [8192, 4096], P('ex', 'par'), may hold values from -6 to 6
- proj_hidden: bfloat16 [11008, 64], P('par'), may hold values from -0.0546875 to 0.0546875
- proj_model: bfloat16 [4096, 64], P('par'), may hold values from -0.09375 to 0.09375
Outputs:
- features: float32 [256, 4096], P(('ex', 'par'))
- gram: float32 [4096, 4096], P('par')
All inputs are finite; a program needn't handle non-finite values.
Results may differ from a plain program's by a relative error of at most 0.022.
Values may be sent and summed in bfloat16 or wider, within the bound.
No kernel may reach another device: no remote copies, remote signals or barrier semaphores. Data moves between devices by JAX's collectives and lax.ppermute only.
A program may use at most 64 MiB of HBM per device.

v0:
```python
import jax
import jax.numpy as jnp
from jax import lax
from jax.sharding import PartitionSpec as P

SEQ = 32


def outer_rows(left_rows, right_rows, count, seq_len):
    width_a = left_rows.shape[1]
    width_b = right_rows.shape[1]
    left_three = left_rows.reshape(count, seq_len, width_a)
    right_three = right_rows.reshape(count, seq_len, width_b)
    outer = jnp.einsum("eta,etb->eab", left_three, right_three, precision=lax.Precision.HIGHEST)
    return outer.reshape(count, width_a * width_b) / jnp.sqrt(jnp.float32(seq_len))


def on_device(inputs, w_gate, w_up, out_grads, proj_hidden, proj_model):
    rows = inputs.shape[0]
    seq_len = SEQ
    group = rows // seq_len
    parts = lax.axis_size("par")
    owned = group // parts
    piece = lax.all_gather(inputs, "par", axis=1, tiled=True)
    gate = jnp.dot(piece, w_gate, preferred_element_type=jnp.float32)
    up = jnp.dot(piece, w_up, preferred_element_type=jnp.float32)
    hidden = (jax.nn.silu(gate) * up).astype(jnp.bfloat16)
    left_part = jnp.dot(hidden, proj_hidden, preferred_element_type=jnp.float32)
    right_part = jnp.dot(out_grads, proj_model, preferred_element_type=jnp.float32)
    right_whole = lax.psum(right_part, "par")
    features = lax.psum_scatter(
        outer_rows(left_part, right_whole, owned * lax.axis_size("par"), seq_len),
        "par",
        scatter_dimension=0,
        tiled=True,
    )
    features_bf = features.astype(jnp.bfloat16)
    proj_width = features.shape[1]
    block_cols = proj_width // parts
    col_start = lax.axis_index("par") * block_cols
    examples_all = group * lax.axis_size("ex")
    piece = lax.all_gather(features_bf, "par", axis=0, tiled=True)
    mine = lax.dynamic_slice_in_dim(piece, col_start, block_cols, 1)
    gram_part = jnp.dot(mine.T, piece, preferred_element_type=jnp.float32)
    gram_total = lax.psum(gram_part.astype(jnp.bfloat16), "ex").astype(jnp.float32)
    gram = gram_total / jnp.float32(examples_all)
    return (features, gram)


def solution(mesh):
    placed = (
        P("ex", "par"),
        P(None, "par"),
        P(None, "par"),
        P("ex", "par"),
        P("par", None),
        P("par", None),
    )
    return jax.shard_map(
        on_device,
        mesh=mesh,
        in_specs=placed,
        out_specs=(P(("ex", "par"), None), P("par", None)),
        check_vma=False,
    )
```

profile of v0, /device:TPU:1, one launch (start us, length us, event | category | flops | bytes accessed | tf_op | source)
XLA Modules:
  0.0 645.4 jit_solution(11274061262303141385)
XLA Ops:
  7.2 0.0 copy-start
  7.2 0.0 all-gather.3.cloned.1.call-start
  7.2 0.7 all-gather.3.cloned.1.call-update
  7.9 0.0 all-reduce.5.cloned.1.call-start
  8.0 0.2 copy-done
  8.1 1.7 fusion.7
  9.8 0.0 all-reduce.5.cloned.1.call-update
  9.8 0.0 copy-start.1
  9.8 0.0 all-reduce.9.cloned.1.call-start
  9.9 83.1 %all-gather.3.cloned.1.call-done = bf16[512,4096]{1,0:T(8,128)(2,1)} async-done(((bf16[512,256]{1,0:T(8,128)(2,1)}), bf16[512,4096]{1,0:T(8,128)(2,1)}) %all-gather.3.cloned.1.call-update) | async-done | bytes 4194320 | tf_op jit(solution)/shard_map/all_gather | solution.py:24
  93.0 6.4 fusion.6
  99.4 0.0 copy-done.1
  99.4 0.0 copy-start.2
  99.4 7.5 %fusion.1 = f32[512,64]{1,0:T(8,128)S(1)} fusion(bf16[688,64]{0,1:T(8,128)(2,1)S(1)} %copy-done.1, bf16[512,4096]{1,0:T(8,128)(2,1)} %all-gather.3.cloned.1.call-done, bf16[4096,688]{0,1:T(8,128)(2,1)} %param.8, f32[512,688]{0,1:T(8,128)S(1)} %fusion.6), kind=kOutput, calls=%fused_computation.5 | convolution fusion | flops 2932883456 | bytes 11458560 | tf_op jit(solution)/shard_map/dot_general | solution.py:28
  107.0 160.9 %all-reduce.5.cloned.1.call-done = f32[16,32,64]{2,1,0:T(8,128)} async-done(((f32[16,32,64]{2,1,0:T(8,128)}), f32[16,32,64]{2,1,0:T(8,128)}) %all-reduce.5.cloned.1.call-update) | async-done | bytes 131088 | tf_op jit(solution)/shard_map/psum | solution.py:30
  267.9 2.0 convolution_multiply_fusion.1
  269.9 0.9 div.21
  270.8 0.0 all-reduce.9.cloned.1.call-update
  270.8 0.0 all-reduce.7.cloned.1.call-start
  270.9 0.0 copy-done.2
  270.9 0.6 dynamic-slice.1
  271.6 176.8 %all-reduce.9.cloned.1.call-done = f32[16,4096]{1,0:T(8,128)} async-done(((f32[16,4096]{1,0:T(8,128)}), f32[16,4096]{1,0:T(8,128)}) %all-reduce.9.cloned.1.call-update) | async-done | bytes 262160
  448.4 2.2 convert_bitcast_fusion
  450.5 29.2 %all-gather = bf16[16,1,4096]{2,1,0:T(2,128)(2,1)S(1)} all-gather(bf16[1,1,4096]{2,1,0:T(2,128)(2,1)S(1)} %get-tuple-element.2), channel_id=1, replica_groups=mesh['ex'=16,'par'=16] {'par'}, dimensions={0}, use_global_device_ids=true | all-gather | bytes 139264 | tf_op jit(solution)/shard_map/all_gather | solution.py:42
  479.7 2.0 convolution_convert_fusion
  481.8 0.0 all-reduce.7.cloned.1.call-update
  481.8 153.0 %all-reduce.7.cloned.1.call-done = bf16[256,4096]{1,0:T(8,128)(2,1)} async-done(((bf16[256,4096]{1,0:T(8,128)(2,1)}), bf16[256,4096]{1,0:T(8,128)(2,1)}) %all-reduce.7.cloned.1.call-update) | async-done | bytes 2097168 | tf_op jit(solution)/shard_map/psum | solution.py:45
  634.8 4.1 convert_multiply_fusion
  (1 shorter events, 0.0 us)
Async XLA Ops:
  7.2 1.0 copy-start
  7.2 85.8 %all-gather.3.cloned.1.call-start = ((), (), s32[]{:S(2)}) async-start(), calls=%async_computation | async-start | bytes 4456448 | tf_op jit(solution)/shard_map/all_gather | solution.py:24
  7.9 260.0 %all-reduce.5.cloned.1.call-start = ((), (), s32[]{:S(2)}) async-start(), calls=%async_computation.1 | async-start | bytes 524288 | tf_op jit(solution)/shard_map/psum | solution.py:30
  9.8 89.6 %copy-start.1 = (bf16[688,64]{0,1:T(8,128)(2,1)S(1)}, bf16[688,64]{0,1:T(8,128)(2,1)}, u32[]{:S(2)}) copy-start(bf16[688,64]{0,1:T(8,128)(2,1)} %param.10) | copy-start | bytes 264196
  9.8 438.5 %all-reduce.9.cloned.1.call-start = ((), (), s32[]{:S(2)}) async-start(), calls=%async_computation.3 | async-start | bytes 524288
  99.4 171.5 %copy-start.2 = (u32[256]{0:T(256)S(1)}, u32[256]{0:T(256)}, u32[]{:S(2)}) copy-start(u32[256]{0:T(256)} %constant.22) | copy-start | bytes 3076
  270.8 364.0 %all-reduce.7.cloned.1.call-start = ((), (), s32[]{:S(2)}) async-start(), calls=%async_computation.2 | async-start | bytes 4194304 | tf_op jit(solution)/shard_map/psum | solution.py:45
Sparse Core Ops, SparseCore 0:
  10.6 82.3 all-gather.2
  96.2 171.6 all-reduce.4
  271.3 177.0 all-reduce.8
  481.9 152.8 all-reduce.6
where the time goes:
time: 654 us; the launch traced here: 645 us
  waiting for transfers between devices  575 us (88%)
  blocking collectives  29.2 us (4%)
  matrix products  19.7 us (3%)
  between operations  13.8 us (2%)
    unnamed x5, waiting for transfers between devices  178 us
    psum x1, waiting for transfers between devices, on_device(): right_whole = lax.psum(right_part, 'par')  161 us
    psum x1, waiting for transfers between devices, on_device(): lax.psum(gram_part.astype(jnp.bfloat16), 'ex').astype(jnp.float32)  153 us
    all_gather x1, waiting for transfers between devices, on_device(): piece = lax.all_gather(inputs, 'par', axis=1, tiled=True)  83.1 us
    all_gather x1, blocking collectives, on_device(): piece = lax.all_gather(features_bf, 'par', axis=0, tiled=True)  29.2 us
  transfers between devices with their start and end apart: 4, of which 4 were waited for; matrix products, arithmetic and copies ran while one was open for 3% of the time, Pallas kernels for 0%

commit v1 on v0

v1 whole, which is shorter than its diff:
```python
import functools

import jax
import jax.numpy as jnp
from jax import lax
from jax.experimental import pallas as pl
from jax.experimental.pallas import tpu as pltpu
from jax.sharding import PartitionSpec as P

SEQ = 32
BOTH = ("ex", "par")


def pairs(move):
    def index(z, y, x, core):
        z, y, x = z % 8, y % 4, x % 4
        return ((z % 4) * 4 + y) * 16 + (z // 4) * 8 + x * 2 + core

    return [
        (index(z, y, x, c), index(*move(z, y, x, c)))
        for z in range(8)
        for y in range(4)
        for x in range(4)
        for c in range(2)
    ]


def send(value, move):
    return lax.ppermute(value, BOTH, pairs(move))


def shift_x(n):
    return lambda z, y, x, c: (z, y, x + n, c)


def shift_z(n):
    return lambda z, y, x, c: (z + n, y, x, c)


def other_core(z, y, x, c):
    return (z, y, x, 1 - c)


def shift_first(n):
    return lambda z, y, x, c: (z, y + n, x, c) if c == 0 else (z, y, x + n, c)


def shift_second(n):
    return lambda z, y, x, c: (z, y + n, x, c) if c == 1 else (z, y, x + n, c)


def hidden_part(first, rows, units, *refs):
    if first:
        order, side, *blocks = refs[:10]
        gate_w, up_w, gate_out, up_out, held, sems = refs[10:]
    else:
        order, side, *blocks = refs[:10]
        gate_w, up_w, gate_in, up_in, proj, right, out, held, gate_acc, up_acc, sems = refs[10:]
        gate_out, up_out = gate_acc, up_acc
    step = pl.program_id(0)

    def copy(j, s):
        lanes = pl.ds(pl.multiple_of((side[0] if s == 0 else 1 - side[0]) * 256, 256), 256)
        return pltpu.make_async_copy(blocks[2 * j + s], held.at[j, :, lanes], sems.at[j, s])

    @pl.when(step == 0)
    def _():
        for j in range(4):
            for s in range(2):
                copy(j, s).start()

    for j in range(4):

        @pl.when(step == j)
        def _(j=j):
            copy(j, 0).wait()
            copy(j, 1).wait()

    block = held[step]
    dims = (((1,), (1,)), ((), ()))
    gate = lax.dot_general(gate_w[...], block, dims, preferred_element_type=jnp.float32)
    up = lax.dot_general(up_w[...], block, dims, preferred_element_type=jnp.float32)

    @pl.when(step == 0)
    def _():
        if first:
            gate_out[...] = gate
            up_out[...] = up
        else:
            gate_out[...] = gate + gate_in[...]
            up_out[...] = up + up_in[...]

    @pl.when(step > 0)
    def _():
        gate_out[...] += gate
        up_out[...] += up

    if not first:

        @pl.when(step == 3)
        def _():
            value = gate_out[...]
            hidden = (value / (1.0 + jnp.exp(-value)) * up_out[...]).astype(jnp.bfloat16)
            left = jnp.dot(proj[...], hidden, preferred_element_type=jnp.float32)
            out[:, :64] = left.T
            out[:, 64:] = right[...]


def call_part(first, order, side, blocks, w_gate, w_up, rest):
    rows, units = blocks[0].shape[0], w_gate.shape[0]
    weight = pl.BlockSpec((units, 512), lambda k, order, side: (0, order[k]))
    whole = lambda shape: pl.BlockSpec(shape, lambda k, order, side: (0,) * len(shape))
    accs = [jax.ShapeDtypeStruct((units, rows), jnp.float32)] * 2
    out = jax.ShapeDtypeStruct((rows, 128), jnp.float32)
    scratch = [pltpu.VMEM((4, rows, 512), jnp.bfloat16)]
    if not first:
        scratch += [pltpu.VMEM((units, rows), jnp.float32)] * 2
    scratch += [pltpu.SemaphoreType.DMA((4, 2))]
    flops = 2 * 2 * rows * units * 2048
    return pl.pallas_call(
        functools.partial(hidden_part, first, rows, units),
        out_shape=accs if first else out,
        grid_spec=pltpu.PrefetchScalarGridSpec(
            num_scalar_prefetch=2,
            grid=(4,),
            in_specs=[pl.BlockSpec(memory_space=pl.ANY)] * 8 + [weight, weight] + [whole(r.shape) for r in rest],
            out_specs=[whole(a.shape) for a in accs] if first else whole(out.shape),
            scratch_shapes=scratch,
        ),
        compiler_params=pltpu.CompilerParams(vmem_limit_bytes=40 * 1024 * 1024),
        cost_estimate=pl.CostEstimate(flops=flops, bytes_accessed=10_000_000, transcendentals=0),
        name="first_half" if first else "second_half",
    )(order, side, *blocks, w_gate, w_up, *rest)


def on_device(inputs, w_gate, w_up, out_grads, proj_hidden, proj_model):
    rows = inputs.shape[0]
    par = lax.axis_index("par")
    z_hi, x, core = par // 8, (par // 2) % 4, par % 2
    w_gate, w_up, proj = w_gate.T, w_up.T, proj_hidden.T

    far = send(inputs, shift_z(4))
    near = [inputs] + [send(inputs, shift_x(n)) for n in (1, 3, 2)]
    near_all = [b for n in near for b in (n, send(n, other_core))]
    far = [far] + [send(far, shift_x(n)) for n in (1, 3, 2)]
    far_all = [b for n in far for b in (n, send(n, other_core))]
    from_x = jnp.stack([x, (x + 3) % 4, (x + 1) % 4, (x + 2) % 4]).astype(jnp.int32)
    side = core.astype(jnp.int32).reshape(1)

    right = jnp.dot(out_grads, proj_model, preferred_element_type=jnp.float32)
    accs = call_part(True, z_hi * 4 + from_x, side, near_all, w_gate, w_up, [])
    both = call_part(False, (1 - z_hi) * 4 + from_x, side, far_all, w_gate, w_up, [*accs, proj, right])

    both = both.reshape(2, 4, 2, SEQ, 128)
    pick = lambda v, i, axis: lax.dynamic_index_in_dim(v, i, axis, keepdims=False)
    both = pick(both, core, 2) + send(pick(both, 1 - core, 2), other_core)
    part = pick(both, x, 1)
    for n in (1, 3, 2):
        part = part + send(pick(both, (x + n) % 4, 1), shift_x(n))

    part = part.astype(jnp.bfloat16)
    along = [part] + [send(part, shift_z(n)) for n in range(1, 8)]
    total = jnp.stack([along[n].astype(jnp.float32) + along[n + 4].astype(jnp.float32) for n in range(4)])
    total = total.reshape(8, SEQ, 128)
    outer = jnp.einsum("eta,etb->eab", total[..., :64], total[..., 64:], precision=lax.Precision.HIGHEST)
    feats = outer.reshape(8, 4096) / jnp.sqrt(jnp.float32(SEQ))
    features = lax.dynamic_slice_in_dim(feats, z_hi, 1, 0)

    feats = feats.astype(jnp.bfloat16)
    feats = jnp.concatenate([feats] + [send(feats, shift_first(n)) for n in (1, 3, 2)])
    feats = jnp.concatenate([feats] + [send(feats, shift_second(n)) for n in (1, 3, 2)])
    feats = jnp.concatenate([feats, send(feats, other_core)])
    mine = lax.dynamic_slice_in_dim(feats, par * 256, 256, 1)
    gram = jnp.dot(mine.T, feats, preferred_element_type=jnp.float32) * (1.0 / 256)
    return (features, gram)


def solution(mesh):
    placed = (
        P("ex", "par"),
        P(None, "par"),
        P(None, "par"),
        P("ex", "par"),
        P("par", None),
        P("par", None),
    )
    return jax.shard_map(
        on_device,
        mesh=mesh,
        in_specs=placed,
        out_specs=(P(("ex", "par"), None), P("par", None)),
        check_vma=False,
    )
```

time: 654 us -> 114 us (0.17); the launches traced: 645 us -> 114 us
  waiting for transfers between devices: 575 us -> 26.4 us
  starting transfers between devices: 0.16 us -> 57.6 us
  blocking collectives: 29.2 us -> 0 us
  matrix products: 19.7 us -> 4.42 us
  Pallas kernels: 0 us -> 15.1 us
  between operations: 13.8 us -> 0.84 us
  local copies, waits for them, and re-layouts: 1.73 us -> 8.56 us
    psum x2 -> x0, waiting for transfers between devices: 314 us -> none  [the longest x1 161 us: on_device(): right_whole = lax.psum(right_part, 'par')]
    unnamed x5 -> x0, waiting for transfers between devices: 178 us -> none
    all_gather x1 -> x0, waiting for transfers between devices: 83.1 us -> none  [on_device(): piece = lax.all_gather(inputs, 'par', axis=1, tiled=True)]
    ppermute x0 -> x33, starting transfers between devices: none -> 57.6 us  [send(): return lax.ppermute(value, BOTH, pairs(move))]
    all_gather x1 -> x0, blocking collectives: 29.2 us -> none  [on_device(): piece = lax.all_gather(features_bf, 'par', axis=0, tiled=True)]
    ppermute x0 -> x33, waiting for transfers between devices: none -> 26.4 us  [send(): return lax.ppermute(value, BOTH, pairs(move))]
    dot_general x5 -> x3, matrix products: 19.7 us -> 4.42 us  [the longest x1 2.78 us: on_device(): jnp.dot(mine.T, feats, preferred_element_type=jnp.float32) * (1.0 / 256)]
    pallas_call x0 -> x2, Pallas kernels: none -> 15.1 us  [call_part(): pl.pallas_call(functools.partial(hidden_part, first, rows, units), out_sh...]
  transfers between devices with their start and end apart: 4 -> 33, of which waited for: 4 -> 18; matrix products, arithmetic and copies ran while one was open for 3% -> 4% of each run, Pallas kernels for 0% -> 6%
where the time goes in v1:
time: 114 us
  starting transfers between devices  57.6 us (51%)
  waiting for transfers between devices  26.4 us (23%)
  Pallas kernels  15.1 us (13%)
  local copies, waits for them, and re-layouts  8.56 us (8%)
  matrix products  4.42 us (4%)
    ppermute x33, starting transfers between devices, send(): return lax.ppermute(value, BOTH, pairs(move))  57.6 us
    ppermute x33, waiting for transfers between devices, send(): return lax.ppermute(value, BOTH, pairs(move))  26.4 us
    pallas_call x2, Pallas kernels, call_part(): pl.pallas_call(functools.partial(hidden_part, first, rows, units), out_sh...  15.1 us
    unnamed x16, local copies, waits for them, and re-layouts  6.96 us
    dot_general x1, matrix products, on_device(): jnp.dot(mine.T, feats, preferred_element_type=jnp.float32) * (1.0 / 256)  2.78 us
  transfers between devices with their start and end apart: 33, of which 18 were waited for; matrix products, arithmetic and copies ran while one was open for 4% of the time, Pallas kernels for 6%

profile of v1, /device:TPU:1, one launch (start us, length us, event | category | flops | bytes accessed | tf_op | source)
XLA Modules:
  0.0 113.7 jit_solution(10256085351787677930)
XLA Ops:
  0.6 7.8 %collective-permute-start = (bf16[512,256]{1,0:T(8,128)(2,1)}, bf16[512,256]{1,0:T(8,128)(2,1)S(1)}, u32[]{:S(2)}, u32[]{:S(2)}) collective-permute-start(bf16[512,256]{1,0:T(8,128)(2,1)} %refs_2_.1), channel_id=1, source_target_pairs={{0,8},{1,9},{2,10},{3,11},{4,12},{5,13},{6,14},{7,15},{16,24},{17,... | collective-permute-start | bytes 786440 | tf_op jit(solution)/shard_map/ppermute | solution.py:29
  8.5 1.0 collective-permute-start.8
  9.4 1.2 %collective-permute-start.9 = (bf16[512,256]{1,0:T(8,128)(2,1)}, bf16[512,256]{1,0:T(8,128)(2,1)S(1)}, u32[]{:S(2)}, u32[]{:S(2)}) collective-permute-start(bf16[512,256]{1,0:T(8,128)(2,1)} %refs_2_.1), channel_id=1, source_target_pairs={{0,2},{1,3},{2,4},{3,5},{4,6},{5,7},{6,0},{7,1},{16,18},{17,19},{1... | collective-permute-start | bytes 786440 | tf_op jit(solution)/shard_map/ppermute | solution.py:29
  10.6 1.5 %collective-permute-start.11 = (bf16[512,256]{1,0:T(8,128)(2,1)}, bf16[512,256]{1,0:T(8,128)(2,1)S(1)}, u32[]{:S(2)}, u32[]{:S(2)}) collective-permute-start(bf16[512,256]{1,0:T(8,128)(2,1)} %refs_2_.1), channel_id=1, source_target_pairs={{0,6},{1,7},{2,0},{3,1},{4,2},{5,3},{6,4},{7,5},{16,22},{17,23},{1... | collective-permute-start | bytes 786440 | tf_op jit(solution)/shard_map/ppermute | solution.py:29
  12.1 1.5 %collective-permute-start.13 = (bf16[512,256]{1,0:T(8,128)(2,1)}, bf16[512,256]{1,0:T(8,128)(2,1)S(1)}, u32[]{:S(2)}, u32[]{:S(2)}) collective-permute-start(bf16[512,256]{1,0:T(8,128)(2,1)} %refs_2_.1), channel_id=1, source_target_pairs={{0,4},{1,5},{2,6},{3,7},{4,0},{5,1},{6,2},{7,3},{16,20},{17,21},{1... | collective-permute-start | bytes 786440 | tf_op jit(solution)/shard_map/ppermute | solution.py:29
  14.2 2.7 %collective-permute-start.2 = (bf16[512,256]{1,0:T(8,128)(2,1)S(1)}, bf16[512,256]{1,0:T(8,128)(2,1)S(1)}, u32[]{:S(2)}, u32[]{:S(2)}) collective-permute-start(bf16[512,256]{1,0:T(8,128)(2,1)S(1)} %collective-permute-done.refs_2_), channel_id=1, source_target_pairs={{0,2},{1,3},{2,4},{3,5},{4,6},{5,7},{6,0},{7,1},{16,18},{17,19},{1... | collective-permute-start | bytes 786440 | tf_op jit(solution)/shard_map/ppermute | solution.py:29
  17.0 1.3 %collective-permute-start.4 = (bf16[512,256]{1,0:T(8,128)(2,1)S(1)}, bf16[512,256]{1,0:T(8,128)(2,1)S(1)}, u32[]{:S(2)}, u32[]{:S(2)}) collective-permute-start(bf16[512,256]{1,0:T(8,128)(2,1)S(1)} %collective-permute-done.refs_2_), channel_id=1, source_target_pairs={{0,6},{1,7},{2,0},{3,1},{4,2},{5,3},{6,4},{7,5},{16,22},{17,23},{1... | collective-permute-start | bytes 786440 | tf_op jit(solution)/shard_map/ppermute | solution.py:29
  18.8 1.6 %collective-permute-start.6 = (bf16[512,256]{1,0:T(8,128)(2,1)S(1)}, bf16[512,256]{1,0:T(8,128)(2,1)S(1)}, u32[]{:S(2)}, u32[]{:S(2)}) collective-permute-start(bf16[512,256]{1,0:T(8,128)(2,1)S(1)} %collective-permute-done.refs_2_), channel_id=1, source_target_pairs={{0,4},{1,5},{2,6},{3,7},{4,0},{5,1},{6,2},{7,3},{16,20},{17,21},{1... | collective-permute-start | bytes 786440 | tf_op jit(solution)/shard_map/ppermute | solution.py:29
  20.3 3.7 %collective-permute-start.10 = (bf16[512,256]{1,0:T(8,128)(2,1)S(1)}, bf16[512,256]{1,0:T(8,128)(2,1)S(1)}, u32[]{:S(2)}, u32[]{:S(2)}) collective-permute-start(bf16[512,256]{1,0:T(8,128)(2,1)S(1)} %collective-permute-done.9.refs_4_), channel_id=1, source_target_pairs={{0,1},{1,0},{2,3},{3,2},{4,5},{5,4},{6,7},{7,6},{16,17},{17,16},{1... | collective-permute-start | bytes 786440 | tf_op jit(solution)/shard_map/ppermute | solution.py:29
  24.1 1.3 %collective-permute-done.13.refs_8_ = bf16[512,256]{1,0:T(8,128)(2,1)S(1)} collective-permute-done((bf16[512,256]{1,0:T(8,128)(2,1)}, bf16[512,256]{1,0:T(8,128)(2,1)S(1)}, u32[]{:S(2)}, u32[]{:S(2)}) %collective-permute-start.13) | collective-permute-done | bytes 262176 | tf_op jit(solution)/shard_map/ppermute | solution.py:29
  25.4 1.2 %collective-permute-start.12 = (bf16[512,256]{1,0:T(8,128)(2,1)S(1)}, bf16[512,256]{1,0:T(8,128)(2,1)S(1)}, u32[]{:S(2)}, u32[]{:S(2)}) collective-permute-start(bf16[512,256]{1,0:T(8,128)(2,1)S(1)} %collective-permute-done.11.refs_6_), channel_id=1, source_target_pairs={{0,1},{1,0},{2,3},{3,2},{4,5},{5,4},{6,7},{7,6},{16,17},{17,16},{1... | collective-permute-start | bytes 786440 | tf_op jit(solution)/shard_map/ppermute | solution.py:29
  26.6 3.2 %collective-permute-done.2.refs_4_ = bf16[512,256]{1,0:T(8,128)(2,1)S(1)} collective-permute-done((bf16[512,256]{1,0:T(8,128)(2,1)S(1)}, bf16[512,256]{1,0:T(8,128)(2,1)S(1)}, u32[]{:S(2)}, u32[]{:S(2)}) %collective-permute-start.2) | collective-permute-done | bytes 262176 | tf_op jit(solution)/shard_map/ppermute | solution.py:29
  29.8 1.3 %collective-permute-start.14 = (bf16[512,256]{1,0:T(8,128)(2,1)S(1)}, bf16[512,256]{1,0:T(8,128)(2,1)S(1)}, u32[]{:S(2)}, u32[]{:S(2)}) collective-permute-start(bf16[512,256]{1,0:T(8,128)(2,1)S(1)} %collective-permute-done.13.refs_8_), channel_id=1, source_target_pairs={{0,1},{1,0},{2,3},{3,2},{4,5},{5,4},{6,7},{7,6},{16,17},{17,16},{1... | collective-permute-start | bytes 786440 | tf_op jit(solution)/shard_map/ppermute | solution.py:29
  31.1 1.0 fusion.7.refs_15_
  32.1 4.5 %collective-permute-done.6.refs_8_ = bf16[512,256]{1,0:T(8,128)(2,1)S(1)} collective-permute-done((bf16[512,256]{1,0:T(8,128)(2,1)S(1)}, bf16[512,256]{1,0:T(8,128)(2,1)S(1)}, u32[]{:S(2)}, u32[]{:S(2)}) %collective-permute-start.6) | collective-permute-done | bytes 262176 | tf_op jit(solution)/shard_map/ppermute | solution.py:29
  36.7 0.8 collective-permute-start.3
  38.0 2.6 %copy-done.1 = bf16[4096,688]{0,1:T(8,128)(2,1)S(1)} copy-done((bf16[4096,688]{0,1:T(8,128)(2,1)S(1)}, bf16[4096,688]{0,1:T(8,128)(2,1)}, u32[]{:S(2)}) %copy-start.1) | copy-done | bytes 5636120
  40.6 0.9 copy-done.3
  41.5 7.3 %first_half.1 = (f32[688,512]{1,0:T(8,128)S(1)}, f32[688,512]{1,0:T(8,128)S(1)}) custom-call(s32[4]{0:T(128)S(1)} %get-tuple-element.8.refs_0_, s32[1]{0:T(128)} %bitcast.4.refs_1_, bf16[512,256]{1,0:T(8,128)(2,1)S(1)} %copy-done.3, bf16[512,256]{1,0:T(8,128)(2,1)S(1)} %collective-permute-done.8.refs_3_, ...), custom_call_target="tpu_custom_call" | custom-call | flops 2885681152 | bytes 10000000 | tf_op jit(solution)/shard_map/first_half/pallas_call | solution.py:120
  48.9 7.8 %second_half.1 = f32[512,128]{1,0:T(8,128)S(1)} custom-call(s32[4]{0:T(128)S(1)} %broadcast_add_fusion.1.refs_0_, s32[1]{0:T(128)} %bitcast.4.refs_1_, bf16[512,256]{1,0:T(8,128)(2,1)S(1)} %collective-permute-done.refs_2_, bf16[512,256]{1,0:T(8,128)(2,1)S(1)} %collective-permute-done.1.refs_3_, bf16[512,256]{1,0:T(8,128)(2,1)S(1)} %collective-permute-done.2.refs_4_, ...), custom_call_target="tpu_custom_call" | custom-call | flops 2885681152 | bytes 10000000 | tf_op jit(solution)/shard_map/second_half/pallas_call | solution.py:120
  57.1 1.1 collective-permute-done.15
  58.8 2.7 %collective-permute-start.17 = (f32[2,32,128]{2,1,0:T(8,128)S(1)}, f32[2,32,128]{2,1,0:T(8,128)S(1)}, u32[]{:S(2)}, u32[]{:S(2)}) collective-permute-start(f32[2,32,128]{2,1,0:T(8,128)S(1)} %get-tuple-element.18), channel_id=1, source_target_pairs={{0,6},{1,7},{2,0},{3,1},{4,2},{5,3},{6,4},{7,5},{16,22},{17,23},{1... | collective-permute-start | bytes 98312 | tf_op jit(solution)/shard_map/ppermute | solution.py:29
  61.5 1.0 collective-permute-done.18
  62.8 2.7 %collective-permute-done.16 = f32[2,32,128]{2,1,0:T(8,128)S(1)} collective-permute-done((f32[2,32,128]{2,1,0:T(8,128)S(1)}, f32[2,32,128]{2,1,0:T(8,128)S(1)}, u32[]{:S(2)}, u32[]{:S(2)}) %collective-permute-start.16) | collective-permute-done | bytes 32800 | tf_op jit(solution)/shard_map/ppermute | solution.py:29
  65.5 0.7 collective-permute-start.19
  66.2 3.4 %collective-permute-start.25 = (bf16[2,32,128]{2,1,0:T(8,128)(2,1)S(1)}, bf16[2,32,128]{2,1,0:T(8,128)(2,1)S(1)}, u32[]{:S(2)}, u32[]{:S(2)}) collective-permute-start(bf16[2,32,128]{2,1,0:T(8,128)(2,1)S(1)} %fusion.5), channel_id=1, source_target_pairs={{0,200},{1,201},{2,202},{3,203},{4,204},{5,205},{6,206},{7,207},{1... | collective-permute-start | bytes 49160 | tf_op jit(solution)/shard_map/ppermute | solution.py:29
  69.7 3.0 %collective-permute-start.24 = (bf16[2,32,128]{2,1,0:T(8,128)(2,1)S(1)}, bf16[2,32,128]{2,1,0:T(8,128)(2,1)S(1)}, u32[]{:S(2)}, u32[]{:S(2)}) collective-permute-start(bf16[2,32,128]{2,1,0:T(8,128)(2,1)S(1)} %fusion.5), channel_id=1, source_target_pairs={{0,192},{1,193},{2,194},{3,195},{4,196},{5,197},{6,198},{7,199},{1... | collective-permute-start | bytes 49160 | tf_op jit(solution)/shard_map/ppermute | solution.py:29
  72.6 1.6 %collective-permute-start.23 = (bf16[2,32,128]{2,1,0:T(8,128)(2,1)S(1)}, bf16[2,32,128]{2,1,0:T(8,128)(2,1)S(1)}, u32[]{:S(2)}, u32[]{:S(2)}) collective-permute-start(bf16[2,32,128]{2,1,0:T(8,128)(2,1)S(1)} %fusion.5), channel_id=1, source_target_pairs={{0,136},{1,137},{2,138},{3,139},{4,140},{5,141},{6,142},{7,143},{1... | collective-permute-start | bytes 49160 | tf_op jit(solution)/shard_map/ppermute | solution.py:29
  74.2 0.8 collective-permute-start.22
  75.0 1.6 %collective-permute-start.21 = (bf16[2,32,128]{2,1,0:T(8,128)(2,1)S(1)}, bf16[2,32,128]{2,1,0:T(8,128)(2,1)S(1)}, u32[]{:S(2)}, u32[]{:S(2)}) collective-permute-start(bf16[2,32,128]{2,1,0:T(8,128)(2,1)S(1)} %fusion.5), channel_id=1, source_target_pairs={{0,72},{1,73},{2,74},{3,75},{4,76},{5,77},{6,78},{7,79},{16,88},{1... | collective-permute-start | bytes 49160 | tf_op jit(solution)/shard_map/ppermute | solution.py:29
  76.6 2.5 %collective-permute-start.20 = (bf16[2,32,128]{2,1,0:T(8,128)(2,1)S(1)}, bf16[2,32,128]{2,1,0:T(8,128)(2,1)S(1)}, u32[]{:S(2)}, u32[]{:S(2)}) collective-permute-start(bf16[2,32,128]{2,1,0:T(8,128)(2,1)S(1)} %fusion.5), channel_id=1, source_target_pairs={{0,64},{1,65},{2,66},{3,67},{4,68},{5,69},{6,70},{7,71},{16,80},{1... | collective-permute-start | bytes 49160 | tf_op jit(solution)/shard_map/ppermute | solution.py:29
  79.5 1.0 collective-permute-done.20
  80.5 0.7 convolution_multiply_fusion.1
  82.0 2.7 %collective-permute-start.27 = (bf16[8,4096]{1,0:T(8,128)(2,1)S(1)}, bf16[8,4096]{1,0:T(8,128)(2,1)S(1)}, u32[]{:S(2)}, u32[]{:S(2)}) collective-permute-start(bf16[8,4096]{1,0:T(8,128)(2,1)S(1)} %get-tuple-element.7), channel_id=1, source_target_pairs={{0,48},{1,7},{2,50},{3,1},{4,52},{5,3},{6,54},{7,5},{16,0},{17,23}... | collective-permute-start | bytes 196616 | tf_op jit(solution)/shard_map/ppermute | solution.py:29
  84.7 1.6 %collective-permute-done.26 = bf16[8,4096]{1,0:T(8,128)(2,1)S(1)} collective-permute-done((bf16[8,4096]{1,0:T(8,128)(2,1)S(1)}, bf16[8,4096]{1,0:T(8,128)(2,1)S(1)}, u32[]{:S(2)}, u32[]{:S(2)}) %collective-permute-start.26) | collective-permute-done | bytes 65568 | tf_op jit(solution)/shard_map/ppermute | solution.py:29
  86.6 2.7 %collective-permute-done.28 = bf16[8,4096]{1,0:T(8,128)(2,1)S(1)} collective-permute-done((bf16[8,4096]{1,0:T(8,128)(2,1)S(1)}, bf16[8,4096]{1,0:T(8,128)(2,1)S(1)}, u32[]{:S(2)}, u32[]{:S(2)}) %collective-permute-start.28) | collective-permute-done | bytes 65568 | tf_op jit(solution)/shard_map/ppermute | solution.py:29
  89.3 1.4 %collective-permute-start.29 = (bf16[32,4096]{1,0:T(8,128)(2,1)S(1)}, bf16[32,4096]{1,0:T(8,128)(2,1)S(1)}, u32[]{:S(2)}, u32[]{:S(2)}) collective-permute-start(bf16[32,4096]{1,0:T(8,128)(2,1)S(1)} %pad_maximum_fusion), channel_id=1, source_target_pairs={{0,2},{1,17},{2,4},{3,19},{4,6},{5,21},{6,0},{7,23},{16,18},{17,33... | collective-permute-start | bytes 786440 | tf_op jit(solution)/shard_map/ppermute | solution.py:29
  90.7 1.5 %collective-permute-start.30 = (bf16[32,4096]{1,0:T(8,128)(2,1)S(1)}, bf16[32,4096]{1,0:T(8,128)(2,1)S(1)}, u32[]{:S(2)}, u32[]{:S(2)}) collective-permute-start(bf16[32,4096]{1,0:T(8,128)(2,1)S(1)} %pad_maximum_fusion), channel_id=1, source_target_pairs={{0,6},{1,49},{2,0},{3,51},{4,2},{5,53},{6,4},{7,55},{16,22},{17,1}... | collective-permute-start | bytes 786440 | tf_op jit(solution)/shard_map/ppermute | solution.py:29
  92.2 1.6 %collective-permute-start.31 = (bf16[32,4096]{1,0:T(8,128)(2,1)S(1)}, bf16[32,4096]{1,0:T(8,128)(2,1)S(1)}, u32[]{:S(2)}, u32[]{:S(2)}) collective-permute-start(bf16[32,4096]{1,0:T(8,128)(2,1)S(1)} %pad_maximum_fusion), channel_id=1, source_target_pairs={{0,4},{1,33},{2,6},{3,35},{4,0},{5,37},{6,2},{7,39},{16,20},{17,49... | collective-permute-start | bytes 786440 | tf_op jit(solution)/shard_map/ppermute | solution.py:29
  95.7 0.9 collective-permute-done.29
  96.6 0.7 constant_dynamic-update-slice_fusion.2
  97.3 1.7 %collective-permute-done.30 = bf16[32,4096]{1,0:T(8,128)(2,1)S(1)} collective-permute-done((bf16[32,4096]{1,0:T(8,128)(2,1)S(1)}, bf16[32,4096]{1,0:T(8,128)(2,1)S(1)}, u32[]{:S(2)}, u32[]{:S(2)}) %collective-permute-start.30) | collective-permute-done | bytes 262176 | tf_op jit(solution)/shard_map/ppermute | solution.py:29
  99.0 0.7 constant_dynamic-update-slice_fusion.1
  99.8 0.8 collective-permute-done.31
  100.5 0.7 constant_dynamic-update-slice_fusion
  101.3 7.0 %collective-permute-start.32 = (bf16[128,4096]{1,0:T(8,128)(2,1)}, bf16[128,4096]{1,0:T(8,128)(2,1)S(1)}, u32[]{:S(2)}, u32[]{:S(2)}) collective-permute-start(bf16[128,4096]{1,0:T(8,128)(2,1)} %get-tuple-element.10), channel_id=1, source_target_pairs={{0,1},{1,0},{2,3},{3,2},{4,5},{5,4},{6,7},{7,6},{16,17},{17,16},{1... | collective-permute-start | bytes 3145736 | tf_op jit(solution)/shard_map/ppermute | solution.py:29
  108.9 1.9 %collective-permute-done.32 = bf16[128,4096]{1,0:T(8,128)(2,1)S(1)} collective-permute-done((bf16[128,4096]{1,0:T(8,128)(2,1)}, bf16[128,4096]{1,0:T(8,128)(2,1)S(1)}, u32[]{:S(2)}, u32[]{:S(2)}) %collective-permute-start.32) | collective-permute-done | bytes 1048608 | tf_op jit(solution)/shard_map/ppermute | solution.py:29
  110.9 2.8 %convolution_multiply_fusion = f32[256,4096]{1,0:T(8,128)} fusion(bf16[256,4096]{1,0:T(8,128)(2,1)S(1)} %constant_dynamic-update-slice_fusion.7, s32[]{:T(128)S(6)} %select_n.76), kind=kOutput, calls=%fused_computation | convolution fusion | flops 537919488 | bytes 6422532 | tf_op jit(solution)/shard_map/dot_general | solution.py:174
  (56 shorter events, 7.1 us)
Async XLA Ops:
  0.6 30.4 %copy-start = (bf16[512,256]{1,0:T(8,128)(2,1)S(1)}, bf16[512,256]{1,0:T(8,128)(2,1)}, u32[]{:S(2)}) copy-start(bf16[512,256]{1,0:T(8,128)(2,1)} %param.9) | copy-start | bytes 786436
  0.6 13.5 %collective-permute-start = (bf16[512,256]{1,0:T(8,128)(2,1)}, bf16[512,256]{1,0:T(8,128)(2,1)S(1)}, u32[]{:S(2)}, u32[]{:S(2)}) collective-permute-start(bf16[512,256]{1,0:T(8,128)(2,1)} %refs_2_.1), channel_id=1, source_target_pairs={{0,8},{1,9},{2,10},{3,11},{4,12},{5,13},{6,14},{7,15},{16,24},{17,... | collective-permute-start | bytes 786440 | tf_op jit(solution)/shard_map/ppermute | solution.py:29
  8.5 8.5 %collective-permute-start.8 = (bf16[512,256]{1,0:T(8,128)(2,1)}, bf16[512,256]{1,0:T(8,128)(2,1)S(1)}, u32[]{:S(2)}, u32[]{:S(2)}) collective-permute-start(bf16[512,256]{1,0:T(8,128)(2,1)} %refs_2_.1), channel_id=1, source_target_pairs={{0,1},{1,0},{2,3},{3,2},{4,5},{5,4},{6,7},{7,6},{16,17},{17,16},{1... | collective-permute-start | bytes 786440 | tf_op jit(solution)/shard_map/ppermute | solution.py:29
  9.4 9.4 %collective-permute-start.9 = (bf16[512,256]{1,0:T(8,128)(2,1)}, bf16[512,256]{1,0:T(8,128)(2,1)S(1)}, u32[]{:S(2)}, u32[]{:S(2)}) collective-permute-start(bf16[512,256]{1,0:T(8,128)(2,1)} %refs_2_.1), channel_id=1, source_target_pairs={{0,2},{1,3},{2,4},{3,5},{4,6},{5,7},{6,0},{7,1},{16,18},{17,19},{1... | collective-permute-start | bytes 786440 | tf_op jit(solution)/shard_map/ppermute | solution.py:29
  10.6 9.7 %collective-permute-start.11 = (bf16[512,256]{1,0:T(8,128)(2,1)}, bf16[512,256]{1,0:T(8,128)(2,1)S(1)}, u32[]{:S(2)}, u32[]{:S(2)}) collective-permute-start(bf16[512,256]{1,0:T(8,128)(2,1)} %refs_2_.1), channel_id=1, source_target_pairs={{0,6},{1,7},{2,0},{3,1},{4,2},{5,3},{6,4},{7,5},{16,22},{17,23},{1... | collective-permute-start | bytes 786440 | tf_op jit(solution)/shard_map/ppermute | solution.py:29
  12.1 13.3 %collective-permute-start.13 = (bf16[512,256]{1,0:T(8,128)(2,1)}, bf16[512,256]{1,0:T(8,128)(2,1)S(1)}, u32[]{:S(2)}, u32[]{:S(2)}) collective-permute-start(bf16[512,256]{1,0:T(8,128)(2,1)} %refs_2_.1), channel_id=1, source_target_pairs={{0,4},{1,5},{2,6},{3,7},{4,0},{5,1},{6,2},{7,3},{16,20},{17,21},{1... | collective-permute-start | bytes 786440 | tf_op jit(solution)/shard_map/ppermute | solution.py:29
  14.2 15.6 %collective-permute-start.2 = (bf16[512,256]{1,0:T(8,128)(2,1)S(1)}, bf16[512,256]{1,0:T(8,128)(2,1)S(1)}, u32[]{:S(2)}, u32[]{:S(2)}) collective-permute-start(bf16[512,256]{1,0:T(8,128)(2,1)S(1)} %collective-permute-done.refs_2_), channel_id=1, source_target_pairs={{0,2},{1,3},{2,4},{3,5},{4,6},{5,7},{6,0},{7,1},{16,18},{17,19},{1... | collective-permute-start | bytes 786440 | tf_op jit(solution)/shard_map/ppermute | solution.py:29
  17.0 15.0 %collective-permute-start.4 = (bf16[512,256]{1,0:T(8,128)(2,1)S(1)}, bf16[512,256]{1,0:T(8,128)(2,1)S(1)}, u32[]{:S(2)}, u32[]{:S(2)}) collective-permute-start(bf16[512,256]{1,0:T(8,128)(2,1)S(1)} %collective-permute-done.refs_2_), channel_id=1, source_target_pairs={{0,6},{1,7},{2,0},{3,1},{4,2},{5,3},{6,4},{7,5},{16,22},{17,23},{1... | collective-permute-start | bytes 786440 | tf_op jit(solution)/shard_map/ppermute | solution.py:29
  18.8 17.9 %collective-permute-start.6 = (bf16[512,256]{1,0:T(8,128)(2,1)S(1)}, bf16[512,256]{1,0:T(8,128)(2,1)S(1)}, u32[]{:S(2)}, u32[]{:S(2)}) collective-permute-start(bf16[512,256]{1,0:T(8,128)(2,1)S(1)} %collective-permute-done.refs_2_), channel_id=1, source_target_pairs={{0,4},{1,5},{2,6},{3,7},{4,0},{5,1},{6,2},{7,3},{16,20},{17,21},{1... | collective-permute-start | bytes 786440 | tf_op jit(solution)/shard_map/ppermute | solution.py:29
  20.3 17.1 %collective-permute-start.10 = (bf16[512,256]{1,0:T(8,128)(2,1)S(1)}, bf16[512,256]{1,0:T(8,128)(2,1)S(1)}, u32[]{:S(2)}, u32[]{:S(2)}) collective-permute-start(bf16[512,256]{1,0:T(8,128)(2,1)S(1)} %collective-permute-done.9.refs_4_), channel_id=1, source_target_pairs={{0,1},{1,0},{2,3},{3,2},{4,5},{5,4},{6,7},{7,6},{16,17},{17,16},{1... | collective-permute-start | bytes 786440 | tf_op jit(solution)/shard_map/ppermute | solution.py:29
  25.4 12.0 %collective-permute-start.12 = (bf16[512,256]{1,0:T(8,128)(2,1)S(1)}, bf16[512,256]{1,0:T(8,128)(2,1)S(1)}, u32[]{:S(2)}, u32[]{:S(2)}) collective-permute-start(bf16[512,256]{1,0:T(8,128)(2,1)S(1)} %collective-permute-done.11.refs_6_), channel_id=1, source_target_pairs={{0,1},{1,0},{2,3},{3,2},{4,5},{5,4},{6,7},{7,6},{16,17},{17,16},{1... | collective-permute-start | bytes 786440 | tf_op jit(solution)/shard_map/ppermute | solution.py:29
  29.8 8.2 %collective-permute-start.14 = (bf16[512,256]{1,0:T(8,128)(2,1)S(1)}, bf16[512,256]{1,0:T(8,128)(2,1)S(1)}, u32[]{:S(2)}, u32[]{:S(2)}) collective-permute-start(bf16[512,256]{1,0:T(8,128)(2,1)S(1)} %collective-permute-done.13.refs_8_), channel_id=1, source_target_pairs={{0,1},{1,0},{2,3},{3,2},{4,5},{5,4},{6,7},{7,6},{16,17},{17,16},{1... | collective-permute-start | bytes 786440 | tf_op jit(solution)/shard_map/ppermute | solution.py:29
  32.0 16.8 %collective-permute-start.1 = (bf16[512,256]{1,0:T(8,128)(2,1)S(1)}, bf16[512,256]{1,0:T(8,128)(2,1)S(1)}, u32[]{:S(2)}, u32[]{:S(2)}) collective-permute-start(bf16[512,256]{1,0:T(8,128)(2,1)S(1)} %collective-permute-done.refs_2_), channel_id=1, source_target_pairs={{0,1},{1,0},{2,3},{3,2},{4,5},{5,4},{6,7},{7,6},{16,17},{17,16},{1... | collective-permute-start | bytes 786440 | tf_op jit(solution)/shard_map/ppermute | solution.py:29
  36.7 12.2 %collective-permute-start.3 = (bf16[512,256]{1,0:T(8,128)(2,1)S(1)}, bf16[512,256]{1,0:T(8,128)(2,1)S(1)}, u32[]{:S(2)}, u32[]{:S(2)}) collective-permute-start(bf16[512,256]{1,0:T(8,128)(2,1)S(1)} %collective-permute-done.2.refs_4_), channel_id=1, source_target_pairs={{0,1},{1,0},{2,3},{3,2},{4,5},{5,4},{6,7},{7,6},{16,17},{17,16},{1... | collective-permute-start | bytes 786440 | tf_op jit(solution)/shard_map/ppermute | solution.py:29
  37.5 11.4 %collective-permute-start.5 = (bf16[512,256]{1,0:T(8,128)(2,1)S(1)}, bf16[512,256]{1,0:T(8,128)(2,1)S(1)}, u32[]{:S(2)}, u32[]{:S(2)}) collective-permute-start(bf16[512,256]{1,0:T(8,128)(2,1)S(1)} %collective-permute-done.4.refs_6_), channel_id=1, source_target_pairs={{0,1},{1,0},{2,3},{3,2},{4,5},{5,4},{6,7},{7,6},{16,17},{17,16},{1... | collective-permute-start | bytes 786440 | tf_op jit(solution)/shard_map/ppermute | solution.py:29
  37.5 11.4 %collective-permute-start.7 = (bf16[512,256]{1,0:T(8,128)(2,1)S(1)}, bf16[512,256]{1,0:T(8,128)(2,1)S(1)}, u32[]{:S(2)}, u32[]{:S(2)}) collective-permute-start(bf16[512,256]{1,0:T(8,128)(2,1)S(1)} %collective-permute-done.6.refs_8_), channel_id=1, source_target_pairs={{0,1},{1,0},{2,3},{3,2},{4,5},{5,4},{6,7},{7,6},{16,17},{17,16},{1... | collective-permute-start | bytes 786440 | tf_op jit(solution)/shard_map/ppermute | solution.py:29
  38.0 2.6 %copy-start.1 = (bf16[4096,688]{0,1:T(8,128)(2,1)S(1)}, bf16[4096,688]{0,1:T(8,128)(2,1)}, u32[]{:S(2)}) copy-start(bf16[4096,688]{0,1:T(8,128)(2,1)} %param.7) | copy-start | bytes 16908292
  40.6 0.9 copy-start.3
  41.5 7.4 %copy-start.2 = (bf16[4096,688]{0,1:T(8,128)(2,1)S(1)}, bf16[4096,688]{0,1:T(8,128)(2,1)}, u32[]{:S(2)}) copy-start(bf16[4096,688]{0,1:T(8,128)(2,1)} %param.7) | copy-start | bytes 16908292
  41.5 7.4 %copy-start.4 = (bf16[688,64]{0,1:T(8,128)(2,1)S(1)}, bf16[688,64]{0,1:T(8,128)(2,1)}, u32[]{:S(2)}) copy-start(bf16[688,64]{0,1:T(8,128)(2,1)} %param.10) | copy-start | bytes 264196
  56.7 1.4 %collective-permute-start.15 = (f32[2,4,32,128]{3,2,1,0:T(8,128)S(1)}, f32[2,4,32,128]{3,2,1,0:T(8,128)S(1)}, u32[]{:S(2)}, u32[]{:S(2)}) collective-permute-start(f32[2,4,32,128]{3,2,1,0:T(8,128)S(1)} %dynamic-slice_bitcast_fusion), channel_id=1, source_target_pairs={{0,1},{1,0},{2,3},{3,2},{4,5},{5,4},{6,7},{7,6},{16,17},{17,16},{1... | collective-permute-start | bytes 393224 | tf_op jit(solution)/shard_map/ppermute | solution.py:29
  58.2 4.4 %collective-permute-start.18 = (f32[2,32,128]{2,1,0:T(8,128)S(1)}, f32[2,32,128]{2,1,0:T(8,128)S(1)}, u32[]{:S(2)}, u32[]{:S(2)}) collective-permute-start(f32[2,32,128]{2,1,0:T(8,128)S(1)} %get-tuple-element.17), channel_id=1, source_target_pairs={{0,4},{1,5},{2,6},{3,7},{4,0},{5,1},{6,2},{7,3},{16,20},{17,21},{1... | collective-permute-start | bytes 98312 | tf_op jit(solution)/shard_map/ppermute | solution.py:29
  58.8 4.0 %collective-permute-start.17 = (f32[2,32,128]{2,1,0:T(8,128)S(1)}, f32[2,32,128]{2,1,0:T(8,128)S(1)}, u32[]{:S(2)}, u32[]{:S(2)}) collective-permute-start(f32[2,32,128]{2,1,0:T(8,128)S(1)} %get-tuple-element.18), channel_id=1, source_target_pairs={{0,6},{1,7},{2,0},{3,1},{4,2},{5,3},{6,4},{7,5},{16,22},{17,23},{1... | collective-permute-start | bytes 98312 | tf_op jit(solution)/shard_map/ppermute | solution.py:29
  61.5 4.0 %collective-permute-start.16 = (f32[2,32,128]{2,1,0:T(8,128)S(1)}, f32[2,32,128]{2,1,0:T(8,128)S(1)}, u32[]{:S(2)}, u32[]{:S(2)}) collective-permute-start(f32[2,32,128]{2,1,0:T(8,128)S(1)} %get-tuple-element.16), channel_id=1, source_target_pairs={{0,2},{1,3},{2,4},{3,5},{4,6},{5,7},{6,0},{7,1},{16,18},{17,19},{1... | collective-permute-start | bytes 98312 | tf_op jit(solution)/shard_map/ppermute | solution.py:29
  65.5 9.5 %collective-permute-start.19 = (bf16[2,32,128]{2,1,0:T(8,128)(2,1)S(1)}, bf16[2,32,128]{2,1,0:T(8,128)(2,1)S(1)}, u32[]{:S(2)}, u32[]{:S(2)}) collective-permute-start(bf16[2,32,128]{2,1,0:T(8,128)(2,1)S(1)} %fusion.5), channel_id=1, source_target_pairs={{0,8},{1,9},{2,10},{3,11},{4,12},{5,13},{6,14},{7,15},{16,24},{17,... | collective-permute-start | bytes 49160 | tf_op jit(solution)/shard_map/ppermute | solution.py:29
  66.2 10.4 %collective-permute-start.25 = (bf16[2,32,128]{2,1,0:T(8,128)(2,1)S(1)}, bf16[2,32,128]{2,1,0:T(8,128)(2,1)S(1)}, u32[]{:S(2)}, u32[]{:S(2)}) collective-permute-start(bf16[2,32,128]{2,1,0:T(8,128)(2,1)S(1)} %fusion.5), channel_id=1, source_target_pairs={{0,200},{1,201},{2,202},{3,203},{4,204},{5,205},{6,206},{7,207},{1... | collective-permute-start | bytes 49160 | tf_op jit(solution)/shard_map/ppermute | solution.py:29
  69.7 9.4 %collective-permute-start.24 = (bf16[2,32,128]{2,1,0:T(8,128)(2,1)S(1)}, bf16[2,32,128]{2,1,0:T(8,128)(2,1)S(1)}, u32[]{:S(2)}, u32[]{:S(2)}) collective-permute-start(bf16[2,32,128]{2,1,0:T(8,128)(2,1)S(1)} %fusion.5), channel_id=1, source_target_pairs={{0,192},{1,193},{2,194},{3,195},{4,196},{5,197},{6,198},{7,199},{1... | collective-permute-start | bytes 49160 | tf_op jit(solution)/shard_map/ppermute | solution.py:29
  72.6 6.5 %collective-permute-start.23 = (bf16[2,32,128]{2,1,0:T(8,128)(2,1)S(1)}, bf16[2,32,128]{2,1,0:T(8,128)(2,1)S(1)}, u32[]{:S(2)}, u32[]{:S(2)}) collective-permute-start(bf16[2,32,128]{2,1,0:T(8,128)(2,1)S(1)} %fusion.5), channel_id=1, source_target_pairs={{0,136},{1,137},{2,138},{3,139},{4,140},{5,141},{6,142},{7,143},{1... | collective-permute-start | bytes 49160 | tf_op jit(solution)/shard_map/ppermute | solution.py:29
  74.2 4.9 %collective-permute-start.22 = (bf16[2,32,128]{2,1,0:T(8,128)(2,1)S(1)}, bf16[2,32,128]{2,1,0:T(8,128)(2,1)S(1)}, u32[]{:S(2)}, u32[]{:S(2)}) collective-permute-start(bf16[2,32,128]{2,1,0:T(8,128)(2,1)S(1)} %fusion.5), channel_id=1, source_target_pairs={{0,128},{1,129},{2,130},{3,131},{4,132},{5,133},{6,134},{7,135},{1... | collective-permute-start | bytes 49160 | tf_op jit(solution)/shard_map/ppermute | solution.py:29
  75.0 4.5 %collective-permute-start.21 = (bf16[2,32,128]{2,1,0:T(8,128)(2,1)S(1)}, bf16[2,32,128]{2,1,0:T(8,128)(2,1)S(1)}, u32[]{:S(2)}, u32[]{:S(2)}) collective-permute-start(bf16[2,32,128]{2,1,0:T(8,128)(2,1)S(1)} %fusion.5), channel_id=1, source_target_pairs={{0,72},{1,73},{2,74},{3,75},{4,76},{5,77},{6,78},{7,79},{16,88},{1... | collective-permute-start | bytes 49160 | tf_op jit(solution)/shard_map/ppermute | solution.py:29
  76.6 3.9 %collective-permute-start.20 = (bf16[2,32,128]{2,1,0:T(8,128)(2,1)S(1)}, bf16[2,32,128]{2,1,0:T(8,128)(2,1)S(1)}, u32[]{:S(2)}, u32[]{:S(2)}) collective-permute-start(bf16[2,32,128]{2,1,0:T(8,128)(2,1)S(1)} %fusion.5), channel_id=1, source_target_pairs={{0,64},{1,65},{2,66},{3,67},{4,68},{5,69},{6,70},{7,71},{16,80},{1... | collective-permute-start | bytes 49160 | tf_op jit(solution)/shard_map/ppermute | solution.py:29
  82.0 4.3 %collective-permute-start.26 = (bf16[8,4096]{1,0:T(8,128)(2,1)S(1)}, bf16[8,4096]{1,0:T(8,128)(2,1)S(1)}, u32[]{:S(2)}, u32[]{:S(2)}) collective-permute-start(bf16[8,4096]{1,0:T(8,128)(2,1)S(1)} %get-tuple-element.7), channel_id=1, source_target_pairs={{0,16},{1,3},{2,18},{3,5},{4,20},{5,7},{6,22},{7,1},{16,32},{17,19... | collective-permute-start | bytes 196616 | tf_op jit(solution)/shard_map/ppermute | solution.py:29
  82.0 4.6 %collective-permute-start.27 = (bf16[8,4096]{1,0:T(8,128)(2,1)S(1)}, bf16[8,4096]{1,0:T(8,128)(2,1)S(1)}, u32[]{:S(2)}, u32[]{:S(2)}) collective-permute-start(bf16[8,4096]{1,0:T(8,128)(2,1)S(1)} %get-tuple-element.7), channel_id=1, source_target_pairs={{0,48},{1,7},{2,50},{3,1},{4,52},{5,3},{6,54},{7,5},{16,0},{17,23}... | collective-permute-start | bytes 196616 | tf_op jit(solution)/shard_map/ppermute | solution.py:29
  84.6 4.6 %collective-permute-start.28 = (bf16[8,4096]{1,0:T(8,128)(2,1)S(1)}, bf16[8,4096]{1,0:T(8,128)(2,1)S(1)}, u32[]{:S(2)}, u32[]{:S(2)}) collective-permute-start(bf16[8,4096]{1,0:T(8,128)(2,1)S(1)} %get-tuple-element.7), channel_id=1, source_target_pairs={{0,32},{1,5},{2,34},{3,7},{4,36},{5,1},{6,38},{7,3},{16,48},{17,21... | collective-permute-start | bytes 196616 | tf_op jit(solution)/shard_map/ppermute | solution.py:29
  89.3 7.3 %collective-permute-start.29 = (bf16[32,4096]{1,0:T(8,128)(2,1)S(1)}, bf16[32,4096]{1,0:T(8,128)(2,1)S(1)}, u32[]{:S(2)}, u32[]{:S(2)}) collective-permute-start(bf16[32,4096]{1,0:T(8,128)(2,1)S(1)} %pad_maximum_fusion), channel_id=1, source_target_pairs={{0,2},{1,17},{2,4},{3,19},{4,6},{5,21},{6,0},{7,23},{16,18},{17,33... | collective-permute-start | bytes 786440 | tf_op jit(solution)/shard_map/ppermute | solution.py:29
  90.7 8.3 %collective-permute-start.30 = (bf16[32,4096]{1,0:T(8,128)(2,1)S(1)}, bf16[32,4096]{1,0:T(8,128)(2,1)S(1)}, u32[]{:S(2)}, u32[]{:S(2)}) collective-permute-start(bf16[32,4096]{1,0:T(8,128)(2,1)S(1)} %pad_maximum_fusion), channel_id=1, source_target_pairs={{0,6},{1,49},{2,0},{3,51},{4,2},{5,53},{6,4},{7,55},{16,22},{17,1}... | collective-permute-start | bytes 786440 | tf_op jit(solution)/shard_map/ppermute | solution.py:29
  92.2 8.4 %collective-permute-start.31 = (bf16[32,4096]{1,0:T(8,128)(2,1)S(1)}, bf16[32,4096]{1,0:T(8,128)(2,1)S(1)}, u32[]{:S(2)}, u32[]{:S(2)}) collective-permute-start(bf16[32,4096]{1,0:T(8,128)(2,1)S(1)} %pad_maximum_fusion), channel_id=1, source_target_pairs={{0,4},{1,33},{2,6},{3,35},{4,0},{5,37},{6,2},{7,39},{16,20},{17,49... | collective-permute-start | bytes 786440 | tf_op jit(solution)/shard_map/ppermute | solution.py:29
  101.3 9.5 %collective-permute-start.32 = (bf16[128,4096]{1,0:T(8,128)(2,1)}, bf16[128,4096]{1,0:T(8,128)(2,1)S(1)}, u32[]{:S(2)}, u32[]{:S(2)}) collective-permute-start(bf16[128,4096]{1,0:T(8,128)(2,1)} %get-tuple-element.10), channel_id=1, source_target_pairs={{0,1},{1,0},{2,3},{3,2},{4,5},{5,4},{6,7},{7,6},{16,17},{17,16},{1... | collective-permute-start | bytes 3145736 | tf_op jit(solution)/shard_map/ppermute | solution.py:29

commit v2 on v0

v2 whole, which is shorter than its diff:
```python
import functools

import jax
import jax.numpy as jnp
from jax import lax
from jax.experimental import pallas as pl
from jax.experimental.pallas import tpu as pltpu
from jax.sharding import PartitionSpec as P

SEQ = 32
BOTH = ("ex", "par")


def pairs(move):
    def index(z, y, x, core):
        z, y, x = z % 8, y % 4, x % 4
        return ((z % 4) * 4 + y) * 16 + (z // 4) * 8 + x * 2 + core

    return [
        (index(z, y, x, c), index(*move(z, y, x, c)))
        for z in range(8)
        for y in range(4)
        for x in range(4)
        for c in range(2)
    ]


def send(value, move):
    return lax.ppermute(value, BOTH, pairs(move))


def shift_x(n):
    return lambda z, y, x, c: (z, y, x + n, c)


def shift_z(n):
    return lambda z, y, x, c: (z + n, y, x, c)


def other_core(z, y, x, c):
    return (z, y, x, 1 - c)


VMEM = pltpu.VMEM
ROWS_TIMES_ROWS = (((1,), (1,)), ((), ()))
LINES = [[(z % 4 * 4 + y) * 16 + z // 4 * 8 + n for z in range(8)] for y in range(4) for n in range(8)]
PLANES = [
    [(z % 4 * 4 + y) * 16 + z // 4 * 8 + x * 2 + c for x in range(4) for y in range(4)]
    for z in range(8)
    for c in range(2)
]


def block_copies(blocks, held, sems):
    return [
        pltpu.make_async_copy(v, held.at[:, pl.ds(n * 256, 256)], sems.at[n // 2, n % 2]) for n, v in enumerate(blocks)
    ]


def weight_copies(starts, first, count, gate, up, weights, sems):
    units, made = gate.shape[0], []
    for n in range(2 * count):
        cols = pl.ds(pl.multiple_of(starts[first + n], 256), 256)
        for m, source in enumerate((gate, up)):
            to = weights.at[pl.ds(m * units, units), pl.ds(n * 256, 256)]
            made.append(pltpu.make_async_copy(source.at[:, cols], to, sems.at[n // 2, 2 + n % 2 * 2 + m]))
    return made


def start(copies):
    for c in copies:
        c.start()


def wait(copies):
    for c in copies:
        c.wait()


def product(weights, held, j):
    cols = slice(j * 512, (j + 1) * 512)
    return lax.dot_general(weights[:, cols], held[:, cols], ROWS_TIMES_ROWS, preferred_element_type=jnp.float32)


def own_kernel(starts, second, first, gate, up, out, held, weights, sems):
    copies = weight_copies(starts, 0, 1, gate, up, weights, sems) + block_copies((first, second), held, sems)
    start(copies)
    wait(copies)
    out[...] = product(weights, held, 0)


def near_kernel(starts, *refs):
    blocks, (gate, up, near, out, held, weights, sems) = refs[:6], refs[6:]
    loads = block_copies(blocks, held, sems)
    columns = weight_copies(starts, 2, 3, gate, up, weights, sems)
    start(loads)
    start(columns)
    for j in range(3):
        wait(loads[2 * j : 2 * j + 2])
        wait(columns[4 * j : 4 * j + 4])
        if j == 0:
            out[...] = product(weights, held, 0) + near[...]
        else:
            out[...] += product(weights, held, j)


def middle_kernel(starts, gate, up, grads, proj_model, *refs):
    blocks, (near, out, later, right, weights, sems) = refs[:6], refs[6:]
    columns = weight_copies(starts, 8, 3, gate, up, weights, sems)
    later_columns = weight_copies(starts, 14, 1, gate, up, later, sems.at[pl.ds(3, 1)])
    start(columns)
    start(later_columns)
    right[...] = lax.dot_general(grads[...], proj_model[...], ROWS_TIMES_ROWS, preferred_element_type=jnp.float32)
    for j in range(3):
        held = jnp.concatenate([blocks[2 * j][...], blocks[2 * j + 1][...]], axis=1)
        wait(columns[4 * j : 4 * j + 4])
        value = lax.dot_general(
            weights[:, j * 512 : (j + 1) * 512], held, ROWS_TIMES_ROWS, preferred_element_type=jnp.float32
        )
        if j == 0:
            out[...] = value + near[...]
        else:
            out[...] += value
    wait(later_columns)


def last_kernel(proj, first, second, weights, sums, right, out):
    units = proj.shape[1]
    held = jnp.concatenate([first[...], second[...]], axis=1)
    value = lax.dot_general(weights[...], held, ROWS_TIMES_ROWS, preferred_element_type=jnp.float32)
    value = value + sums[...]
    gate, up = value[:units], value[units:]
    hidden = (gate / (1.0 + jnp.exp(-gate)) * up).astype(jnp.bfloat16)
    left = jnp.dot(proj[...], hidden, preferred_element_type=jnp.float32)
    out[:, :64] = left.T
    out[:, 64:] = right[...]


def call(kernel, name, out, flops, scalars, anywhere, in_hbm, copied, in_vmem, scratch):
    vmem = pl.BlockSpec(memory_space=VMEM)
    return pl.pallas_call(
        kernel,
        out_shape=[VMEM(shape, dtype) for shape, dtype in out],
        in_specs=[pl.BlockSpec(memory_space=pltpu.SMEM)] * len(scalars)
        + [pl.BlockSpec(memory_space=pl.ANY)] * len(anywhere)
        + [pl.BlockSpec(memory_space=pltpu.HBM)] * len(in_hbm)
        + [vmem] * (len(copied) + len(in_vmem)),
        out_specs=[vmem] * len(out),
        scratch_shapes=scratch,
        compiler_params=pltpu.CompilerParams(vmem_limit_bytes=24 * 1024 * 1024),
        cost_estimate=pl.CostEstimate(flops=flops, bytes_accessed=0, transcendentals=0),
        name=name,
    )(
        *scalars,
        *anywhere,
        *[pltpu.with_memory_space_constraint(v, pltpu.HBM) for v in in_hbm],
        *copied,
        *[pltpu.with_memory_space_constraint(v, VMEM) for v in in_vmem],
    )


def on_device(inputs, w_gate, w_up, out_grads, proj_hidden, proj_model):
    rows, units = inputs.shape[0], w_gate.shape[1]
    par = lax.axis_index("par")
    z_hi, x, core = par // 8, (par // 2) % 4, par % 2

    far = send(inputs, shift_z(4))
    sibling = send(inputs, other_core)
    own, sibling = lax.optimization_barrier((inputs, sibling))
    by_x = [send(own, shift_x(n)) for n in (1, 3, 2)]

    chips = jnp.stack([x, (x + 3) % 4, (x + 1) % 4, (x + 2) % 4])
    cores = jnp.stack([core, 1 - core])
    starts = jnp.stack([z_hi, 1 - z_hi])[:, None, None] * 2048 + chips[:, None] * 512 + cores * 256
    starts = starts.reshape(16).astype(jnp.int32)
    w_gate, w_up = w_gate.T, w_up.T
    sums_type, bf16 = ((2 * units, rows), jnp.float32), jnp.bfloat16
    held = lambda n: VMEM((rows, n * 512), bf16)
    columns = lambda n: VMEM((2 * units, n * 512), bf16)
    sems = pltpu.SemaphoreType.DMA((3, 6))
    flops = 4 * rows * units * 512
    (sums,) = call(
        own_kernel,
        "own",
        [sums_type],
        flops,
        [starts],
        [sibling],
        [inputs, w_gate, w_up],
        [],
        [],
        [held(1), columns(1), sems],
    )
    far, sums = lax.optimization_barrier((far, sums))
    far = [far] + [send(far, shift_x(n)) for n in (1, 3, 2)]
    *by_x, _ = lax.optimization_barrier((*by_x, far[0]))
    near_all = [b for n in by_x for b in (n, send(n, other_core))]
    (sums,) = call(
        near_kernel,
        "near",
        [sums_type],
        0,
        [starts],
        [],
        near_all + [w_gate, w_up],
        [],
        [sums],
        [held(3), columns(3), sems],
    )
    *by_x, sums = lax.optimization_barrier((*far[1:], sums))
    far_all = [b for n in (far[0], *by_x) for b in (n, send(n, other_core))]
    sums, weights, right = call(
        middle_kernel,
        "middle",
        [sums_type, ((2 * units, 512), bf16), ((rows, 64), jnp.float32)],
        3 * flops,
        [starts],
        [],
        [w_gate, w_up],
        [out_grads, proj_model.T],
        [*far_all[:6], sums],
        [columns(3), pltpu.SemaphoreType.DMA((4, 6))],
    )
    (both,) = call(
        last_kernel,
        "last",
        [((rows, 128), jnp.float32)],
        flops,
        [],
        [],
        [],
        [proj_hidden.T],
        [*far_all[6:], weights, sums, right],
        [],
    )

    both = both.reshape(2, 4, 2, SEQ, 128)
    pick = lambda v, i, axis: lax.dynamic_index_in_dim(v, i, axis, keepdims=False)
    both = pick(both, core, 2) + send(pick(both, 1 - core, 2), other_core)
    part = pick(both, x, 1)
    for n in (1, 3, 2):
        part = part + send(pick(both, (x + n) % 4, 1), shift_x(n))

    part = jnp.broadcast_to(part.astype(jnp.bfloat16), (8, *part.shape))
    along = lax.all_to_all(part, BOTH, 0, 0, axis_index_groups=LINES).astype(jnp.float32)
    total = (along[:4] + along[4:]).reshape(8, SEQ, 128)
    outer = jnp.einsum("eta,etb->eab", total[..., :64], total[..., 64:], precision=lax.Precision.HIGHEST)
    feats = outer.reshape(8, 4096) / jnp.sqrt(jnp.float32(SEQ))
    z_lo = lax.axis_index("ex") // 4
    features = lax.dynamic_slice_in_dim(feats, z_lo * 2 + z_hi, 1, 0)

    feats = jnp.broadcast_to(feats.astype(jnp.bfloat16), (16, 8, 4096))
    feats = lax.all_to_all(feats, BOTH, 0, 0, axis_index_groups=PLANES).reshape(128, 4096)
    feats = jnp.concatenate([feats, send(feats, other_core)])
    mine = lax.dynamic_slice_in_dim(feats, par * 256, 256, 1)
    gram = jnp.dot(mine.T, feats, preferred_element_type=jnp.float32) * (1.0 / 256)
    return (features, gram)


def solution(mesh):
    placed = (
        P("ex", "par"),
        P(None, "par"),
        P(None, "par"),
        P("ex", "par"),
        P("par", None),
        P("par", None),
    )
    return jax.shard_map(
        on_device,
        mesh=mesh,
        in_specs=placed,
        out_specs=(P(("ex", "par"), None), P("par", None)),
        check_vma=False,
    )
```

time: 654 us -> 101 us (0.15); the launches traced: 645 us -> 101 us
  waiting for transfers between devices: 575 us -> 20.8 us
  starting transfers between devices: 0.16 us -> 28.5 us
  Pallas kernels: 0 us -> 16.7 us
  matrix products: 19.7 us -> 3.45 us
  between operations: 13.8 us -> 0.81 us
    psum x2 -> x0, waiting for transfers between devices: 314 us -> none  [the longest x1 161 us: on_device(): right_whole = lax.psum(right_part, 'par')]
    unnamed x5 -> x0, waiting for transfers between devices: 178 us -> none
    all_gather x1 -> x0, waiting for transfers between devices: 83.1 us -> none  [on_device(): piece = lax.all_gather(inputs, 'par', axis=1, tiled=True)]
    all_gather x1 -> x0, blocking collectives: 29.2 us -> none  [on_device(): piece = lax.all_gather(features_bf, 'par', axis=0, tiled=True)]
    all_to_all x0 -> x2, blocking collectives: none -> 28.9 us  [the longest x1 18 us: on_device(): lax.all_to_all(feats, BOTH, 0, 0, axis_index_groups=PLANES)]
    ppermute x0 -> x20, starting transfers between devices: none -> 28.5 us  [send(): return lax.ppermute(value, BOTH, pairs(move))]
    ppermute x0 -> x20, waiting for transfers between devices: none -> 20.8 us  [send(): return lax.ppermute(value, BOTH, pairs(move))]
    pallas_call x0 -> x4, Pallas kernels: none -> 16.7 us  [call(): pl.pallas_call(kernel, out_shape=[VMEM(shape, dtype) for shape, dtype in...]
  transfers between devices with their start and end apart: 4 -> 20, of which waited for: 4 -> 10; matrix products, arithmetic and copies ran while one was open for 3% -> 1% of each run, Pallas kernels for 0% -> 14%
where the time goes in v2:
time: 101 us
  blocking collectives  28.9 us (29%)
  starting transfers between devices  28.5 us (28%)
  waiting for transfers between devices  20.8 us (21%)
  Pallas kernels  16.7 us (17%)
  matrix products  3.45 us (3%)
  local copies, waits for them, and re-layouts  1.73 us (2%)
    ppermute x20, starting transfers between devices, send(): return lax.ppermute(value, BOTH, pairs(move))  28.5 us
    ppermute x20, waiting for transfers between devices, send(): return lax.ppermute(value, BOTH, pairs(move))  20.8 us
    all_to_all x1, blocking collectives, on_device(): lax.all_to_all(feats, BOTH, 0, 0, axis_index_groups=PLANES)  18 us
    pallas_call x4, Pallas kernels, call(): pl.pallas_call(kernel, out_shape=[VMEM(shape, dtype) for shape, dtype in...  16.7 us
    all_to_all x1, blocking collectives, on_device(): lax.all_to_all(part, BOTH, 0, 0, axis_index_groups=LINES)  11 us
    dot_general x1, matrix products, on_device(): jnp.dot(mine.T, feats, preferred_element_type=jnp.float32) * (1.0 / 256)  2.77 us
  transfers between devices with their start and end apart: 20, of which 10 were waited for; matrix products, arithmetic and copies ran while one was open for 1% of the time, Pallas kernels for 14%

profile of v2, /device:TPU:1, one launch (start us, length us, event | category | flops | bytes accessed | tf_op | source)
XLA Modules:
  0.0 101.2 jit_solution(3835231708087038179)
XLA Ops:
  0.6 3.3 %collective-permute-start.1 = (bf16[512,256]{1,0:T(8,128)(2,1)}, bf16[512,256]{1,0:T(8,128)(2,1)S(1)}, u32[]{:S(2)}, u32[]{:S(2)}) collective-permute-start(bf16[512,256]{1,0:T(8,128)(2,1)} %first.1), channel_id=1, source_target_pairs={{0,1},{1,0},{2,3},{3,2},{4,5},{5,4},{6,7},{7,6},{16,17},{17,16},{1... | collective-permute-start | bytes 786440 | tf_op jit(solution)/shard_map/ppermute | solution.py:29
  4.0 5.2 %collective-permute-start = (bf16[512,256]{1,0:T(8,128)(2,1)}, bf16[512,256]{1,0:T(8,128)(2,1)S(1)}, u32[]{:S(2)}, u32[]{:S(2)}) collective-permute-start(bf16[512,256]{1,0:T(8,128)(2,1)} %first.1), channel_id=1, source_target_pairs={{0,8},{1,9},{2,10},{3,11},{4,12},{5,13},{6,14},{7,15},{16,24},{17,... | collective-permute-start | bytes 786440 | tf_op jit(solution)/shard_map/ppermute | solution.py:29
  9.2 0.1 add_multiply_fusion
  9.2 0.1 add_multiply_fusion.1
  9.3 0.1 broadcast_add_fusion.1
  9.4 1.2 %collective-permute-start.5 = (bf16[512,256]{1,0:T(8,128)(2,1)}, bf16[512,256]{1,0:T(8,128)(2,1)S(1)}, u32[]{:S(2)}, u32[]{:S(2)}) collective-permute-start(bf16[512,256]{1,0:T(8,128)(2,1)} %first.1), channel_id=1, source_target_pairs={{0,2},{1,3},{2,4},{3,5},{4,6},{5,7},{6,0},{7,1},{16,18},{17,19},{1... | collective-permute-start | bytes 786440 | tf_op jit(solution)/shard_map/ppermute | solution.py:29
  10.6 1.5 %collective-permute-start.6 = (bf16[512,256]{1,0:T(8,128)(2,1)}, bf16[512,256]{1,0:T(8,128)(2,1)S(1)}, u32[]{:S(2)}, u32[]{:S(2)}) collective-permute-start(bf16[512,256]{1,0:T(8,128)(2,1)} %first.1), channel_id=1, source_target_pairs={{0,6},{1,7},{2,0},{3,1},{4,2},{5,3},{6,4},{7,5},{16,22},{17,23},{1... | collective-permute-start | bytes 786440 | tf_op jit(solution)/shard_map/ppermute | solution.py:29
  12.1 1.5 %collective-permute-start.7 = (bf16[512,256]{1,0:T(8,128)(2,1)}, bf16[512,256]{1,0:T(8,128)(2,1)S(1)}, u32[]{:S(2)}, u32[]{:S(2)}) collective-permute-start(bf16[512,256]{1,0:T(8,128)(2,1)} %first.1), channel_id=1, source_target_pairs={{0,4},{1,5},{2,6},{3,7},{4,0},{5,1},{6,2},{7,3},{16,20},{17,21},{1... | collective-permute-start | bytes 786440 | tf_op jit(solution)/shard_map/ppermute | solution.py:29
  13.6 0.1 broadcast_add_fusion
  13.7 0.1 add.128.starts
  13.8 3.0 %own.1.refs_8_ = f32[1376,512]{1,0:T(8,128)S(1)} custom-call(s32[16]{0:T(128)S(1)} %add.128.starts, bf16[512,256]{1,0:T(8,128)(2,1)S(1)} %collective-permute-done.1.second, bf16[512,256]{1,0:T(8,128)(2,1)} %first.1, bf16[688,4096]{1,0:T(8,128)(2,1)} %bitcast.37, bf16[688,4096]{1,0:T(8,128)(2,1)} %bitcast.40), custom_call_target="tpu_custom_call" | custom-call | flops 721420288 | tf_op jit(solution)/shard_map/own/pallas_call | solution.py:141
  16.8 0.0 copy-start
  16.8 0.0 copy-start.2
  16.8 0.1 collective-permute-done.refs_0_
  17.0 1.4 %collective-permute-done.5.refs_0_ = bf16[512,256]{1,0:T(8,128)(2,1)S(1)} collective-permute-done((bf16[512,256]{1,0:T(8,128)(2,1)}, bf16[512,256]{1,0:T(8,128)(2,1)S(1)}, u32[]{:S(2)}, u32[]{:S(2)}) %collective-permute-start.5) | collective-permute-done | bytes 262176 | tf_op jit(solution)/shard_map/ppermute | solution.py:29
  18.4 6.6 %collective-permute-done.7.refs_4_ = bf16[512,256]{1,0:T(8,128)(2,1)S(1)} collective-permute-done((bf16[512,256]{1,0:T(8,128)(2,1)}, bf16[512,256]{1,0:T(8,128)(2,1)S(1)}, u32[]{:S(2)}, u32[]{:S(2)}) %collective-permute-start.7) | collective-permute-done | bytes 262176 | tf_op jit(solution)/shard_map/ppermute | solution.py:29
  25.0 1.2 %collective-permute-start.10 = (bf16[512,256]{1,0:T(8,128)(2,1)S(1)}, bf16[512,256]{1,0:T(8,128)(2,1)S(1)}, u32[]{:S(2)}, u32[]{:S(2)}) collective-permute-start(bf16[512,256]{1,0:T(8,128)(2,1)S(1)} %collective-permute-done.7.refs_4_), channel_id=1, source_target_pairs={{0,1},{1,0},{2,3},{3,2},{4,5},{5,4},{6,7},{7,6},{16,17},{17,16},{1... | collective-permute-start | bytes 786440 | tf_op jit(solution)/shard_map/ppermute | solution.py:29
  26.1 0.5 collective-permute-start.9
  26.7 0.9 collective-permute-start.2
  27.5 1.8 %collective-permute-start.3 = (bf16[512,256]{1,0:T(8,128)(2,1)S(1)}, bf16[512,256]{1,0:T(8,128)(2,1)}, u32[]{:S(2)}, u32[]{:S(2)}) collective-permute-start(bf16[512,256]{1,0:T(8,128)(2,1)S(1)} %collective-permute-done.refs_0_), channel_id=1, source_target_pairs={{0,6},{1,7},{2,0},{3,1},{4,2},{5,3},{6,4},{7,5},{16,22},{17,23},{1... | collective-permute-start | bytes 786440 | tf_op jit(solution)/shard_map/ppermute | solution.py:29
  29.3 0.4 collective-permute-start.4
  29.7 0.6 collective-permute-start.12
  30.4 0.0 copy-done.7
  30.4 0.7 copy-done.8
  31.1 5.4 %near.1.refs_6_ = f32[1376,512]{1,0:T(8,128)S(1)} custom-call(s32[16]{0:T(128)S(1)} %add.128.starts, bf16[512,256]{1,0:T(8,128)(2,1)} %copy-done.3, bf16[512,256]{1,0:T(8,128)(2,1)} %copy-done.7, bf16[512,256]{1,0:T(8,128)(2,1)} %copy-done.4, bf16[512,256]{1,0:T(8,128)(2,1)} %copy-done.8, bf16[512,256]{1,0:T(8,128)(2,1)} %copy-done.5, ...), custom_call_target="tpu_custom_call" | custom-call | tf_op jit(solution)/shard_map/near/pallas_call | solution.py:141
  36.5 5.2 %collective-permute-done.4.first = bf16[512,256]{1,0:T(8,128)(2,1)} collective-permute-done((bf16[512,256]{1,0:T(8,128)(2,1)S(1)}, bf16[512,256]{1,0:T(8,128)(2,1)}, u32[]{:S(2)}, u32[]{:S(2)}) %collective-permute-start.4) | collective-permute-done | bytes 262176 | tf_op jit(solution)/shard_map/ppermute | solution.py:29
  41.7 0.9 collective-permute-start.13
  42.6 0.5 collective-permute-start.11
  43.1 1.0 collective-permute-done.13.refs_3_
  44.1 0.4 collective-permute-done.14.refs_5_
  44.5 5.7 %middle.1 = (f32[1376,512]{1,0:T(8,128)S(1)}, bf16[1376,512]{1,0:T(8,128)(2,1)S(1)}, f32[512,64]{1,0:T(8,128)S(1)}) custom-call(s32[16]{0:T(128)S(1)} %add.128.starts, bf16[688,4096]{1,0:T(8,128)(2,1)} %bitcast.39, bf16[688,4096]{1,0:T(8,128)(2,1)} %bitcast.42, bf16[512,256]{1,0:T(8,128)(2,1)S(1)} %copy-done, bf16[64,256]{1,0:T(8,128)(2,1)S(1)} %bitcast.36, ...), custom_call_target="tpu_custom_call" | custom-call | flops 2164260864 | tf_op jit(solution)/shard_map/middle/pallas_call | solution.py:141
  50.2 2.6 %last.1 = f32[512,128]{1,0:T(8,128)S(1)} custom-call(bf16[64,688]{1,0:T(8,128)(2,1)S(1)} %bitcast.35, bf16[512,256]{1,0:T(8,128)(2,1)} %collective-permute-done.4.first, bf16[512,256]{1,0:T(8,128)(2,1)} %collective-permute-done.11.second, bf16[1376,512]{1,0:T(8,128)(2,1)S(1)} %get-tuple-element.27.weights, f32[1376,512]{1,0:T(8,128)S(1)} %get-tuple-element.28.sums, ...), custom_call_target="tpu_custom_call" | custom-call | flops 721420288 | tf_op jit(solution)/shard_map/last/pallas_call | solution.py:141
  52.8 0.5 collective-permute-start.15
  53.3 1.0 collective-permute-done.15
  54.3 0.9 collective-permute-start.16
  55.3 1.8 %collective-permute-start.17 = (f32[2,32,128]{2,1,0:T(8,128)S(1)}, f32[2,32,128]{2,1,0:T(8,128)S(1)}, u32[]{:S(2)}, u32[]{:S(2)}) collective-permute-start(f32[2,32,128]{2,1,0:T(8,128)S(1)} %get-tuple-element.32), channel_id=1, source_target_pairs={{0,6},{1,7},{2,0},{3,1},{4,2},{5,3},{6,4},{7,5},{16,22},{17,23},{1... | collective-permute-start | bytes 98312 | tf_op jit(solution)/shard_map/ppermute | solution.py:29
  57.1 0.9 collective-permute-start.18
  58.0 0.4 collective-permute-done.16
  58.4 3.0 %collective-permute-done.18 = f32[2,32,128]{2,1,0:T(8,128)S(1)} collective-permute-done((f32[2,32,128]{2,1,0:T(8,128)S(1)}, f32[2,32,128]{2,1,0:T(8,128)S(1)}, u32[]{:S(2)}, u32[]{:S(2)}) %collective-permute-start.18) | collective-permute-done | bytes 32800 | tf_op jit(solution)/shard_map/ppermute | solution.py:29
  61.4 11.0 %all_to_all.10 = bf16[8,2,32,128]{3,2,1,0:T(8,128)(2,1)S(1)} all-to-all(bf16[8,2,32,128]{3,2,1,0:T(8,128)(2,1)S(1)} %broadcast_in_dim.4), channel_id=1, replica_groups={{0,64,128,192,8,72,136,200},{1,65,129,193,9,73,137,201},{2,66,130,194,1..., dimensions={0} | all-to-all | bytes 262144 | tf_op jit(solution)/shard_map/all_to_all | solution.py:245
  72.4 0.7 convolution_multiply_fusion.1
  73.1 0.1 div.38
  73.2 0.1 broadcast_in_dim.5
  73.3 18.0 %all_to_all.11 = bf16[16,8,4096]{2,1,0:T(8,128)(2,1)S(1)} all-to-all(bf16[16,8,4096]{2,1,0:T(8,128)(2,1)S(1)} %broadcast_in_dim.5), channel_id=1, replica_groups={{0,16,32,48,2,18,34,50,4,20,36,52,6,22,38,54},{1,17,33,49,3,19,35,51,5,..., dimensions={0} | all-to-all | bytes 2097152 | tf_op jit(solution)/shard_map/all_to_all | solution.py:253
  91.3 4.8 %collective-permute-start.19 = (bf16[128,4096]{1,0:T(8,128)(2,1)S(1)}, bf16[128,4096]{1,0:T(8,128)(2,1)S(1)}, u32[]{:S(2)}, u32[]{:S(2)}) collective-permute-start(bf16[128,4096]{1,0:T(8,128)(2,1)S(1)} %bitcast.43), channel_id=1, source_target_pairs={{0,1},{1,0},{2,3},{3,2},{4,5},{5,4},{6,7},{7,6},{16,17},{17,16},{1... | collective-permute-start | bytes 3145736 | tf_op jit(solution)/shard_map/ppermute | solution.py:29
  96.2 0.6 constant_dynamic-slice_fusion
  96.8 1.7 %collective-permute-done.19 = bf16[128,4096]{1,0:T(8,128)(2,1)S(1)} collective-permute-done((bf16[128,4096]{1,0:T(8,128)(2,1)S(1)}, bf16[128,4096]{1,0:T(8,128)(2,1)S(1)}, u32[]{:S(2)}, u32[]{:S(2)}) %collective-permute-start.19) | collective-permute-done | bytes 1048608 | tf_op jit(solution)/shard_map/ppermute | solution.py:29
  98.4 2.8 %convolution_multiply_fusion = f32[256,4096]{1,0:T(8,128)} fusion(bf16[128,4096]{1,0:T(8,128)(2,1)S(1)} %collective-permute-done.19, bf16[128,4096]{1,0:T(8,128)(2,1)S(1)} %bitcast.44, s32[]{:T(128)S(6)} %select_n.80), kind=kOutput, calls=%fused_computation | convolution fusion | flops 542375936 | bytes 8388612 | tf_op jit(solution)/shard_map/dot_general | solution.py:256
  (34 shorter events, 0.2 us)
Async XLA Ops:
  0.6 8.8 %collective-permute-start.1 = (bf16[512,256]{1,0:T(8,128)(2,1)}, bf16[512,256]{1,0:T(8,128)(2,1)S(1)}, u32[]{:S(2)}, u32[]{:S(2)}) collective-permute-start(bf16[512,256]{1,0:T(8,128)(2,1)} %first.1), channel_id=1, source_target_pairs={{0,1},{1,0},{2,3},{3,2},{4,5},{5,4},{6,7},{7,6},{16,17},{17,16},{1... | collective-permute-start | bytes 786440 | tf_op jit(solution)/shard_map/ppermute | solution.py:29
  4.0 13.0 %collective-permute-start = (bf16[512,256]{1,0:T(8,128)(2,1)}, bf16[512,256]{1,0:T(8,128)(2,1)S(1)}, u32[]{:S(2)}, u32[]{:S(2)}) collective-permute-start(bf16[512,256]{1,0:T(8,128)(2,1)} %first.1), channel_id=1, source_target_pairs={{0,8},{1,9},{2,10},{3,11},{4,12},{5,13},{6,14},{7,15},{16,24},{17,... | collective-permute-start | bytes 786440 | tf_op jit(solution)/shard_map/ppermute | solution.py:29
  9.4 9.0 %collective-permute-start.5 = (bf16[512,256]{1,0:T(8,128)(2,1)}, bf16[512,256]{1,0:T(8,128)(2,1)S(1)}, u32[]{:S(2)}, u32[]{:S(2)}) collective-permute-start(bf16[512,256]{1,0:T(8,128)(2,1)} %first.1), channel_id=1, source_target_pairs={{0,2},{1,3},{2,4},{3,5},{4,6},{5,7},{6,0},{7,1},{16,18},{17,19},{1... | collective-permute-start | bytes 786440 | tf_op jit(solution)/shard_map/ppermute | solution.py:29
  10.6 7.7 %collective-permute-start.6 = (bf16[512,256]{1,0:T(8,128)(2,1)}, bf16[512,256]{1,0:T(8,128)(2,1)S(1)}, u32[]{:S(2)}, u32[]{:S(2)}) collective-permute-start(bf16[512,256]{1,0:T(8,128)(2,1)} %first.1), channel_id=1, source_target_pairs={{0,6},{1,7},{2,0},{3,1},{4,2},{5,3},{6,4},{7,5},{16,22},{17,23},{1... | collective-permute-start | bytes 786440 | tf_op jit(solution)/shard_map/ppermute | solution.py:29
  12.1 12.9 %collective-permute-start.7 = (bf16[512,256]{1,0:T(8,128)(2,1)}, bf16[512,256]{1,0:T(8,128)(2,1)S(1)}, u32[]{:S(2)}, u32[]{:S(2)}) collective-permute-start(bf16[512,256]{1,0:T(8,128)(2,1)} %first.1), channel_id=1, source_target_pairs={{0,4},{1,5},{2,6},{3,7},{4,0},{5,1},{6,2},{7,3},{16,20},{17,21},{1... | collective-permute-start | bytes 786440 | tf_op jit(solution)/shard_map/ppermute | solution.py:29
  16.8 27.7 %copy-start = (bf16[512,256]{1,0:T(8,128)(2,1)S(1)}, bf16[512,256]{1,0:T(8,128)(2,1)}, u32[]{:S(2)}) copy-start(bf16[512,256]{1,0:T(8,128)(2,1)} %grads.1) | copy-start | bytes 786436
  16.8 27.7 %copy-start.2 = (bf16[256,64]{0,1:T(8,128)(2,1)S(1)}, bf16[256,64]{0,1:T(8,128)(2,1)}, u32[]{:S(2)}) copy-start(bf16[256,64]{0,1:T(8,128)(2,1)} %param.11) | copy-start | bytes 98308
  18.3 12.0 %copy-start.3 = (bf16[512,256]{1,0:T(8,128)(2,1)}, bf16[512,256]{1,0:T(8,128)(2,1)S(1)}, u32[]{:S(2)}) copy-start(bf16[512,256]{1,0:T(8,128)(2,1)S(1)} %collective-permute-done.5.refs_0_) | copy-start | bytes 786436
  18.4 12.0 %copy-start.4 = (bf16[512,256]{1,0:T(8,128)(2,1)}, bf16[512,256]{1,0:T(8,128)(2,1)S(1)}, u32[]{:S(2)}) copy-start(bf16[512,256]{1,0:T(8,128)(2,1)S(1)} %collective-permute-done.6.refs_2_) | copy-start | bytes 786436
  24.9 5.4 %copy-start.5 = (bf16[512,256]{1,0:T(8,128)(2,1)}, bf16[512,256]{1,0:T(8,128)(2,1)S(1)}, u32[]{:S(2)}) copy-start(bf16[512,256]{1,0:T(8,128)(2,1)S(1)} %collective-permute-done.7.refs_4_) | copy-start | bytes 786436
  25.0 4.4 %collective-permute-start.10 = (bf16[512,256]{1,0:T(8,128)(2,1)S(1)}, bf16[512,256]{1,0:T(8,128)(2,1)S(1)}, u32[]{:S(2)}, u32[]{:S(2)}) collective-permute-start(bf16[512,256]{1,0:T(8,128)(2,1)S(1)} %collective-permute-done.7.refs_4_), channel_id=1, source_target_pairs={{0,1},{1,0},{2,3},{3,2},{4,5},{5,4},{6,7},{7,6},{16,17},{17,16},{1... | collective-permute-start | bytes 786440 | tf_op jit(solution)/shard_map/ppermute | solution.py:29
  26.1 3.6 %collective-permute-start.8 = (bf16[512,256]{1,0:T(8,128)(2,1)S(1)}, bf16[512,256]{1,0:T(8,128)(2,1)S(1)}, u32[]{:S(2)}, u32[]{:S(2)}) collective-permute-start(bf16[512,256]{1,0:T(8,128)(2,1)S(1)} %collective-permute-done.5.refs_0_), channel_id=1, source_target_pairs={{0,1},{1,0},{2,3},{3,2},{4,5},{5,4},{6,7},{7,6},{16,17},{17,16},{1... | collective-permute-start | bytes 786440 | tf_op jit(solution)/shard_map/ppermute | solution.py:29
  26.1 4.2 %collective-permute-start.9 = (bf16[512,256]{1,0:T(8,128)(2,1)S(1)}, bf16[512,256]{1,0:T(8,128)(2,1)S(1)}, u32[]{:S(2)}, u32[]{:S(2)}) collective-permute-start(bf16[512,256]{1,0:T(8,128)(2,1)S(1)} %collective-permute-done.6.refs_2_), channel_id=1, source_target_pairs={{0,1},{1,0},{2,3},{3,2},{4,5},{5,4},{6,7},{7,6},{16,17},{17,16},{1... | collective-permute-start | bytes 786440 | tf_op jit(solution)/shard_map/ppermute | solution.py:29
  26.7 9.9 %collective-permute-start.2 = (bf16[512,256]{1,0:T(8,128)(2,1)S(1)}, bf16[512,256]{1,0:T(8,128)(2,1)}, u32[]{:S(2)}, u32[]{:S(2)}) collective-permute-start(bf16[512,256]{1,0:T(8,128)(2,1)S(1)} %collective-permute-done.refs_0_), channel_id=1, source_target_pairs={{0,2},{1,3},{2,4},{3,5},{4,6},{5,7},{6,0},{7,1},{16,18},{17,19},{1... | collective-permute-start | bytes 786440 | tf_op jit(solution)/shard_map/ppermute | solution.py:29
  27.5 9.0 %collective-permute-start.3 = (bf16[512,256]{1,0:T(8,128)(2,1)S(1)}, bf16[512,256]{1,0:T(8,128)(2,1)}, u32[]{:S(2)}, u32[]{:S(2)}) collective-permute-start(bf16[512,256]{1,0:T(8,128)(2,1)S(1)} %collective-permute-done.refs_0_), channel_id=1, source_target_pairs={{0,6},{1,7},{2,0},{3,1},{4,2},{5,3},{6,4},{7,5},{16,22},{17,23},{1... | collective-permute-start | bytes 786440 | tf_op jit(solution)/shard_map/ppermute | solution.py:29
  29.3 1.1 %copy-start.6 = (bf16[512,256]{1,0:T(8,128)(2,1)}, bf16[512,256]{1,0:T(8,128)(2,1)S(1)}, u32[]{:S(2)}) copy-start(bf16[512,256]{1,0:T(8,128)(2,1)S(1)} %collective-permute-done.10.refs_5_) | copy-start | bytes 786436
  29.3 12.4 %collective-permute-start.4 = (bf16[512,256]{1,0:T(8,128)(2,1)S(1)}, bf16[512,256]{1,0:T(8,128)(2,1)}, u32[]{:S(2)}, u32[]{:S(2)}) collective-permute-start(bf16[512,256]{1,0:T(8,128)(2,1)S(1)} %collective-permute-done.refs_0_), channel_id=1, source_target_pairs={{0,4},{1,5},{2,6},{3,7},{4,0},{5,1},{6,2},{7,3},{16,20},{17,21},{1... | collective-permute-start | bytes 786440 | tf_op jit(solution)/shard_map/ppermute | solution.py:29
  29.7 0.7 copy-start.7
  29.7 13.4 %collective-permute-start.12 = (bf16[512,256]{1,0:T(8,128)(2,1)S(1)}, bf16[512,256]{1,0:T(8,128)(2,1)}, u32[]{:S(2)}, u32[]{:S(2)}) collective-permute-start(bf16[512,256]{1,0:T(8,128)(2,1)S(1)} %collective-permute-done.refs_0_), channel_id=1, source_target_pairs={{0,1},{1,0},{2,3},{3,2},{4,5},{5,4},{6,7},{7,6},{16,17},{17,16},{1... | collective-permute-start | bytes 786440 | tf_op jit(solution)/shard_map/ppermute | solution.py:29
  30.4 0.7 copy-start.8
  41.7 2.4 %collective-permute-start.13 = (bf16[512,256]{1,0:T(8,128)(2,1)}, bf16[512,256]{1,0:T(8,128)(2,1)}, u32[]{:S(2)}, u32[]{:S(2)}) collective-permute-start(bf16[512,256]{1,0:T(8,128)(2,1)} %collective-permute-done.2.refs_2_), channel_id=1, source_target_pairs={{0,1},{1,0},{2,3},{3,2},{4,5},{5,4},{6,7},{7,6},{16,17},{17,16},{1... | collective-permute-start | bytes 786440 | tf_op jit(solution)/shard_map/ppermute | solution.py:29
  42.6 1.9 %collective-permute-start.14 = (bf16[512,256]{1,0:T(8,128)(2,1)}, bf16[512,256]{1,0:T(8,128)(2,1)}, u32[]{:S(2)}, u32[]{:S(2)}) collective-permute-start(bf16[512,256]{1,0:T(8,128)(2,1)} %collective-permute-done.3.refs_4_), channel_id=1, source_target_pairs={{0,1},{1,0},{2,3},{3,2},{4,5},{5,4},{6,7},{7,6},{16,17},{17,16},{1... | collective-permute-start | bytes 786440 | tf_op jit(solution)/shard_map/ppermute | solution.py:29
  42.6 7.6 %collective-permute-start.11 = (bf16[512,256]{1,0:T(8,128)(2,1)}, bf16[512,256]{1,0:T(8,128)(2,1)}, u32[]{:S(2)}, u32[]{:S(2)}) collective-permute-start(bf16[512,256]{1,0:T(8,128)(2,1)} %collective-permute-done.4.first), channel_id=1, source_target_pairs={{0,1},{1,0},{2,3},{3,2},{4,5},{5,4},{6,7},{7,6},{16,17},{17,16},{1... | collective-permute-start | bytes 786440 | tf_op jit(solution)/shard_map/ppermute | solution.py:29
  44.5 5.7 %copy-start.1 = (bf16[688,64]{0,1:T(8,128)(2,1)S(1)}, bf16[688,64]{0,1:T(8,128)(2,1)}, u32[]{:S(2)}) copy-start(bf16[688,64]{0,1:T(8,128)(2,1)} %param.10) | copy-start | bytes 264196
  52.8 1.5 %collective-permute-start.15 = (f32[2,4,32,128]{3,2,1,0:T(8,128)S(1)}, f32[2,4,32,128]{3,2,1,0:T(8,128)S(1)}, u32[]{:S(2)}, u32[]{:S(2)}) collective-permute-start(f32[2,4,32,128]{3,2,1,0:T(8,128)S(1)} %dynamic-slice_bitcast_fusion), channel_id=1, source_target_pairs={{0,1},{1,0},{2,3},{3,2},{4,5},{5,4},{6,7},{7,6},{16,17},{17,16},{1... | collective-permute-start | bytes 393224 | tf_op jit(solution)/shard_map/ppermute | solution.py:29
  54.3 4.1 %collective-permute-start.16 = (f32[2,32,128]{2,1,0:T(8,128)S(1)}, f32[2,32,128]{2,1,0:T(8,128)S(1)}, u32[]{:S(2)}, u32[]{:S(2)}) collective-permute-start(f32[2,32,128]{2,1,0:T(8,128)S(1)} %get-tuple-element.30), channel_id=1, source_target_pairs={{0,2},{1,3},{2,4},{3,5},{4,6},{5,7},{6,0},{7,1},{16,18},{17,19},{1... | collective-permute-start | bytes 98312 | tf_op jit(solution)/shard_map/ppermute | solution.py:29
  55.3 3.1 %collective-permute-start.17 = (f32[2,32,128]{2,1,0:T(8,128)S(1)}, f32[2,32,128]{2,1,0:T(8,128)S(1)}, u32[]{:S(2)}, u32[]{:S(2)}) collective-permute-start(f32[2,32,128]{2,1,0:T(8,128)S(1)} %get-tuple-element.32), channel_id=1, source_target_pairs={{0,6},{1,7},{2,0},{3,1},{4,2},{5,3},{6,4},{7,5},{16,22},{17,23},{1... | collective-permute-start | bytes 98312 | tf_op jit(solution)/shard_map/ppermute | solution.py:29
  57.1 4.3 %collective-permute-start.18 = (f32[2,32,128]{2,1,0:T(8,128)S(1)}, f32[2,32,128]{2,1,0:T(8,128)S(1)}, u32[]{:S(2)}, u32[]{:S(2)}) collective-permute-start(f32[2,32,128]{2,1,0:T(8,128)S(1)} %get-tuple-element.31), channel_id=1, source_target_pairs={{0,4},{1,5},{2,6},{3,7},{4,0},{5,1},{6,2},{7,3},{16,20},{17,21},{1... | collective-permute-start | bytes 98312 | tf_op jit(solution)/shard_map/ppermute | solution.py:29
  91.3 7.1 %collective-permute-start.19 = (bf16[128,4096]{1,0:T(8,128)(2,1)S(1)}, bf16[128,4096]{1,0:T(8,128)(2,1)S(1)}, u32[]{:S(2)}, u32[]{:S(2)}) collective-permute-start(bf16[128,4096]{1,0:T(8,128)(2,1)S(1)} %bitcast.43), channel_id=1, source_target_pairs={{0,1},{1,0},{2,3},{3,2},{4,5},{5,4},{6,7},{7,6},{16,17},{17,16},{1... | collective-permute-start | bytes 3145736 | tf_op jit(solution)/shard_map/ppermute | solution.py:29

commit v3 on v2

v3 whole, which is shorter than its diff:
```python
import functools

import jax
import jax.numpy as jnp
from jax import lax
from jax.experimental import pallas as pl
from jax.experimental.pallas import tpu as pltpu
from jax.sharding import PartitionSpec as P

SEQ = 32
BOTH = ("ex", "par")


def pairs(move):
    def index(z, y, x, core):
        z, y, x = z % 8, y % 4, x % 4
        return ((z % 4) * 4 + y) * 16 + (z // 4) * 8 + x * 2 + core

    return [
        (index(z, y, x, c), index(*move(z, y, x, c)))
        for z in range(8)
        for y in range(4)
        for x in range(4)
        for c in range(2)
    ]


def send(value, move):
    return lax.ppermute(value, BOTH, pairs(move))


def shift_x(n):
    return lambda z, y, x, c: (z, y, x + n, c)


def shift_z(n):
    return lambda z, y, x, c: (z + n, y, x, c)


def other_core(z, y, x, c):
    return (z, y, x, 1 - c)


VMEM = pltpu.VMEM
ROWS_TIMES_ROWS = (((1,), (1,)), ((), ()))
LINES = [[(z % 4 * 4 + y) * 16 + z // 4 * 8 + n for z in range(8)] for y in range(4) for n in range(8)]
PLANES = [
    [(z % 4 * 4 + y) * 16 + z // 4 * 8 + x * 2 + c for x in range(4) for y in range(4)]
    for z in range(8)
    for c in range(2)
]


PARTS = ((0, 1), (1, 3), (4, 3), (7, 1))


def stage_kernel(starts, inputs, gate, up, held, *refs):
    outs, sem, sems = refs[:4], refs[4], refs[5]
    units = gate.shape[0]
    copies = [pltpu.make_async_copy(inputs, held, sem)]
    for out, (first, count) in zip(outs, PARTS):
        for n in range(2 * count):
            cols = pl.ds(pl.multiple_of(starts[2 * first + n], 256), 256)
            for m, source in enumerate((gate, up)):
                to = out.at[pl.ds(m * units, units), pl.ds(n * 256, 256)]
                copies.append(pltpu.make_async_copy(source.at[:, cols], to, sems.at[2 * first + n, m]))
    for c in copies:
        c.start()
    for c in copies:
        c.wait()


def product(weights, j, first, second):
    held = jnp.concatenate([first[...], second[...]], axis=1)
    cols = weights[:, j * 512 : (j + 1) * 512]
    return lax.dot_general(cols, held, ROWS_TIMES_ROWS, preferred_element_type=jnp.float32)


def own_kernel(first, second, weights, out):
    out[...] = product(weights, 0, first, second)


def three_chips(blocks, weights, near, out):
    out[...] = product(weights, 0, *blocks[:2]) + near[...]
    for j in range(1, 3):
        out[...] += product(weights, j, *blocks[2 * j : 2 * j + 2])


def near_kernel(*refs):
    blocks, (weights, near, out) = refs[:6], refs[6:]
    three_chips(blocks, weights, near, out)


def middle_kernel(grads, proj_model, *refs):
    blocks, (weights, near, out, right) = refs[:6], refs[6:]
    right[...] = lax.dot_general(grads[...], proj_model[...], ROWS_TIMES_ROWS, preferred_element_type=jnp.float32)
    three_chips(blocks, weights, near, out)


def last_kernel(starts, proj, first, second, weights, sums, right, keep, give, whole):
    units = proj.shape[1]
    value = product(weights, 0, first, second) + sums[...]
    gate, up = value[:units], value[units:]
    hidden = (gate / (1.0 + jnp.exp(-gate)) * up).astype(jnp.bfloat16)
    left = jnp.dot(proj[...], hidden, preferred_element_type=jnp.float32)
    whole[:, :64] = left.T
    whole[:, 64:] = right[...]
    par = starts[16]
    core, x = lax.rem(par, 2), lax.rem(par // 2, 4)
    for n in range(4):
        for z_hi in range(2):
            first_row = (z_hi * 4 + lax.rem(x + n, 4)) * 2 * SEQ
            for out, side in ((keep, core), (give, 1 - core)):
                rows = pl.ds(pl.multiple_of(first_row + side * SEQ, SEQ), SEQ)
                out[n, z_hi] = whole[rows]


def call(kernel, name, out, flops, scalars, anywhere, in_hbm, copied, in_vmem, scratch):
    vmem = pl.BlockSpec(memory_space=VMEM)
    return pl.pallas_call(
        kernel,
        out_shape=[VMEM(shape, dtype) for shape, dtype in out],
        in_specs=[pl.BlockSpec(memory_space=pltpu.SMEM)] * len(scalars)
        + [pl.BlockSpec(memory_space=pl.ANY)] * len(anywhere)
        + [pl.BlockSpec(memory_space=pltpu.HBM)] * len(in_hbm)
        + [vmem] * (len(copied) + len(in_vmem)),
        out_specs=[vmem] * len(out),
        scratch_shapes=scratch,
        compiler_params=pltpu.CompilerParams(vmem_limit_bytes=16 * 1024 * 1024),
        cost_estimate=pl.CostEstimate(flops=flops, bytes_accessed=0, transcendentals=0),
        name=name,
    )(
        *scalars,
        *anywhere,
        *[pltpu.with_memory_space_constraint(v, pltpu.HBM) for v in in_hbm],
        *copied,
        *[pltpu.with_memory_space_constraint(v, VMEM) for v in in_vmem],
    )


def on_device(inputs, w_gate, w_up, out_grads, proj_hidden, proj_model):
    rows, units = inputs.shape[0], w_gate.shape[1]
    par, ex = lax.axis_index("par"), lax.axis_index("ex")
    z_hi, x, core = par // 8, (par // 2) % 4, par % 2

    far = send(inputs, shift_z(4))
    sibling = send(inputs, other_core)
    own, sibling = lax.optimization_barrier((inputs, sibling))
    by_x = [send(own, shift_x(n)) for n in (2, 1, 3)]
    by_x = by_x[1:] + by_x[:1]

    chips = jnp.stack([x, (x + 3) % 4, (x + 1) % 4, (x + 2) % 4])
    cores = jnp.stack([core, 1 - core])
    starts = jnp.stack([z_hi, 1 - z_hi])[:, None, None] * 2048 + chips[:, None] * 512 + cores * 256
    starts = jnp.concatenate([starts.reshape(16), jnp.stack([par, ex])]).astype(jnp.int32)
    w_gate, w_up = w_gate.T, w_up.T
    sums_type, bf16 = ((2 * units, rows), jnp.float32), jnp.bfloat16
    flops = 4 * rows * units * 512
    held, *weights = call(
        stage_kernel,
        "stage",
        [((rows, 256), bf16)] + [((2 * units, 512 * count), bf16) for _, count in PARTS],
        0,
        [starts],
        [],
        [inputs, w_gate, w_up],
        [],
        [],
        [pltpu.SemaphoreType.DMA(()), pltpu.SemaphoreType.DMA((16, 2))],
    )
    far, sibling, held, *weights = lax.optimization_barrier((far, sibling, held, *weights))
    (sums,) = call(own_kernel, "own", [sums_type], flops, [], [], [], [], [held, sibling, weights[0]], [])
    far = [far] + [send(far, shift_x(n)) for n in (1, 3, 2)]
    *by_x, _ = lax.optimization_barrier((*by_x, far[0]))
    near_all = [b for n in by_x for b in (n, send(n, other_core))]
    (sums,) = call(
        near_kernel, "near", [sums_type], 3 * flops, [], [], [], [], [*near_all, weights[1], sums], []
    )
    far[1], far[2], sums = lax.optimization_barrier((far[1], far[2], sums))
    far_all = [b for n in far for b in (n, send(n, other_core))]
    sums, right = call(
        middle_kernel,
        "middle",
        [sums_type, ((rows, 64), jnp.float32)],
        3 * flops,
        [],
        [],
        [],
        [out_grads, proj_model.T],
        [*far_all[:6], weights[2], sums],
        [],
    )
    keep, give = call(
        last_kernel,
        "last",
        [((4, 2, SEQ, 128), jnp.float32)] * 2,
        flops,
        [starts],
        [],
        [],
        [proj_hidden.T],
        [*far_all[6:], weights[3], sums, right],
        [VMEM((rows, 128), jnp.float32)],
    )
    keep, give, par, ex = lax.optimization_barrier((keep, give, par, ex))

    keep = keep + send(give, other_core)
    part = keep[0] + sum(send(keep[n], shift_x(n)) for n in (1, 3, 2))

    part = jnp.broadcast_to(part.astype(jnp.bfloat16), (8, *part.shape))
    along = lax.all_to_all(part, BOTH, 0, 0, axis_index_groups=LINES).astype(jnp.float32)
    total = (along[:4] + along[4:]).reshape(8, SEQ, 128)
    outer = jnp.einsum("eta,etb->eab", total[..., :64], total[..., 64:], precision=lax.Precision.HIGHEST)
    feats = outer.reshape(8, 4096) / jnp.sqrt(jnp.float32(SEQ))
    features = lax.dynamic_slice_in_dim(feats, ex // 4 * 2 + par // 8, 1, 0)

    feats = jnp.broadcast_to(feats.astype(jnp.bfloat16), (16, 8, 4096))
    feats = lax.all_to_all(feats, BOTH, 0, 0, axis_index_groups=PLANES).reshape(128, 4096)
    feats = jnp.concatenate([feats, send(feats, other_core)])
    mine = lax.dynamic_slice_in_dim(feats, par * 256, 256, 1)
    gram = jnp.dot(mine.T, feats, preferred_element_type=jnp.float32) * (1.0 / 256)
    return (features, gram)


def solution(mesh):
    placed = (
        P("ex", "par"),
        P(None, "par"),
        P(None, "par"),
        P("ex", "par"),
        P("par", None),
        P("par", None),
    )
    return jax.shard_map(
        on_device,
        mesh=mesh,
        in_specs=placed,
        out_specs=(P(("ex", "par"), None), P("par", None)),
        check_vma=False,
    )
```

time: 101 us -> 97.1 us (0.961)
  waiting for transfers between devices: 20.8 us -> 14.8 us
  starting transfers between devices: 28.5 us -> 34.2 us
  Pallas kernels: 16.7 us -> 13.1 us
    ppermute x20, waiting for transfers between devices: 20.8 us -> 14.8 us  [send(): return lax.ppermute(value, BOTH, pairs(move))]
    ppermute x20, starting transfers between devices: 28.5 us -> 34.2 us  [send(): return lax.ppermute(value, BOTH, pairs(move))]
    pallas_call x4 -> x5, Pallas kernels: 16.7 us -> 13.1 us  [call(): pl.pallas_call(kernel, out_shape=[VMEM(shape, dtype) for shape, dtype in...]
  transfers between devices with their start and end apart: 20 -> 20, of which waited for: 10 -> 9; matrix products, arithmetic and copies ran while one was open for 1% -> 1% of each run, Pallas kernels for 14% -> 11%
where the time goes in v3:
time: 97.1 us; the launch traced here: 97 us
  starting transfers between devices  34.2 us (35%)
  blocking collectives  29.2 us (30%)
  waiting for transfers between devices  14.8 us (15%)
  Pallas kernels  13.1 us (13%)
  matrix products  3.45 us (4%)
    ppermute x20, starting transfers between devices, send(): return lax.ppermute(value, BOTH, pairs(move))  34.2 us
    all_to_all x1, blocking collectives, on_device(): lax.all_to_all(feats, BOTH, 0, 0, axis_index_groups=PLANES)  18.4 us
    ppermute x20, waiting for transfers between devices, send(): return lax.ppermute(value, BOTH, pairs(move))  14.8 us
    pallas_call x5, Pallas kernels, call(): pl.pallas_call(kernel, out_shape=[VMEM(shape, dtype) for shape, dtype in...  13.1 us
    all_to_all x1, blocking collectives, on_device(): lax.all_to_all(part, BOTH, 0, 0, axis_index_groups=LINES)  10.7 us
    dot_general x1, matrix products, on_device(): jnp.dot(mine.T, feats, preferred_element_type=jnp.float32) * (1.0 / 256)  2.77 us
  transfers between devices with their start and end apart: 20, of which 9 were waited for; matrix products, arithmetic and copies ran while one was open for 1% of the time, Pallas kernels for 11%

profile of v3, /device:TPU:1, one launch (start us, length us, event | category | flops | bytes accessed | tf_op | source)
XLA Modules:
  0.0 97.0 jit_solution(12815034221451977609)
XLA Ops:
  0.6 3.3 %collective-permute-start.1 = (bf16[512,256]{1,0:T(8,128)(2,1)}, bf16[512,256]{1,0:T(8,128)(2,1)S(1)}, u32[]{:S(2)}, u32[]{:S(2)}) collective-permute-start(bf16[512,256]{1,0:T(8,128)(2,1)} %inputs.1), channel_id=1, source_target_pairs={{0,1},{1,0},{2,3},{3,2},{4,5},{5,4},{6,7},{7,6},{16,17},{17,16},{1... | collective-permute-start | bytes 786440 | tf_op jit(solution)/shard_map/ppermute | solution.py:29
  4.0 5.2 %collective-permute-start = (bf16[512,256]{1,0:T(8,128)(2,1)}, bf16[512,256]{1,0:T(8,128)(2,1)S(1)}, u32[]{:S(2)}, u32[]{:S(2)}) collective-permute-start(bf16[512,256]{1,0:T(8,128)(2,1)} %inputs.1), channel_id=1, source_target_pairs={{0,8},{1,9},{2,10},{3,11},{4,12},{5,13},{6,14},{7,15},{16,24},{17,... | collective-permute-start | bytes 786440 | tf_op jit(solution)/shard_map/ppermute | solution.py:29
  9.2 0.1 add_multiply_fusion
  9.2 0.1 add_multiply_fusion.1
  9.3 0.1 broadcast_add_fusion.1
  9.4 1.2 %collective-permute-start.7 = (bf16[512,256]{1,0:T(8,128)(2,1)}, bf16[512,256]{1,0:T(8,128)(2,1)S(1)}, u32[]{:S(2)}, u32[]{:S(2)}) collective-permute-start(bf16[512,256]{1,0:T(8,128)(2,1)} %inputs.1), channel_id=1, source_target_pairs={{0,2},{1,3},{2,4},{3,5},{4,6},{5,7},{6,0},{7,1},{16,18},{17,19},{1... | collective-permute-start | bytes 786440 | tf_op jit(solution)/shard_map/ppermute | solution.py:29
  10.6 1.5 %collective-permute-start.8 = (bf16[512,256]{1,0:T(8,128)(2,1)}, bf16[512,256]{1,0:T(8,128)(2,1)S(1)}, u32[]{:S(2)}, u32[]{:S(2)}) collective-permute-start(bf16[512,256]{1,0:T(8,128)(2,1)} %inputs.1), channel_id=1, source_target_pairs={{0,6},{1,7},{2,0},{3,1},{4,2},{5,3},{6,4},{7,5},{16,22},{17,23},{1... | collective-permute-start | bytes 786440 | tf_op jit(solution)/shard_map/ppermute | solution.py:29
  12.1 1.5 %collective-permute-start.9 = (bf16[512,256]{1,0:T(8,128)(2,1)}, bf16[512,256]{1,0:T(8,128)(2,1)S(1)}, u32[]{:S(2)}, u32[]{:S(2)}) collective-permute-start(bf16[512,256]{1,0:T(8,128)(2,1)} %inputs.1), channel_id=1, source_target_pairs={{0,4},{1,5},{2,6},{3,7},{4,0},{5,1},{6,2},{7,3},{16,20},{17,21},{1... | collective-permute-start | bytes 786440 | tf_op jit(solution)/shard_map/ppermute | solution.py:29
  13.6 0.1 broadcast_add_fusion
  13.7 0.1 add.102
  13.8 0.1 pad_add_fusion.starts
  13.8 5.3 %stage.1 = (bf16[512,256]{1,0:T(8,128)(2,1)S(1)}, bf16[1376,512]{1,0:T(8,128)(2,1)S(1)}, bf16[1376,1536]{1,0:T(8,128)(2,1)S(1)}, bf16[1376,1536]{1,0:T(8,128)(2,1)S(1)}, bf16[1376,512]{1,0:T(8,128)(2,1)S(1)}) custom-call(s32[18]{0:T(128)S(1)} %pad_add_fusion.starts, bf16[512,256]{1,0:T(8,128)(2,1)} %inputs.1, bf16[688,4096]{1,0:T(8,128)(2,1)} %bitcast.32, ...), custom_call_target="tpu_custom_call" | custom-call | tf_op jit(solution)/shard_map/stage/pallas_call | solution.py:120
  19.1 0.0 collective-permute-done.refs_0_
  19.2 5.8 %collective-permute-done.9.refs_4_ = bf16[512,256]{1,0:T(8,128)(2,1)S(1)} collective-permute-done((bf16[512,256]{1,0:T(8,128)(2,1)}, bf16[512,256]{1,0:T(8,128)(2,1)S(1)}, u32[]{:S(2)}, u32[]{:S(2)}) %collective-permute-start.9) | collective-permute-done | bytes 262176 | tf_op jit(solution)/shard_map/ppermute | solution.py:29
  24.9 1.2 %collective-permute-start.10 = (bf16[512,256]{1,0:T(8,128)(2,1)S(1)}, bf16[512,256]{1,0:T(8,128)(2,1)S(1)}, u32[]{:S(2)}, u32[]{:S(2)}) collective-permute-start(bf16[512,256]{1,0:T(8,128)(2,1)S(1)} %collective-permute-done.7.refs_0_), channel_id=1, source_target_pairs={{0,1},{1,0},{2,3},{3,2},{4,5},{5,4},{6,7},{7,6},{16,17},{17,16},{1... | collective-permute-start | bytes 786440 | tf_op jit(solution)/shard_map/ppermute | solution.py:29
  26.1 0.0 collective-permute-start.11
  26.1 0.5 collective-permute-start.12
  26.7 0.9 collective-permute-start.5
  27.5 1.8 %collective-permute-start.6 = (bf16[512,256]{1,0:T(8,128)(2,1)S(1)}, bf16[512,256]{1,0:T(8,128)(2,1)S(1)}, u32[]{:S(2)}, u32[]{:S(2)}) collective-permute-start(bf16[512,256]{1,0:T(8,128)(2,1)S(1)} %collective-permute-done.refs_0_), channel_id=1, source_target_pairs={{0,6},{1,7},{2,0},{3,1},{4,2},{5,3},{6,4},{7,5},{16,22},{17,23},{1... | collective-permute-start | bytes 786440 | tf_op jit(solution)/shard_map/ppermute | solution.py:29
  29.3 0.9 own.1.refs_7_
  30.3 0.0 copy-start
  30.3 0.0 copy-start.2
  30.3 0.6 collective-permute-start.4
  31.0 2.4 %near.1.refs_7_ = f32[1376,512]{1,0:T(8,128)S(1)} custom-call(bf16[512,256]{1,0:T(8,128)(2,1)S(1)} %collective-permute-done.7.refs_0_, bf16[512,256]{1,0:T(8,128)(2,1)S(1)} %collective-permute-done.10.refs_1_, bf16[512,256]{1,0:T(8,128)(2,1)S(1)} %collective-permute-done.8.refs_2_, bf16[512,256]{1,0:T(8,128)(2,1)S(1)} %collective-permute-done.11.refs_3_, ...), custom_call_target="tpu_custom_call" | custom-call | flops 2164260864 | tf_op jit(solution)/shard_map/near/pallas_call | solution.py:120
  33.3 2.5 %collective-permute-done.5.refs_2_ = bf16[512,256]{1,0:T(8,128)(2,1)S(1)} collective-permute-done((bf16[512,256]{1,0:T(8,128)(2,1)S(1)}, bf16[512,256]{1,0:T(8,128)(2,1)S(1)}, u32[]{:S(2)}, u32[]{:S(2)}) %collective-permute-start.5) | collective-permute-done | bytes 262176 | tf_op jit(solution)/shard_map/ppermute | solution.py:29
  35.8 5.7 %collective-permute-start.13 = (bf16[512,256]{1,0:T(8,128)(2,1)S(1)}, bf16[512,256]{1,0:T(8,128)(2,1)S(1)}, u32[]{:S(2)}, u32[]{:S(2)}) collective-permute-start(bf16[512,256]{1,0:T(8,128)(2,1)S(1)} %collective-permute-done.5.refs_2_), channel_id=1, source_target_pairs={{0,1},{1,0},{2,3},{3,2},{4,5},{5,4},{6,7},{7,6},{16,17},{17,16},{1... | collective-permute-start | bytes 786440 | tf_op jit(solution)/shard_map/ppermute | solution.py:29
  41.5 0.1 collective-permute-done.2.first
  41.6 0.8 collective-permute-start.3
  42.4 0.3 collective-permute-done.13.refs_3_
  42.7 0.4 collective-permute-done.14.refs_5_
  43.0 2.4 %middle.1 = (f32[1376,512]{1,0:T(8,128)S(1)}, f32[512,64]{1,0:T(8,128)S(1)}) custom-call(bf16[512,256]{1,0:T(8,128)(2,1)S(1)} %copy-done, bf16[64,256]{1,0:T(8,128)(2,1)S(1)} %bitcast.29, bf16[512,256]{1,0:T(8,128)(2,1)S(1)} %collective-permute-done.refs_0_, bf16[512,256]{1,0:T(8,128)(2,1)S(1)} %collective-permute-done.4.refs_1_, ...), custom_call_target="tpu_custom_call" | custom-call | flops 2164260864 | tf_op jit(solution)/shard_map/middle/pallas_call | solution.py:120
  45.5 2.1 %last.1 = (f32[4,2,32,128]{3,2,1,0:T(8,128)S(1)}, f32[4,2,32,128]{3,2,1,0:T(8,128)S(1)}) custom-call(s32[18]{0:T(128)S(1)} %pad_add_fusion.starts, bf16[64,688]{1,0:T(8,128)(2,1)S(1)} %bitcast.28, bf16[512,256]{1,0:T(8,128)(2,1)S(1)} %collective-permute-done.2.first, bf16[512,256]{1,0:T(8,128)(2,1)S(1)} %collective-permute-done.3.second, ...), custom_call_target="tpu_custom_call" | custom-call | flops 721420288 | tf_op jit(solution)/shard_map/last/pallas_call | solution.py:120
  47.6 0.5 collective-permute-start.15
  48.1 1.0 %collective-permute-done.15 = f32[4,2,32,128]{3,2,1,0:T(8,128)S(1)} collective-permute-done((f32[4,2,32,128]{3,2,1,0:T(8,128)S(1)}, f32[4,2,32,128]{3,2,1,0:T(8,128)S(1)}, u32[]{:S(2)}, u32[]{:S(2)}) %collective-permute-start.15) | collective-permute-done | bytes 131104 | tf_op jit(solution)/shard_map/ppermute | solution.py:29
  49.1 0.3 collective-permute-start.16
  49.4 3.2 %collective-permute-start.17 = (f32[2,32,128]{2,1,0:T(8,128)S(1)}, f32[2,32,128]{2,1,0:T(8,128)S(1)}, u32[]{:S(2)}, u32[]{:S(2)}) collective-permute-start(f32[2,32,128]{2,1,0:T(8,128)S(1)} %get-tuple-element.58), channel_id=1, source_target_pairs={{0,6},{1,7},{2,0},{3,1},{4,2},{5,3},{6,4},{7,5},{16,22},{17,23},{1... | collective-permute-start | bytes 98312 | tf_op jit(solution)/shard_map/ppermute | solution.py:29
  52.7 1.1 %collective-permute-start.18 = (f32[2,32,128]{2,1,0:T(8,128)S(1)}, f32[2,32,128]{2,1,0:T(8,128)S(1)}, u32[]{:S(2)}, u32[]{:S(2)}) collective-permute-start(f32[2,32,128]{2,1,0:T(8,128)S(1)} %get-tuple-element.59), channel_id=1, source_target_pairs={{0,4},{1,5},{2,6},{3,7},{4,0},{5,1},{6,2},{7,3},{16,20},{17,21},{1... | collective-permute-start | bytes 98312 | tf_op jit(solution)/shard_map/ppermute | solution.py:29
  53.7 0.1 collective-permute-done.16
  53.9 3.1 %collective-permute-done.18 = f32[2,32,128]{2,1,0:T(8,128)S(1)} collective-permute-done((f32[2,32,128]{2,1,0:T(8,128)S(1)}, f32[2,32,128]{2,1,0:T(8,128)S(1)}, u32[]{:S(2)}, u32[]{:S(2)}) %collective-permute-start.18) | collective-permute-done | bytes 32800 | tf_op jit(solution)/shard_map/ppermute | solution.py:29
  57.0 10.7 %all_to_all.10 = bf16[8,2,32,128]{3,2,1,0:T(8,128)(2,1)S(1)} all-to-all(bf16[8,2,32,128]{3,2,1,0:T(8,128)(2,1)S(1)} %broadcast_in_dim.4), channel_id=1, replica_groups={{0,64,128,192,8,72,136,200},{1,65,129,193,9,73,137,201},{2,66,130,194,1..., dimensions={0} | all-to-all | bytes 262144 | tf_op jit(solution)/shard_map/all_to_all | solution.py:211
  67.8 0.7 convolution_multiply_fusion.1
  68.4 0.1 div.45
  68.6 0.1 broadcast_in_dim.5
  68.7 18.4 %all_to_all.11 = bf16[16,8,4096]{2,1,0:T(8,128)(2,1)S(1)} all-to-all(bf16[16,8,4096]{2,1,0:T(8,128)(2,1)S(1)} %broadcast_in_dim.5), channel_id=1, replica_groups={{0,16,32,48,2,18,34,50,4,20,36,52,6,22,38,54},{1,17,33,49,3,19,35,51,5,..., dimensions={0} | all-to-all | bytes 2097152 | tf_op jit(solution)/shard_map/all_to_all | solution.py:218
  87.1 4.8 %collective-permute-start.19 = (bf16[128,4096]{1,0:T(8,128)(2,1)S(1)}, bf16[128,4096]{1,0:T(8,128)(2,1)S(1)}, u32[]{:S(2)}, u32[]{:S(2)}) collective-permute-start(bf16[128,4096]{1,0:T(8,128)(2,1)S(1)} %bitcast.30), channel_id=1, source_target_pairs={{0,1},{1,0},{2,3},{3,2},{4,5},{5,4},{6,7},{7,6},{16,17},{17,16},{1... | collective-permute-start | bytes 3145736 | tf_op jit(solution)/shard_map/ppermute | solution.py:29
  91.9 0.6 constant_dynamic-slice_fusion
  92.5 1.7 %collective-permute-done.19 = bf16[128,4096]{1,0:T(8,128)(2,1)S(1)} collective-permute-done((bf16[128,4096]{1,0:T(8,128)(2,1)S(1)}, bf16[128,4096]{1,0:T(8,128)(2,1)S(1)}, u32[]{:S(2)}, u32[]{:S(2)}) %collective-permute-start.19) | collective-permute-done | bytes 1048608 | tf_op jit(solution)/shard_map/ppermute | solution.py:29
  94.2 2.8 %convolution_multiply_fusion = f32[256,4096]{1,0:T(8,128)} fusion(bf16[128,4096]{1,0:T(8,128)(2,1)S(1)} %collective-permute-done.19, bf16[128,4096]{1,0:T(8,128)(2,1)S(1)} %bitcast.31, s32[]{:T(128)S(6)} %select_n.52), kind=kOutput, calls=%fused_computation | convolution fusion | flops 542375936 | bytes 8388612 | tf_op jit(solution)/shard_map/dot_general | solution.py:221
  (23 shorter events, 0.1 us)
Async XLA Ops:
  0.6 8.8 %collective-permute-start.1 = (bf16[512,256]{1,0:T(8,128)(2,1)}, bf16[512,256]{1,0:T(8,128)(2,1)S(1)}, u32[]{:S(2)}, u32[]{:S(2)}) collective-permute-start(bf16[512,256]{1,0:T(8,128)(2,1)} %inputs.1), channel_id=1, source_target_pairs={{0,1},{1,0},{2,3},{3,2},{4,5},{5,4},{6,7},{7,6},{16,17},{17,16},{1... | collective-permute-start | bytes 786440 | tf_op jit(solution)/shard_map/ppermute | solution.py:29
  4.0 15.2 %collective-permute-start = (bf16[512,256]{1,0:T(8,128)(2,1)}, bf16[512,256]{1,0:T(8,128)(2,1)S(1)}, u32[]{:S(2)}, u32[]{:S(2)}) collective-permute-start(bf16[512,256]{1,0:T(8,128)(2,1)} %inputs.1), channel_id=1, source_target_pairs={{0,8},{1,9},{2,10},{3,11},{4,12},{5,13},{6,14},{7,15},{16,24},{17,... | collective-permute-start | bytes 786440 | tf_op jit(solution)/shard_map/ppermute | solution.py:29
  9.4 9.8 %collective-permute-start.7 = (bf16[512,256]{1,0:T(8,128)(2,1)}, bf16[512,256]{1,0:T(8,128)(2,1)S(1)}, u32[]{:S(2)}, u32[]{:S(2)}) collective-permute-start(bf16[512,256]{1,0:T(8,128)(2,1)} %inputs.1), channel_id=1, source_target_pairs={{0,2},{1,3},{2,4},{3,5},{4,6},{5,7},{6,0},{7,1},{16,18},{17,19},{1... | collective-permute-start | bytes 786440 | tf_op jit(solution)/shard_map/ppermute | solution.py:29
  10.6 8.6 %collective-permute-start.8 = (bf16[512,256]{1,0:T(8,128)(2,1)}, bf16[512,256]{1,0:T(8,128)(2,1)S(1)}, u32[]{:S(2)}, u32[]{:S(2)}) collective-permute-start(bf16[512,256]{1,0:T(8,128)(2,1)} %inputs.1), channel_id=1, source_target_pairs={{0,6},{1,7},{2,0},{3,1},{4,2},{5,3},{6,4},{7,5},{16,22},{17,23},{1... | collective-permute-start | bytes 786440 | tf_op jit(solution)/shard_map/ppermute | solution.py:29
  12.1 12.9 %collective-permute-start.9 = (bf16[512,256]{1,0:T(8,128)(2,1)}, bf16[512,256]{1,0:T(8,128)(2,1)S(1)}, u32[]{:S(2)}, u32[]{:S(2)}) collective-permute-start(bf16[512,256]{1,0:T(8,128)(2,1)} %inputs.1), channel_id=1, source_target_pairs={{0,4},{1,5},{2,6},{3,7},{4,0},{5,1},{6,2},{7,3},{16,20},{17,21},{1... | collective-permute-start | bytes 786440 | tf_op jit(solution)/shard_map/ppermute | solution.py:29
  24.9 5.3 %collective-permute-start.10 = (bf16[512,256]{1,0:T(8,128)(2,1)S(1)}, bf16[512,256]{1,0:T(8,128)(2,1)S(1)}, u32[]{:S(2)}, u32[]{:S(2)}) collective-permute-start(bf16[512,256]{1,0:T(8,128)(2,1)S(1)} %collective-permute-done.7.refs_0_), channel_id=1, source_target_pairs={{0,1},{1,0},{2,3},{3,2},{4,5},{5,4},{6,7},{7,6},{16,17},{17,16},{1... | collective-permute-start | bytes 786440 | tf_op jit(solution)/shard_map/ppermute | solution.py:29
  26.1 4.8 %collective-permute-start.11 = (bf16[512,256]{1,0:T(8,128)(2,1)S(1)}, bf16[512,256]{1,0:T(8,128)(2,1)S(1)}, u32[]{:S(2)}, u32[]{:S(2)}) collective-permute-start(bf16[512,256]{1,0:T(8,128)(2,1)S(1)} %collective-permute-done.8.refs_2_), channel_id=1, source_target_pairs={{0,1},{1,0},{2,3},{3,2},{4,5},{5,4},{6,7},{7,6},{16,17},{17,16},{1... | collective-permute-start | bytes 786440 | tf_op jit(solution)/shard_map/ppermute | solution.py:29
  26.1 4.8 %collective-permute-start.12 = (bf16[512,256]{1,0:T(8,128)(2,1)S(1)}, bf16[512,256]{1,0:T(8,128)(2,1)S(1)}, u32[]{:S(2)}, u32[]{:S(2)}) collective-permute-start(bf16[512,256]{1,0:T(8,128)(2,1)S(1)} %collective-permute-done.9.refs_4_), channel_id=1, source_target_pairs={{0,1},{1,0},{2,3},{3,2},{4,5},{5,4},{6,7},{7,6},{16,17},{17,16},{1... | collective-permute-start | bytes 786440 | tf_op jit(solution)/shard_map/ppermute | solution.py:29
  26.7 9.1 %collective-permute-start.5 = (bf16[512,256]{1,0:T(8,128)(2,1)S(1)}, bf16[512,256]{1,0:T(8,128)(2,1)S(1)}, u32[]{:S(2)}, u32[]{:S(2)}) collective-permute-start(bf16[512,256]{1,0:T(8,128)(2,1)S(1)} %collective-permute-done.refs_0_), channel_id=1, source_target_pairs={{0,2},{1,3},{2,4},{3,5},{4,6},{5,7},{6,0},{7,1},{16,18},{17,19},{1... | collective-permute-start | bytes 786440 | tf_op jit(solution)/shard_map/ppermute | solution.py:29
  27.5 8.3 %collective-permute-start.6 = (bf16[512,256]{1,0:T(8,128)(2,1)S(1)}, bf16[512,256]{1,0:T(8,128)(2,1)S(1)}, u32[]{:S(2)}, u32[]{:S(2)}) collective-permute-start(bf16[512,256]{1,0:T(8,128)(2,1)S(1)} %collective-permute-done.refs_0_), channel_id=1, source_target_pairs={{0,6},{1,7},{2,0},{3,1},{4,2},{5,3},{6,4},{7,5},{16,22},{17,23},{1... | collective-permute-start | bytes 786440 | tf_op jit(solution)/shard_map/ppermute | solution.py:29
  30.3 12.8 %copy-start = (bf16[512,256]{1,0:T(8,128)(2,1)S(1)}, bf16[512,256]{1,0:T(8,128)(2,1)}, u32[]{:S(2)}) copy-start(bf16[512,256]{1,0:T(8,128)(2,1)} %grads.1) | copy-start | bytes 786436
  30.3 12.8 %copy-start.2 = (bf16[256,64]{0,1:T(8,128)(2,1)S(1)}, bf16[256,64]{0,1:T(8,128)(2,1)}, u32[]{:S(2)}) copy-start(bf16[256,64]{0,1:T(8,128)(2,1)} %param.11) | copy-start | bytes 98308
  30.3 12.1 %collective-permute-start.4 = (bf16[512,256]{1,0:T(8,128)(2,1)S(1)}, bf16[512,256]{1,0:T(8,128)(2,1)S(1)}, u32[]{:S(2)}, u32[]{:S(2)}) collective-permute-start(bf16[512,256]{1,0:T(8,128)(2,1)S(1)} %collective-permute-done.refs_0_), channel_id=1, source_target_pairs={{0,1},{1,0},{2,3},{3,2},{4,5},{5,4},{6,7},{7,6},{16,17},{17,16},{1... | collective-permute-start | bytes 786440 | tf_op jit(solution)/shard_map/ppermute | solution.py:29
  30.9 10.7 %collective-permute-start.2 = (bf16[512,256]{1,0:T(8,128)(2,1)S(1)}, bf16[512,256]{1,0:T(8,128)(2,1)S(1)}, u32[]{:S(2)}, u32[]{:S(2)}) collective-permute-start(bf16[512,256]{1,0:T(8,128)(2,1)S(1)} %collective-permute-done.refs_0_), channel_id=1, source_target_pairs={{0,4},{1,5},{2,6},{3,7},{4,0},{5,1},{6,2},{7,3},{16,20},{17,21},{1... | collective-permute-start | bytes 786440 | tf_op jit(solution)/shard_map/ppermute | solution.py:29
  35.8 6.9 %collective-permute-start.13 = (bf16[512,256]{1,0:T(8,128)(2,1)S(1)}, bf16[512,256]{1,0:T(8,128)(2,1)S(1)}, u32[]{:S(2)}, u32[]{:S(2)}) collective-permute-start(bf16[512,256]{1,0:T(8,128)(2,1)S(1)} %collective-permute-done.5.refs_2_), channel_id=1, source_target_pairs={{0,1},{1,0},{2,3},{3,2},{4,5},{5,4},{6,7},{7,6},{16,17},{17,16},{1... | collective-permute-start | bytes 786440 | tf_op jit(solution)/shard_map/ppermute | solution.py:29
  41.5 1.5 %collective-permute-start.14 = (bf16[512,256]{1,0:T(8,128)(2,1)S(1)}, bf16[512,256]{1,0:T(8,128)(2,1)S(1)}, u32[]{:S(2)}, u32[]{:S(2)}) collective-permute-start(bf16[512,256]{1,0:T(8,128)(2,1)S(1)} %collective-permute-done.6.refs_4_), channel_id=1, source_target_pairs={{0,1},{1,0},{2,3},{3,2},{4,5},{5,4},{6,7},{7,6},{16,17},{17,16},{1... | collective-permute-start | bytes 786440 | tf_op jit(solution)/shard_map/ppermute | solution.py:29
  41.6 3.8 %collective-permute-start.3 = (bf16[512,256]{1,0:T(8,128)(2,1)S(1)}, bf16[512,256]{1,0:T(8,128)(2,1)S(1)}, u32[]{:S(2)}, u32[]{:S(2)}) collective-permute-start(bf16[512,256]{1,0:T(8,128)(2,1)S(1)} %collective-permute-done.2.first), channel_id=1, source_target_pairs={{0,1},{1,0},{2,3},{3,2},{4,5},{5,4},{6,7},{7,6},{16,17},{17,16},{1... | collective-permute-start | bytes 786440 | tf_op jit(solution)/shard_map/ppermute | solution.py:29
  43.0 2.4 %copy-start.1 = (bf16[688,64]{0,1:T(8,128)(2,1)S(1)}, bf16[688,64]{0,1:T(8,128)(2,1)}, u32[]{:S(2)}) copy-start(bf16[688,64]{0,1:T(8,128)(2,1)} %param.10) | copy-start | bytes 264196
  47.6 1.4 %collective-permute-start.15 = (f32[4,2,32,128]{3,2,1,0:T(8,128)S(1)}, f32[4,2,32,128]{3,2,1,0:T(8,128)S(1)}, u32[]{:S(2)}, u32[]{:S(2)}) collective-permute-start(f32[4,2,32,128]{3,2,1,0:T(8,128)S(1)} %get-tuple-element.55), channel_id=1, source_target_pairs={{0,1},{1,0},{2,3},{3,2},{4,5},{5,4},{6,7},{7,6},{16,17},{17,16},{1... | collective-permute-start | bytes 393224 | tf_op jit(solution)/shard_map/ppermute | solution.py:29
  49.1 4.8 %collective-permute-start.16 = (f32[2,32,128]{2,1,0:T(8,128)S(1)}, f32[2,32,128]{2,1,0:T(8,128)S(1)}, u32[]{:S(2)}, u32[]{:S(2)}) collective-permute-start(f32[2,32,128]{2,1,0:T(8,128)S(1)} %get-tuple-element.60), channel_id=1, source_target_pairs={{0,2},{1,3},{2,4},{3,5},{4,6},{5,7},{6,0},{7,1},{16,18},{17,19},{1... | collective-permute-start | bytes 98312 | tf_op jit(solution)/shard_map/ppermute | solution.py:29
  49.4 4.4 %collective-permute-start.17 = (f32[2,32,128]{2,1,0:T(8,128)S(1)}, f32[2,32,128]{2,1,0:T(8,128)S(1)}, u32[]{:S(2)}, u32[]{:S(2)}) collective-permute-start(f32[2,32,128]{2,1,0:T(8,128)S(1)} %get-tuple-element.58), channel_id=1, source_target_pairs={{0,6},{1,7},{2,0},{3,1},{4,2},{5,3},{6,4},{7,5},{16,22},{17,23},{1... | collective-permute-start | bytes 98312 | tf_op jit(solution)/shard_map/ppermute | solution.py:29
  52.7 4.3 %collective-permute-start.18 = (f32[2,32,128]{2,1,0:T(8,128)S(1)}, f32[2,32,128]{2,1,0:T(8,128)S(1)}, u32[]{:S(2)}, u32[]{:S(2)}) collective-permute-start(f32[2,32,128]{2,1,0:T(8,128)S(1)} %get-tuple-element.59), channel_id=1, source_target_pairs={{0,4},{1,5},{2,6},{3,7},{4,0},{5,1},{6,2},{7,3},{16,20},{17,21},{1... | collective-permute-start | bytes 98312 | tf_op jit(solution)/shard_map/ppermute | solution.py:29
  87.1 7.1 %collective-permute-start.19 = (bf16[128,4096]{1,0:T(8,128)(2,1)S(1)}, bf16[128,4096]{1,0:T(8,128)(2,1)S(1)}, u32[]{:S(2)}, u32[]{:S(2)}) collective-permute-start(bf16[128,4096]{1,0:T(8,128)(2,1)S(1)} %bitcast.30), channel_id=1, source_target_pairs={{0,1},{1,0},{2,3},{3,2},{4,5},{5,4},{6,7},{7,6},{16,17},{17,16},{1... | collective-permute-start | bytes 3145736 | tf_op jit(solution)/shard_map/ppermute | solution.py:29

commit v4 on v3

--- a/solution.py
+++ b/solution.py
@@ -44,6 +44,7 @@
 VMEM = pltpu.VMEM
 ROWS_TIMES_ROWS = (((1,), (1,)), ((), ()))
 LINES = [[(z % 4 * 4 + y) * 16 + z // 4 * 8 + n for z in range(8)] for y in range(4) for n in range(8)]
+SQUARES = [[(z % 4 * 4 + y) * 16 + z // 4 * 8 + n for n in range(8)] for z in range(8) for y in range(4)]
 PLANES = [
     [(z % 4 * 4 + y) * 16 + z // 4 * 8 + x * 2 + c for x in range(4) for y in range(4)]
     for z in range(8)
@@ -97,7 +98,7 @@
     three_chips(blocks, weights, near, out)
 
 
-def last_kernel(starts, proj, first, second, weights, sums, right, keep, give, whole):
+def last_kernel(proj, first, second, weights, sums, right, out, whole):
     units = proj.shape[1]
     value = product(weights, 0, first, second) + sums[...]
     gate, up = value[:units], value[units:]
@@ -105,14 +106,10 @@
     left = jnp.dot(proj[...], hidden, preferred_element_type=jnp.float32)
     whole[:, :64] = left.T
     whole[:, 64:] = right[...]
-    par = starts[16]
-    core, x = lax.rem(par, 2), lax.rem(par // 2, 4)
-    for n in range(4):
+    for owner in range(8):
         for z_hi in range(2):
-            first_row = (z_hi * 4 + lax.rem(x + n, 4)) * 2 * SEQ
-            for out, side in ((keep, core), (give, 1 - core)):
-                rows = pl.ds(pl.multiple_of(first_row + side * SEQ, SEQ), SEQ)
-                out[n, z_hi] = whole[rows]
+            first_row = (z_hi * 8 + owner) * SEQ
+            out[owner, z_hi] = whole[first_row : first_row + SEQ].astype(out.dtype)
 
 
 def call(kernel, name, out, flops, scalars, anywhere, in_hbm, copied, in_vmem, scratch):
@@ -176,7 +173,7 @@
     (sums,) = call(
         near_kernel, "near", [sums_type], 3 * flops, [], [], [], [], [*near_all, weights[1], sums], []
     )
-    far[1], far[2], sums = lax.optimization_barrier((far[1], far[2], sums))
+    far[3], sums = lax.optimization_barrier((far[3], sums))
     far_all = [b for n in far for b in (n, send(n, other_core))]
     sums, right = call(
         middle_kernel,
@@ -190,22 +187,22 @@
         [*far_all[:6], weights[2], sums],
         [],
     )
-    keep, give = call(
+    (shares,) = call(
         last_kernel,
         "last",
-        [((4, 2, SEQ, 128), jnp.float32)] * 2,
+        [((8, 2, SEQ, 128), bf16)],
         flops,
-        [starts],
+        [],
         [],
         [],
         [proj_hidden.T],
         [*far_all[6:], weights[3], sums, right],
         [VMEM((rows, 128), jnp.float32)],
     )
-    keep, give, par, ex = lax.optimization_barrier((keep, give, par, ex))
-
-    keep = keep + send(give, other_core)
-    part = keep[0] + sum(send(keep[n], shift_x(n)) for n in (1, 3, 2))
+    shares, par, ex = lax.optimization_barrier((shares, par, ex))
+
+    shares = lax.all_to_all(shares, BOTH, 0, 0, axis_index_groups=SQUARES)
+    part = jnp.sum(shares.astype(jnp.float32), axis=0)
 
     part = jnp.broadcast_to(part.astype(jnp.bfloat16), (8, *part.shape))
     along = lax.all_to_all(part, BOTH, 0, 0, axis_index_groups=LINES).astype(jnp.float32)

time: 97.1 us -> 94.9 us (0.977)
  blocking collectives: 29.2 us -> 38.9 us
  starting transfers between devices: 34.2 us -> 25.5 us
  waiting for transfers between devices: 14.8 us -> 12.2 us
    ppermute x20 -> x16, starting transfers between devices: 34.2 us -> 25.5 us  [send(): return lax.ppermute(value, BOTH, pairs(move))]
    all_to_all x0 -> x1, blocking collectives: none -> 7.67 us  [on_device(): shares = lax.all_to_all(shares, BOTH, 0, 0, axis_index_groups=SQUARES)]
    ppermute x20 -> x16, waiting for transfers between devices: 14.8 us -> 12.2 us  [send(): return lax.ppermute(value, BOTH, pairs(move))]
    all_to_all x1, blocking collectives: 10.7 us -> 12.7 us  [on_device(): lax.all_to_all(part, BOTH, 0, 0, axis_index_groups=LINES)]
  transfers between devices with their start and end apart: 20 -> 16, of which waited for: 9 -> 4; matrix products, arithmetic and copies ran while one was open for 1% -> 1% of each run, Pallas kernels for 11% -> 12%
where the time goes in v4:
time: 94.9 us; the launch traced here: 94.7 us
  blocking collectives  38.9 us (41%)
  starting transfers between devices  25.5 us (27%)
  Pallas kernels  12.5 us (13%)
  waiting for transfers between devices  12.2 us (13%)
  matrix products  3.45 us (4%)
  local copies, waits for them, and re-layouts  0.95 us (1%)
    ppermute x16, starting transfers between devices, send(): return lax.ppermute(value, BOTH, pairs(move))  25.5 us
    all_to_all x1, blocking collectives, on_device(): lax.all_to_all(feats, BOTH, 0, 0, axis_index_groups=PLANES)  18.6 us
    all_to_all x1, blocking collectives, on_device(): lax.all_to_all(part, BOTH, 0, 0, axis_index_groups=LINES)  12.7 us
    pallas_call x5, Pallas kernels, call(): pl.pallas_call(kernel, out_shape=[VMEM(shape, dtype) for shape, dtype in...  12.5 us
    ppermute x16, waiting for transfers between devices, send(): return lax.ppermute(value, BOTH, pairs(move))  12.2 us
    all_to_all x1, blocking collectives, on_device(): shares = lax.all_to_all(shares, BOTH, 0, 0, axis_index_groups=SQUARES)  7.67 us
    dot_general x1, matrix products, on_device(): jnp.dot(mine.T, feats, preferred_element_type=jnp.float32) * (1.0 / 256)  2.77 us
  transfers between devices with their start and end apart: 16, of which 4 were waited for; matrix products, arithmetic and copies ran while one was open for 1% of the time, Pallas kernels for 12%

profile of v4, /device:TPU:1, one launch (start us, length us, event | category | flops | bytes accessed | tf_op | source)
XLA Modules:
  0.0 94.7 jit_solution(10797072607565395087)
XLA Ops:
  0.6 3.3 %collective-permute-start.1 = (bf16[512,256]{1,0:T(8,128)(2,1)}, bf16[512,256]{1,0:T(8,128)(2,1)S(1)}, u32[]{:S(2)}, u32[]{:S(2)}) collective-permute-start(bf16[512,256]{1,0:T(8,128)(2,1)} %inputs.1), channel_id=1, source_target_pairs={{0,1},{1,0},{2,3},{3,2},{4,5},{5,4},{6,7},{7,6},{16,17},{17,16},{1... | collective-permute-start | bytes 786440 | tf_op jit(solution)/shard_map/ppermute | solution.py:29
  4.0 5.2 %collective-permute-start = (bf16[512,256]{1,0:T(8,128)(2,1)}, bf16[512,256]{1,0:T(8,128)(2,1)S(1)}, u32[]{:S(2)}, u32[]{:S(2)}) collective-permute-start(bf16[512,256]{1,0:T(8,128)(2,1)} %inputs.1), channel_id=1, source_target_pairs={{0,8},{1,9},{2,10},{3,11},{4,12},{5,13},{6,14},{7,15},{16,24},{17,... | collective-permute-start | bytes 786440 | tf_op jit(solution)/shard_map/ppermute | solution.py:29
  9.2 0.1 add_multiply_fusion
  9.2 0.1 add_multiply_fusion.1
  9.3 0.1 broadcast_add_fusion.1
  9.4 1.2 %collective-permute-start.3 = (bf16[512,256]{1,0:T(8,128)(2,1)}, bf16[512,256]{1,0:T(8,128)(2,1)S(1)}, u32[]{:S(2)}, u32[]{:S(2)}) collective-permute-start(bf16[512,256]{1,0:T(8,128)(2,1)} %inputs.1), channel_id=1, source_target_pairs={{0,2},{1,3},{2,4},{3,5},{4,6},{5,7},{6,0},{7,1},{16,18},{17,19},{1... | collective-permute-start | bytes 786440 | tf_op jit(solution)/shard_map/ppermute | solution.py:29
  10.6 1.5 %collective-permute-start.4 = (bf16[512,256]{1,0:T(8,128)(2,1)}, bf16[512,256]{1,0:T(8,128)(2,1)S(1)}, u32[]{:S(2)}, u32[]{:S(2)}) collective-permute-start(bf16[512,256]{1,0:T(8,128)(2,1)} %inputs.1), channel_id=1, source_target_pairs={{0,6},{1,7},{2,0},{3,1},{4,2},{5,3},{6,4},{7,5},{16,22},{17,23},{1... | collective-permute-start | bytes 786440 | tf_op jit(solution)/shard_map/ppermute | solution.py:29
  12.1 1.5 %collective-permute-start.5 = (bf16[512,256]{1,0:T(8,128)(2,1)}, bf16[512,256]{1,0:T(8,128)(2,1)S(1)}, u32[]{:S(2)}, u32[]{:S(2)}) collective-permute-start(bf16[512,256]{1,0:T(8,128)(2,1)} %inputs.1), channel_id=1, source_target_pairs={{0,4},{1,5},{2,6},{3,7},{4,0},{5,1},{6,2},{7,3},{16,20},{17,21},{1... | collective-permute-start | bytes 786440 | tf_op jit(solution)/shard_map/ppermute | solution.py:29
  13.6 0.1 broadcast_add_fusion
  13.7 0.1 add.90
  13.8 0.1 pad_add_fusion.starts
  13.8 5.3 %stage.1 = (bf16[512,256]{1,0:T(8,128)(2,1)S(1)}, bf16[1376,512]{1,0:T(8,128)(2,1)S(1)}, bf16[1376,1536]{1,0:T(8,128)(2,1)S(1)}, bf16[1376,1536]{1,0:T(8,128)(2,1)S(1)}, bf16[1376,512]{1,0:T(8,128)(2,1)S(1)}) custom-call(s32[18]{0:T(128)S(1)} %pad_add_fusion.starts, bf16[512,256]{1,0:T(8,128)(2,1)} %inputs.1, bf16[688,4096]{1,0:T(8,128)(2,1)} %bitcast.20, ...), custom_call_target="tpu_custom_call" | custom-call | tf_op jit(solution)/shard_map/stage/pallas_call | solution.py:117
  19.1 0.0 collective-permute-done.refs_0_
  19.1 0.4 collective-permute-start.11
  19.5 2.4 %collective-permute-start.13 = (bf16[512,256]{1,0:T(8,128)(2,1)S(1)}, bf16[512,256]{1,0:T(8,128)(2,1)S(1)}, u32[]{:S(2)}, u32[]{:S(2)}) collective-permute-start(bf16[512,256]{1,0:T(8,128)(2,1)S(1)} %collective-permute-done.refs_0_), channel_id=1, source_target_pairs={{0,6},{1,7},{2,0},{3,1},{4,2},{5,3},{6,4},{7,5},{16,22},{17,23},{1... | collective-permute-start | bytes 786440 | tf_op jit(solution)/shard_map/ppermute | solution.py:29
  21.9 0.0 collective-permute-done.3.refs_0_
  21.9 0.0 collective-permute-done.4.refs_2_
  21.9 3.1 %collective-permute-done.5.refs_4_ = bf16[512,256]{1,0:T(8,128)(2,1)S(1)} collective-permute-done((bf16[512,256]{1,0:T(8,128)(2,1)}, bf16[512,256]{1,0:T(8,128)(2,1)S(1)}, u32[]{:S(2)}, u32[]{:S(2)}) %collective-permute-start.5) | collective-permute-done | bytes 262176 | tf_op jit(solution)/shard_map/ppermute | solution.py:29
  25.0 2.0 %collective-permute-start.6 = (bf16[512,256]{1,0:T(8,128)(2,1)S(1)}, bf16[512,256]{1,0:T(8,128)(2,1)S(1)}, u32[]{:S(2)}, u32[]{:S(2)}) collective-permute-start(bf16[512,256]{1,0:T(8,128)(2,1)S(1)} %collective-permute-done.3.refs_0_), channel_id=1, source_target_pairs={{0,1},{1,0},{2,3},{3,2},{4,5},{5,4},{6,7},{7,6},{16,17},{17,16},{1... | collective-permute-start | bytes 786440 | tf_op jit(solution)/shard_map/ppermute | solution.py:29
  27.0 0.0 collective-permute-start.7
  27.0 0.5 collective-permute-start.8
  27.5 3.8 %collective-permute-done.11.refs_2_ = bf16[512,256]{1,0:T(8,128)(2,1)S(1)} collective-permute-done((bf16[512,256]{1,0:T(8,128)(2,1)S(1)}, bf16[512,256]{1,0:T(8,128)(2,1)S(1)}, u32[]{:S(2)}, u32[]{:S(2)}) %collective-permute-start.11) | collective-permute-done | bytes 262176 | tf_op jit(solution)/shard_map/ppermute | solution.py:29
  31.3 0.6 collective-permute-start.2
  31.8 0.9 own.1.refs_7_
  32.8 0.0 copy-start
  32.8 0.0 copy-start.2
  32.8 0.8 collective-permute-start.10
  33.6 0.0 collective-permute-done.6.refs_1_
  33.6 0.1 collective-permute-start.12
  33.7 0.0 collective-permute-done.7.refs_3_
  33.7 0.4 collective-permute-start.14
  34.2 0.0 collective-permute-done.8.refs_5_
  34.2 2.4 %near.1.refs_7_ = f32[1376,512]{1,0:T(8,128)S(1)} custom-call(bf16[512,256]{1,0:T(8,128)(2,1)S(1)} %collective-permute-done.3.refs_0_, bf16[512,256]{1,0:T(8,128)(2,1)S(1)} %collective-permute-done.6.refs_1_, bf16[512,256]{1,0:T(8,128)(2,1)S(1)} %collective-permute-done.4.refs_2_, bf16[512,256]{1,0:T(8,128)(2,1)S(1)} %collective-permute-done.7.refs_3_, ...), custom_call_target="tpu_custom_call" | custom-call | flops 2164260864 | tf_op jit(solution)/shard_map/near/pallas_call | solution.py:117
  36.5 3.6 %collective-permute-done.2.first = bf16[512,256]{1,0:T(8,128)(2,1)S(1)} collective-permute-done((bf16[512,256]{1,0:T(8,128)(2,1)S(1)}, bf16[512,256]{1,0:T(8,128)(2,1)S(1)}, u32[]{:S(2)}, u32[]{:S(2)}) %collective-permute-start.2) | collective-permute-done | bytes 262176 | tf_op jit(solution)/shard_map/ppermute | solution.py:29
  40.2 1.3 %collective-permute-start.9 = (bf16[512,256]{1,0:T(8,128)(2,1)S(1)}, bf16[512,256]{1,0:T(8,128)(2,1)S(1)}, u32[]{:S(2)}, u32[]{:S(2)}) collective-permute-start(bf16[512,256]{1,0:T(8,128)(2,1)S(1)} %collective-permute-done.2.first), channel_id=1, source_target_pairs={{0,1},{1,0},{2,3},{3,2},{4,5},{5,4},{6,7},{7,6},{16,17},{17,16},{1... | collective-permute-start | bytes 786440 | tf_op jit(solution)/shard_map/ppermute | solution.py:29
  41.5 0.0 copy-start.1
  41.5 2.4 %middle.1 = (f32[1376,512]{1,0:T(8,128)S(1)}, f32[512,64]{1,0:T(8,128)S(1)}) custom-call(bf16[512,256]{1,0:T(8,128)(2,1)S(1)} %copy-done, bf16[64,256]{1,0:T(8,128)(2,1)S(1)} %bitcast.17, bf16[512,256]{1,0:T(8,128)(2,1)S(1)} %collective-permute-done.refs_0_, bf16[512,256]{1,0:T(8,128)(2,1)S(1)} %collective-permute-done.10.refs_1_, ...), custom_call_target="tpu_custom_call" | custom-call | flops 2164260864 | tf_op jit(solution)/shard_map/middle/pallas_call | solution.py:117
  44.0 1.5 %last.1 = bf16[8,2,32,128]{3,2,1,0:T(8,128)(2,1)S(1)} custom-call(bf16[64,688]{1,0:T(8,128)(2,1)S(1)} %bitcast.16, bf16[512,256]{1,0:T(8,128)(2,1)S(1)} %collective-permute-done.2.first, bf16[512,256]{1,0:T(8,128)(2,1)S(1)} %collective-permute-done.9.second, bf16[1376,512]{1,0:T(8,128)(2,1)S(1)} %get-tuple-element.42.weights, ...), custom_call_target="tpu_custom_call" | custom-call | flops 721420288 | tf_op jit(solution)/shard_map/last/pallas_call | solution.py:117
  45.4 7.7 %all_to_all.15 = bf16[8,2,32,128]{3,2,1,0:T(8,128)(2,1)S(1)} all-to-all(bf16[8,2,32,128]{3,2,1,0:T(8,128)(2,1)S(1)} %last.1), channel_id=1, replica_groups={{0,1,2,3,4,5,6,7},{16,17,18,19,20,21,22,23},{32,33,34,35,36,37,38,39},{..., dimensions={0} | all-to-all | bytes 262144 | tf_op jit(solution)/shard_map/all_to_all | solution.py:204
  53.2 12.7 %all_to_all.16 = bf16[8,2,32,128]{3,2,1,0:T(8,128)(2,1)S(1)} all-to-all(bf16[8,2,32,128]{3,2,1,0:T(8,128)(2,1)S(1)} %broadcast_in_dim.4), channel_id=1, replica_groups={{0,64,128,192,8,72,136,200},{1,65,129,193,9,73,137,201},{2,66,130,194,1..., dimensions={0} | all-to-all | bytes 262144 | tf_op jit(solution)/shard_map/all_to_all | solution.py:208
  65.9 0.7 convolution_multiply_fusion.1
  66.6 0.1 div.45
  66.7 0.1 broadcast_in_dim.5
  66.8 18.6 %all_to_all.17 = bf16[16,8,4096]{2,1,0:T(8,128)(2,1)S(1)} all-to-all(bf16[16,8,4096]{2,1,0:T(8,128)(2,1)S(1)} %broadcast_in_dim.5), channel_id=1, replica_groups={{0,16,32,48,2,18,34,50,4,20,36,52,6,22,38,54},{1,17,33,49,3,19,35,51,5,..., dimensions={0} | all-to-all | bytes 2097152 | tf_op jit(solution)/shard_map/all_to_all | solution.py:215
  85.4 4.2 %collective-permute-start.15 = (bf16[128,4096]{1,0:T(8,128)(2,1)S(1)}, bf16[128,4096]{1,0:T(8,128)(2,1)S(1)}, u32[]{:S(2)}, u32[]{:S(2)}) collective-permute-start(bf16[128,4096]{1,0:T(8,128)(2,1)S(1)} %bitcast.18), channel_id=1, source_target_pairs={{0,1},{1,0},{2,3},{3,2},{4,5},{5,4},{6,7},{7,6},{16,17},{17,16},{1... | collective-permute-start | bytes 3145736 | tf_op jit(solution)/shard_map/ppermute | solution.py:29
  89.6 0.6 constant_dynamic-slice_fusion
  90.2 1.7 %collective-permute-done.15 = bf16[128,4096]{1,0:T(8,128)(2,1)S(1)} collective-permute-done((bf16[128,4096]{1,0:T(8,128)(2,1)S(1)}, bf16[128,4096]{1,0:T(8,128)(2,1)S(1)}, u32[]{:S(2)}, u32[]{:S(2)}) %collective-permute-start.15) | collective-permute-done | bytes 1048608 | tf_op jit(solution)/shard_map/ppermute | solution.py:29
  91.9 2.8 %convolution_multiply_fusion = f32[256,4096]{1,0:T(8,128)} fusion(bf16[128,4096]{1,0:T(8,128)(2,1)S(1)} %collective-permute-done.15, bf16[128,4096]{1,0:T(8,128)(2,1)S(1)} %bitcast.19, s32[]{:T(128)S(6)} %select_n.52), kind=kOutput, calls=%fused_computation | convolution fusion | flops 542375936 | bytes 8388612 | tf_op jit(solution)/shard_map/dot_general | solution.py:218
  (14 shorter events, 0.1 us)
Async XLA Ops:
  0.6 8.8 %collective-permute-start.1 = (bf16[512,256]{1,0:T(8,128)(2,1)}, bf16[512,256]{1,0:T(8,128)(2,1)S(1)}, u32[]{:S(2)}, u32[]{:S(2)}) collective-permute-start(bf16[512,256]{1,0:T(8,128)(2,1)} %inputs.1), channel_id=1, source_target_pairs={{0,1},{1,0},{2,3},{3,2},{4,5},{5,4},{6,7},{7,6},{16,17},{17,16},{1... | collective-permute-start | bytes 786440 | tf_op jit(solution)/shard_map/ppermute | solution.py:29
  4.0 15.2 %collective-permute-start = (bf16[512,256]{1,0:T(8,128)(2,1)}, bf16[512,256]{1,0:T(8,128)(2,1)S(1)}, u32[]{:S(2)}, u32[]{:S(2)}) collective-permute-start(bf16[512,256]{1,0:T(8,128)(2,1)} %inputs.1), channel_id=1, source_target_pairs={{0,8},{1,9},{2,10},{3,11},{4,12},{5,13},{6,14},{7,15},{16,24},{17,... | collective-permute-start | bytes 786440 | tf_op jit(solution)/shard_map/ppermute | solution.py:29
  9.4 12.5 %collective-permute-start.3 = (bf16[512,256]{1,0:T(8,128)(2,1)}, bf16[512,256]{1,0:T(8,128)(2,1)S(1)}, u32[]{:S(2)}, u32[]{:S(2)}) collective-permute-start(bf16[512,256]{1,0:T(8,128)(2,1)} %inputs.1), channel_id=1, source_target_pairs={{0,2},{1,3},{2,4},{3,5},{4,6},{5,7},{6,0},{7,1},{16,18},{17,19},{1... | collective-permute-start | bytes 786440 | tf_op jit(solution)/shard_map/ppermute | solution.py:29
  10.6 11.3 %collective-permute-start.4 = (bf16[512,256]{1,0:T(8,128)(2,1)}, bf16[512,256]{1,0:T(8,128)(2,1)S(1)}, u32[]{:S(2)}, u32[]{:S(2)}) collective-permute-start(bf16[512,256]{1,0:T(8,128)(2,1)} %inputs.1), channel_id=1, source_target_pairs={{0,6},{1,7},{2,0},{3,1},{4,2},{5,3},{6,4},{7,5},{16,22},{17,23},{1... | collective-permute-start | bytes 786440 | tf_op jit(solution)/shard_map/ppermute | solution.py:29
  12.1 12.9 %collective-permute-start.5 = (bf16[512,256]{1,0:T(8,128)(2,1)}, bf16[512,256]{1,0:T(8,128)(2,1)S(1)}, u32[]{:S(2)}, u32[]{:S(2)}) collective-permute-start(bf16[512,256]{1,0:T(8,128)(2,1)} %inputs.1), channel_id=1, source_target_pairs={{0,4},{1,5},{2,6},{3,7},{4,0},{5,1},{6,2},{7,3},{16,20},{17,21},{1... | collective-permute-start | bytes 786440 | tf_op jit(solution)/shard_map/ppermute | solution.py:29
  19.1 12.1 %collective-permute-start.11 = (bf16[512,256]{1,0:T(8,128)(2,1)S(1)}, bf16[512,256]{1,0:T(8,128)(2,1)S(1)}, u32[]{:S(2)}, u32[]{:S(2)}) collective-permute-start(bf16[512,256]{1,0:T(8,128)(2,1)S(1)} %collective-permute-done.refs_0_), channel_id=1, source_target_pairs={{0,2},{1,3},{2,4},{3,5},{4,6},{5,7},{6,0},{7,1},{16,18},{17,19},{1... | collective-permute-start | bytes 786440 | tf_op jit(solution)/shard_map/ppermute | solution.py:29
  19.5 13.3 %collective-permute-start.13 = (bf16[512,256]{1,0:T(8,128)(2,1)S(1)}, bf16[512,256]{1,0:T(8,128)(2,1)S(1)}, u32[]{:S(2)}, u32[]{:S(2)}) collective-permute-start(bf16[512,256]{1,0:T(8,128)(2,1)S(1)} %collective-permute-done.refs_0_), channel_id=1, source_target_pairs={{0,6},{1,7},{2,0},{3,1},{4,2},{5,3},{6,4},{7,5},{16,22},{17,23},{1... | collective-permute-start | bytes 786440 | tf_op jit(solution)/shard_map/ppermute | solution.py:29
  25.0 8.7 %collective-permute-start.6 = (bf16[512,256]{1,0:T(8,128)(2,1)S(1)}, bf16[512,256]{1,0:T(8,128)(2,1)S(1)}, u32[]{:S(2)}, u32[]{:S(2)}) collective-permute-start(bf16[512,256]{1,0:T(8,128)(2,1)S(1)} %collective-permute-done.3.refs_0_), channel_id=1, source_target_pairs={{0,1},{1,0},{2,3},{3,2},{4,5},{5,4},{6,7},{7,6},{16,17},{17,16},{1... | collective-permute-start | bytes 786440 | tf_op jit(solution)/shard_map/ppermute | solution.py:29
  27.0 6.8 %collective-permute-start.7 = (bf16[512,256]{1,0:T(8,128)(2,1)S(1)}, bf16[512,256]{1,0:T(8,128)(2,1)S(1)}, u32[]{:S(2)}, u32[]{:S(2)}) collective-permute-start(bf16[512,256]{1,0:T(8,128)(2,1)S(1)} %collective-permute-done.4.refs_2_), channel_id=1, source_target_pairs={{0,1},{1,0},{2,3},{3,2},{4,5},{5,4},{6,7},{7,6},{16,17},{17,16},{1... | collective-permute-start | bytes 786440 | tf_op jit(solution)/shard_map/ppermute | solution.py:29
  27.0 7.2 %collective-permute-start.8 = (bf16[512,256]{1,0:T(8,128)(2,1)S(1)}, bf16[512,256]{1,0:T(8,128)(2,1)S(1)}, u32[]{:S(2)}, u32[]{:S(2)}) collective-permute-start(bf16[512,256]{1,0:T(8,128)(2,1)S(1)} %collective-permute-done.5.refs_4_), channel_id=1, source_target_pairs={{0,1},{1,0},{2,3},{3,2},{4,5},{5,4},{6,7},{7,6},{16,17},{17,16},{1... | collective-permute-start | bytes 786440 | tf_op jit(solution)/shard_map/ppermute | solution.py:29
  31.3 8.9 %collective-permute-start.2 = (bf16[512,256]{1,0:T(8,128)(2,1)S(1)}, bf16[512,256]{1,0:T(8,128)(2,1)S(1)}, u32[]{:S(2)}, u32[]{:S(2)}) collective-permute-start(bf16[512,256]{1,0:T(8,128)(2,1)S(1)} %collective-permute-done.refs_0_), channel_id=1, source_target_pairs={{0,4},{1,5},{2,6},{3,7},{4,0},{5,1},{6,2},{7,3},{16,20},{17,21},{1... | collective-permute-start | bytes 786440 | tf_op jit(solution)/shard_map/ppermute | solution.py:29
  32.8 8.7 %copy-start = (bf16[512,256]{1,0:T(8,128)(2,1)S(1)}, bf16[512,256]{1,0:T(8,128)(2,1)}, u32[]{:S(2)}) copy-start(bf16[512,256]{1,0:T(8,128)(2,1)} %grads.1) | copy-start | bytes 786436
  32.8 8.7 %copy-start.2 = (bf16[256,64]{0,1:T(8,128)(2,1)S(1)}, bf16[256,64]{0,1:T(8,128)(2,1)}, u32[]{:S(2)}) copy-start(bf16[256,64]{0,1:T(8,128)(2,1)} %param.11) | copy-start | bytes 98308
  32.8 8.7 %collective-permute-start.10 = (bf16[512,256]{1,0:T(8,128)(2,1)S(1)}, bf16[512,256]{1,0:T(8,128)(2,1)S(1)}, u32[]{:S(2)}, u32[]{:S(2)}) collective-permute-start(bf16[512,256]{1,0:T(8,128)(2,1)S(1)} %collective-permute-done.refs_0_), channel_id=1, source_target_pairs={{0,1},{1,0},{2,3},{3,2},{4,5},{5,4},{6,7},{7,6},{16,17},{17,16},{1... | collective-permute-start | bytes 786440 | tf_op jit(solution)/shard_map/ppermute | solution.py:29
  33.6 7.9 %collective-permute-start.12 = (bf16[512,256]{1,0:T(8,128)(2,1)S(1)}, bf16[512,256]{1,0:T(8,128)(2,1)S(1)}, u32[]{:S(2)}, u32[]{:S(2)}) collective-permute-start(bf16[512,256]{1,0:T(8,128)(2,1)S(1)} %collective-permute-done.11.refs_2_), channel_id=1, source_target_pairs={{0,1},{1,0},{2,3},{3,2},{4,5},{5,4},{6,7},{7,6},{16,17},{17,16},{1... | collective-permute-start | bytes 786440 | tf_op jit(solution)/shard_map/ppermute | solution.py:29
  33.7 7.8 %collective-permute-start.14 = (bf16[512,256]{1,0:T(8,128)(2,1)S(1)}, bf16[512,256]{1,0:T(8,128)(2,1)S(1)}, u32[]{:S(2)}, u32[]{:S(2)}) collective-permute-start(bf16[512,256]{1,0:T(8,128)(2,1)S(1)} %collective-permute-done.13.refs_4_), channel_id=1, source_target_pairs={{0,1},{1,0},{2,3},{3,2},{4,5},{5,4},{6,7},{7,6},{16,17},{17,16},{1... | collective-permute-start | bytes 786440 | tf_op jit(solution)/shard_map/ppermute | solution.py:29
  40.2 3.8 %collective-permute-start.9 = (bf16[512,256]{1,0:T(8,128)(2,1)S(1)}, bf16[512,256]{1,0:T(8,128)(2,1)S(1)}, u32[]{:S(2)}, u32[]{:S(2)}) collective-permute-start(bf16[512,256]{1,0:T(8,128)(2,1)S(1)} %collective-permute-done.2.first), channel_id=1, source_target_pairs={{0,1},{1,0},{2,3},{3,2},{4,5},{5,4},{6,7},{7,6},{16,17},{17,16},{1... | collective-permute-start | bytes 786440 | tf_op jit(solution)/shard_map/ppermute | solution.py:29
  41.5 2.4 %copy-start.1 = (bf16[688,64]{0,1:T(8,128)(2,1)S(1)}, bf16[688,64]{0,1:T(8,128)(2,1)}, u32[]{:S(2)}) copy-start(bf16[688,64]{0,1:T(8,128)(2,1)} %param.10) | copy-start | bytes 264196
  85.4 6.5 %collective-permute-start.15 = (bf16[128,4096]{1,0:T(8,128)(2,1)S(1)}, bf16[128,4096]{1,0:T(8,128)(2,1)S(1)}, u32[]{:S(2)}, u32[]{:S(2)}) collective-permute-start(bf16[128,4096]{1,0:T(8,128)(2,1)S(1)} %bitcast.18), channel_id=1, source_target_pairs={{0,1},{1,0},{2,3},{3,2},{4,5},{5,4},{6,7},{7,6},{16,17},{17,16},{1... | collective-permute-start | bytes 3145736 | tf_op jit(solution)/shard_map/ppermute | solution.py:29

commit v5 on v4

--- a/solution.py
+++ b/solution.py
@@ -45,8 +45,9 @@
 ROWS_TIMES_ROWS = (((1,), (1,)), ((), ()))
 LINES = [[(z % 4 * 4 + y) * 16 + z // 4 * 8 + n for z in range(8)] for y in range(4) for n in range(8)]
 SQUARES = [[(z % 4 * 4 + y) * 16 + z // 4 * 8 + n for n in range(8)] for z in range(8) for y in range(4)]
+SPIRAL = [(x, (x + y) % 4) for y in range(4) for x in range(4)]
 PLANES = [
-    [(z % 4 * 4 + y) * 16 + z // 4 * 8 + x * 2 + c for x in range(4) for y in range(4)]
+    [(z % 4 * 4 + y) * 16 + z // 4 * 8 + x * 2 + c for x, y in SPIRAL]
     for z in range(8)
     for c in range(2)
 ]

time: 94.9 us -> 94.2 us (level)
  no operation moved by 1% of the time
where the time goes in v5:
time: 94.2 us; the launch traced here: 94 us
  blocking collectives  38.6 us (41%)
  starting transfers between devices  25.2 us (27%)
  Pallas kernels  12.5 us (13%)
  waiting for transfers between devices  12.2 us (13%)
  matrix products  3.45 us (4%)
  local copies, waits for them, and re-layouts  0.95 us (1%)
    ppermute x16, starting transfers between devices, send(): return lax.ppermute(value, BOTH, pairs(move))  25.2 us
    all_to_all x1, blocking collectives, on_device(): lax.all_to_all(feats, BOTH, 0, 0, axis_index_groups=PLANES)  18.2 us
    all_to_all x1, blocking collectives, on_device(): lax.all_to_all(part, BOTH, 0, 0, axis_index_groups=LINES)  12.7 us
    pallas_call x5, Pallas kernels, call(): pl.pallas_call(kernel, out_shape=[VMEM(shape, dtype) for shape, dtype in...  12.5 us
    ppermute x16, waiting for transfers between devices, send(): return lax.ppermute(value, BOTH, pairs(move))  12.2 us
    all_to_all x1, blocking collectives, on_device(): shares = lax.all_to_all(shares, BOTH, 0, 0, axis_index_groups=SQUARES)  7.67 us
    dot_general x1, matrix products, on_device(): jnp.dot(mine.T, feats, preferred_element_type=jnp.float32) * (1.0 / 256)  2.77 us
  transfers between devices with their start and end apart: 16, of which 4 were waited for; matrix products, arithmetic and copies ran while one was open for 1% of the time, Pallas kernels for 12%

profile of v5, /device:TPU:1, one launch (start us, length us, event | category | flops | bytes accessed | tf_op | source)
XLA Modules:
  0.0 94.0 jit_solution(6101635862796793881)
XLA Ops:
  0.6 3.3 %collective-permute-start.1 = (bf16[512,256]{1,0:T(8,128)(2,1)}, bf16[512,256]{1,0:T(8,128)(2,1)S(1)}, u32[]{:S(2)}, u32[]{:S(2)}) collective-permute-start(bf16[512,256]{1,0:T(8,128)(2,1)} %inputs.1), channel_id=1, source_target_pairs={{0,1},{1,0},{2,3},{3,2},{4,5},{5,4},{6,7},{7,6},{16,17},{17,16},{1... | collective-permute-start | bytes 786440 | tf_op jit(solution)/shard_map/ppermute | solution.py:29
  4.0 5.2 %collective-permute-start = (bf16[512,256]{1,0:T(8,128)(2,1)}, bf16[512,256]{1,0:T(8,128)(2,1)S(1)}, u32[]{:S(2)}, u32[]{:S(2)}) collective-permute-start(bf16[512,256]{1,0:T(8,128)(2,1)} %inputs.1), channel_id=1, source_target_pairs={{0,8},{1,9},{2,10},{3,11},{4,12},{5,13},{6,14},{7,15},{16,24},{17,... | collective-permute-start | bytes 786440 | tf_op jit(solution)/shard_map/ppermute | solution.py:29
  9.2 0.1 add_multiply_fusion
  9.2 0.1 add_multiply_fusion.1
  9.3 0.1 broadcast_add_fusion.1
  9.4 0.0 collective-permute-done.1.second
  9.4 1.2 %collective-permute-start.3 = (bf16[512,256]{1,0:T(8,128)(2,1)}, bf16[512,256]{1,0:T(8,128)(2,1)S(1)}, u32[]{:S(2)}, u32[]{:S(2)}) collective-permute-start(bf16[512,256]{1,0:T(8,128)(2,1)} %inputs.1), channel_id=1, source_target_pairs={{0,2},{1,3},{2,4},{3,5},{4,6},{5,7},{6,0},{7,1},{16,18},{17,19},{1... | collective-permute-start | bytes 786440 | tf_op jit(solution)/shard_map/ppermute | solution.py:29
  10.6 1.5 %collective-permute-start.4 = (bf16[512,256]{1,0:T(8,128)(2,1)}, bf16[512,256]{1,0:T(8,128)(2,1)S(1)}, u32[]{:S(2)}, u32[]{:S(2)}) collective-permute-start(bf16[512,256]{1,0:T(8,128)(2,1)} %inputs.1), channel_id=1, source_target_pairs={{0,6},{1,7},{2,0},{3,1},{4,2},{5,3},{6,4},{7,5},{16,22},{17,23},{1... | collective-permute-start | bytes 786440 | tf_op jit(solution)/shard_map/ppermute | solution.py:29
  12.1 1.5 %collective-permute-start.5 = (bf16[512,256]{1,0:T(8,128)(2,1)}, bf16[512,256]{1,0:T(8,128)(2,1)S(1)}, u32[]{:S(2)}, u32[]{:S(2)}) collective-permute-start(bf16[512,256]{1,0:T(8,128)(2,1)} %inputs.1), channel_id=1, source_target_pairs={{0,4},{1,5},{2,6},{3,7},{4,0},{5,1},{6,2},{7,3},{16,20},{17,21},{1... | collective-permute-start | bytes 786440 | tf_op jit(solution)/shard_map/ppermute | solution.py:29
  13.6 0.1 broadcast_add_fusion
  13.7 0.1 add.90
  13.8 0.1 pad_add_fusion.starts
  13.8 5.3 %stage.1 = (bf16[512,256]{1,0:T(8,128)(2,1)S(1)}, bf16[1376,512]{1,0:T(8,128)(2,1)S(1)}, bf16[1376,1536]{1,0:T(8,128)(2,1)S(1)}, bf16[1376,1536]{1,0:T(8,128)(2,1)S(1)}, bf16[1376,512]{1,0:T(8,128)(2,1)S(1)}) custom-call(s32[18]{0:T(128)S(1)} %pad_add_fusion.starts, bf16[512,256]{1,0:T(8,128)(2,1)} %inputs.1, bf16[688,4096]{1,0:T(8,128)(2,1)} %bitcast.20, ...), custom_call_target="tpu_custom_call" | custom-call | tf_op jit(solution)/shard_map/stage/pallas_call | solution.py:118
  19.1 0.4 collective-permute-start.11
  19.5 2.4 %collective-permute-start.13 = (bf16[512,256]{1,0:T(8,128)(2,1)S(1)}, bf16[512,256]{1,0:T(8,128)(2,1)S(1)}, u32[]{:S(2)}, u32[]{:S(2)}) collective-permute-start(bf16[512,256]{1,0:T(8,128)(2,1)S(1)} %collective-permute-done.refs_0_), channel_id=1, source_target_pairs={{0,6},{1,7},{2,0},{3,1},{4,2},{5,3},{6,4},{7,5},{16,22},{17,23},{1... | collective-permute-start | bytes 786440 | tf_op jit(solution)/shard_map/ppermute | solution.py:29
  21.9 3.1 %collective-permute-done.5.refs_4_ = bf16[512,256]{1,0:T(8,128)(2,1)S(1)} collective-permute-done((bf16[512,256]{1,0:T(8,128)(2,1)}, bf16[512,256]{1,0:T(8,128)(2,1)S(1)}, u32[]{:S(2)}, u32[]{:S(2)}) %collective-permute-start.5) | collective-permute-done | bytes 262176 | tf_op jit(solution)/shard_map/ppermute | solution.py:29
  25.0 2.0 %collective-permute-start.6 = (bf16[512,256]{1,0:T(8,128)(2,1)S(1)}, bf16[512,256]{1,0:T(8,128)(2,1)S(1)}, u32[]{:S(2)}, u32[]{:S(2)}) collective-permute-start(bf16[512,256]{1,0:T(8,128)(2,1)S(1)} %collective-permute-done.3.refs_0_), channel_id=1, source_target_pairs={{0,1},{1,0},{2,3},{3,2},{4,5},{5,4},{6,7},{7,6},{16,17},{17,16},{1... | collective-permute-start | bytes 786440 | tf_op jit(solution)/shard_map/ppermute | solution.py:29
  27.0 0.0 collective-permute-start.7
  27.0 0.5 collective-permute-start.8
  27.5 3.8 %collective-permute-done.11.refs_2_ = bf16[512,256]{1,0:T(8,128)(2,1)S(1)} collective-permute-done((bf16[512,256]{1,0:T(8,128)(2,1)S(1)}, bf16[512,256]{1,0:T(8,128)(2,1)S(1)}, u32[]{:S(2)}, u32[]{:S(2)}) %collective-permute-start.11) | collective-permute-done | bytes 262176 | tf_op jit(solution)/shard_map/ppermute | solution.py:29
  31.3 0.6 collective-permute-start.2
  31.8 0.9 own.1.refs_7_
  32.8 0.0 copy-start
  32.8 0.0 copy-start.2
  32.8 0.0 collective-permute-done.13.refs_4_
  32.8 0.8 collective-permute-start.10
  33.6 0.1 collective-permute-start.12
  33.7 0.0 collective-permute-done.7.refs_3_
  33.7 0.4 collective-permute-start.14
  34.2 2.4 %near.1.refs_7_ = f32[1376,512]{1,0:T(8,128)S(1)} custom-call(bf16[512,256]{1,0:T(8,128)(2,1)S(1)} %collective-permute-done.3.refs_0_, bf16[512,256]{1,0:T(8,128)(2,1)S(1)} %collective-permute-done.6.refs_1_, bf16[512,256]{1,0:T(8,128)(2,1)S(1)} %collective-permute-done.4.refs_2_, bf16[512,256]{1,0:T(8,128)(2,1)S(1)} %collective-permute-done.7.refs_3_, ...), custom_call_target="tpu_custom_call" | custom-call | flops 2164260864 | tf_op jit(solution)/shard_map/near/pallas_call | solution.py:118
  36.5 3.6 %collective-permute-done.2.first = bf16[512,256]{1,0:T(8,128)(2,1)S(1)} collective-permute-done((bf16[512,256]{1,0:T(8,128)(2,1)S(1)}, bf16[512,256]{1,0:T(8,128)(2,1)S(1)}, u32[]{:S(2)}, u32[]{:S(2)}) %collective-permute-start.2) | collective-permute-done | bytes 262176 | tf_op jit(solution)/shard_map/ppermute | solution.py:29
  40.2 1.3 %collective-permute-start.9 = (bf16[512,256]{1,0:T(8,128)(2,1)S(1)}, bf16[512,256]{1,0:T(8,128)(2,1)S(1)}, u32[]{:S(2)}, u32[]{:S(2)}) collective-permute-start(bf16[512,256]{1,0:T(8,128)(2,1)S(1)} %collective-permute-done.2.first), channel_id=1, source_target_pairs={{0,1},{1,0},{2,3},{3,2},{4,5},{5,4},{6,7},{7,6},{16,17},{17,16},{1... | collective-permute-start | bytes 786440 | tf_op jit(solution)/shard_map/ppermute | solution.py:29
  41.5 0.0 collective-permute-done.10.refs_1_
  41.5 0.0 collective-permute-done.12.refs_3_
  41.5 0.0 copy-start.1
  41.5 2.4 %middle.1 = (f32[1376,512]{1,0:T(8,128)S(1)}, f32[512,64]{1,0:T(8,128)S(1)}) custom-call(bf16[512,256]{1,0:T(8,128)(2,1)S(1)} %copy-done, bf16[64,256]{1,0:T(8,128)(2,1)S(1)} %bitcast.17, bf16[512,256]{1,0:T(8,128)(2,1)S(1)} %collective-permute-done.refs_0_, bf16[512,256]{1,0:T(8,128)(2,1)S(1)} %collective-permute-done.10.refs_1_, ...), custom_call_target="tpu_custom_call" | custom-call | flops 2164260864 | tf_op jit(solution)/shard_map/middle/pallas_call | solution.py:118
  43.9 0.0 collective-permute-done.9.second
  44.0 1.5 %last.1 = bf16[8,2,32,128]{3,2,1,0:T(8,128)(2,1)S(1)} custom-call(bf16[64,688]{1,0:T(8,128)(2,1)S(1)} %bitcast.16, bf16[512,256]{1,0:T(8,128)(2,1)S(1)} %collective-permute-done.2.first, bf16[512,256]{1,0:T(8,128)(2,1)S(1)} %collective-permute-done.9.second, bf16[1376,512]{1,0:T(8,128)(2,1)S(1)} %get-tuple-element.42.weights, ...), custom_call_target="tpu_custom_call" | custom-call | flops 721420288 | tf_op jit(solution)/shard_map/last/pallas_call | solution.py:118
  45.4 7.7 %all_to_all.15 = bf16[8,2,32,128]{3,2,1,0:T(8,128)(2,1)S(1)} all-to-all(bf16[8,2,32,128]{3,2,1,0:T(8,128)(2,1)S(1)} %last.1), channel_id=1, replica_groups={{0,1,2,3,4,5,6,7},{16,17,18,19,20,21,22,23},{32,33,34,35,36,37,38,39},{..., dimensions={0} | all-to-all | bytes 262144 | tf_op jit(solution)/shard_map/all_to_all | solution.py:205
  53.2 12.7 %all_to_all.16 = bf16[8,2,32,128]{3,2,1,0:T(8,128)(2,1)S(1)} all-to-all(bf16[8,2,32,128]{3,2,1,0:T(8,128)(2,1)S(1)} %broadcast_in_dim.4), channel_id=1, replica_groups={{0,64,128,192,8,72,136,200},{1,65,129,193,9,73,137,201},{2,66,130,194,1..., dimensions={0} | all-to-all | bytes 262144 | tf_op jit(solution)/shard_map/all_to_all | solution.py:209
  65.9 0.7 convolution_multiply_fusion.1
  66.6 0.1 div.45
  66.7 0.1 broadcast_in_dim.5
  66.8 18.2 %all_to_all.17 = bf16[16,8,4096]{2,1,0:T(8,128)(2,1)S(1)} all-to-all(bf16[16,8,4096]{2,1,0:T(8,128)(2,1)S(1)} %broadcast_in_dim.5), channel_id=1, replica_groups={{0,18,36,54,16,34,52,6,32,50,4,22,48,2,20,38},{1,19,37,55,17,35,53,7,33..., dimensions={0} | all-to-all | bytes 2097152 | tf_op jit(solution)/shard_map/all_to_all | solution.py:216
  85.1 3.9 %collective-permute-start.15 = (bf16[128,4096]{1,0:T(8,128)(2,1)S(1)}, bf16[128,4096]{1,0:T(8,128)(2,1)S(1)}, u32[]{:S(2)}, u32[]{:S(2)}) collective-permute-start(bf16[128,4096]{1,0:T(8,128)(2,1)S(1)} %bitcast.18), channel_id=1, source_target_pairs={{0,1},{1,0},{2,3},{3,2},{4,5},{5,4},{6,7},{7,6},{16,17},{17,16},{1... | collective-permute-start | bytes 3145736 | tf_op jit(solution)/shard_map/ppermute | solution.py:29
  89.0 0.6 constant_dynamic-slice_fusion
  89.6 1.7 %collective-permute-done.15 = bf16[128,4096]{1,0:T(8,128)(2,1)S(1)} collective-permute-done((bf16[128,4096]{1,0:T(8,128)(2,1)S(1)}, bf16[128,4096]{1,0:T(8,128)(2,1)S(1)}, u32[]{:S(2)}, u32[]{:S(2)}) %collective-permute-start.15) | collective-permute-done | bytes 1048608 | tf_op jit(solution)/shard_map/ppermute | solution.py:29
  91.2 2.8 %convolution_multiply_fusion = f32[256,4096]{1,0:T(8,128)} fusion(bf16[128,4096]{1,0:T(8,128)(2,1)S(1)} %collective-permute-done.15, bf16[128,4096]{1,0:T(8,128)(2,1)S(1)} %bitcast.19, s32[]{:T(128)S(6)} %select_n.52), kind=kOutput, calls=%fused_computation | convolution fusion | flops 542375936 | bytes 8388612 | tf_op jit(solution)/shard_map/dot_general | solution.py:219
  (14 shorter events, 0.1 us)
Async XLA Ops:
  0.6 8.8 %collective-permute-start.1 = (bf16[512,256]{1,0:T(8,128)(2,1)}, bf16[512,256]{1,0:T(8,128)(2,1)S(1)}, u32[]{:S(2)}, u32[]{:S(2)}) collective-permute-start(bf16[512,256]{1,0:T(8,128)(2,1)} %inputs.1), channel_id=1, source_target_pairs={{0,1},{1,0},{2,3},{3,2},{4,5},{5,4},{6,7},{7,6},{16,17},{17,16},{1... | collective-permute-start | bytes 786440 | tf_op jit(solution)/shard_map/ppermute | solution.py:29
  4.0 15.2 %collective-permute-start = (bf16[512,256]{1,0:T(8,128)(2,1)}, bf16[512,256]{1,0:T(8,128)(2,1)S(1)}, u32[]{:S(2)}, u32[]{:S(2)}) collective-permute-start(bf16[512,256]{1,0:T(8,128)(2,1)} %inputs.1), channel_id=1, source_target_pairs={{0,8},{1,9},{2,10},{3,11},{4,12},{5,13},{6,14},{7,15},{16,24},{17,... | collective-permute-start | bytes 786440 | tf_op jit(solution)/shard_map/ppermute | solution.py:29
  9.4 12.5 %collective-permute-start.3 = (bf16[512,256]{1,0:T(8,128)(2,1)}, bf16[512,256]{1,0:T(8,128)(2,1)S(1)}, u32[]{:S(2)}, u32[]{:S(2)}) collective-permute-start(bf16[512,256]{1,0:T(8,128)(2,1)} %inputs.1), channel_id=1, source_target_pairs={{0,2},{1,3},{2,4},{3,5},{4,6},{5,7},{6,0},{7,1},{16,18},{17,19},{1... | collective-permute-start | bytes 786440 | tf_op jit(solution)/shard_map/ppermute | solution.py:29
  10.6 11.3 %collective-permute-start.4 = (bf16[512,256]{1,0:T(8,128)(2,1)}, bf16[512,256]{1,0:T(8,128)(2,1)S(1)}, u32[]{:S(2)}, u32[]{:S(2)}) collective-permute-start(bf16[512,256]{1,0:T(8,128)(2,1)} %inputs.1), channel_id=1, source_target_pairs={{0,6},{1,7},{2,0},{3,1},{4,2},{5,3},{6,4},{7,5},{16,22},{17,23},{1... | collective-permute-start | bytes 786440 | tf_op jit(solution)/shard_map/ppermute | solution.py:29
  12.1 12.9 %collective-permute-start.5 = (bf16[512,256]{1,0:T(8,128)(2,1)}, bf16[512,256]{1,0:T(8,128)(2,1)S(1)}, u32[]{:S(2)}, u32[]{:S(2)}) collective-permute-start(bf16[512,256]{1,0:T(8,128)(2,1)} %inputs.1), channel_id=1, source_target_pairs={{0,4},{1,5},{2,6},{3,7},{4,0},{5,1},{6,2},{7,3},{16,20},{17,21},{1... | collective-permute-start | bytes 786440 | tf_op jit(solution)/shard_map/ppermute | solution.py:29
  19.1 12.1 %collective-permute-start.11 = (bf16[512,256]{1,0:T(8,128)(2,1)S(1)}, bf16[512,256]{1,0:T(8,128)(2,1)S(1)}, u32[]{:S(2)}, u32[]{:S(2)}) collective-permute-start(bf16[512,256]{1,0:T(8,128)(2,1)S(1)} %collective-permute-done.refs_0_), channel_id=1, source_target_pairs={{0,2},{1,3},{2,4},{3,5},{4,6},{5,7},{6,0},{7,1},{16,18},{17,19},{1... | collective-permute-start | bytes 786440 | tf_op jit(solution)/shard_map/ppermute | solution.py:29
  19.5 13.3 %collective-permute-start.13 = (bf16[512,256]{1,0:T(8,128)(2,1)S(1)}, bf16[512,256]{1,0:T(8,128)(2,1)S(1)}, u32[]{:S(2)}, u32[]{:S(2)}) collective-permute-start(bf16[512,256]{1,0:T(8,128)(2,1)S(1)} %collective-permute-done.refs_0_), channel_id=1, source_target_pairs={{0,6},{1,7},{2,0},{3,1},{4,2},{5,3},{6,4},{7,5},{16,22},{17,23},{1... | collective-permute-start | bytes 786440 | tf_op jit(solution)/shard_map/ppermute | solution.py:29
  25.0 8.7 %collective-permute-start.6 = (bf16[512,256]{1,0:T(8,128)(2,1)S(1)}, bf16[512,256]{1,0:T(8,128)(2,1)S(1)}, u32[]{:S(2)}, u32[]{:S(2)}) collective-permute-start(bf16[512,256]{1,0:T(8,128)(2,1)S(1)} %collective-permute-done.3.refs_0_), channel_id=1, source_target_pairs={{0,1},{1,0},{2,3},{3,2},{4,5},{5,4},{6,7},{7,6},{16,17},{17,16},{1... | collective-permute-start | bytes 786440 | tf_op jit(solution)/shard_map/ppermute | solution.py:29
  27.0 6.8 %collective-permute-start.7 = (bf16[512,256]{1,0:T(8,128)(2,1)S(1)}, bf16[512,256]{1,0:T(8,128)(2,1)S(1)}, u32[]{:S(2)}, u32[]{:S(2)}) collective-permute-start(bf16[512,256]{1,0:T(8,128)(2,1)S(1)} %collective-permute-done.4.refs_2_), channel_id=1, source_target_pairs={{0,1},{1,0},{2,3},{3,2},{4,5},{5,4},{6,7},{7,6},{16,17},{17,16},{1... | collective-permute-start | bytes 786440 | tf_op jit(solution)/shard_map/ppermute | solution.py:29
  27.0 7.2 %collective-permute-start.8 = (bf16[512,256]{1,0:T(8,128)(2,1)S(1)}, bf16[512,256]{1,0:T(8,128)(2,1)S(1)}, u32[]{:S(2)}, u32[]{:S(2)}) collective-permute-start(bf16[512,256]{1,0:T(8,128)(2,1)S(1)} %collective-permute-done.5.refs_4_), channel_id=1, source_target_pairs={{0,1},{1,0},{2,3},{3,2},{4,5},{5,4},{6,7},{7,6},{16,17},{17,16},{1... | collective-permute-start | bytes 786440 | tf_op jit(solution)/shard_map/ppermute | solution.py:29
  31.3 8.9 %collective-permute-start.2 = (bf16[512,256]{1,0:T(8,128)(2,1)S(1)}, bf16[512,256]{1,0:T(8,128)(2,1)S(1)}, u32[]{:S(2)}, u32[]{:S(2)}) collective-permute-start(bf16[512,256]{1,0:T(8,128)(2,1)S(1)} %collective-permute-done.refs_0_), channel_id=1, source_target_pairs={{0,4},{1,5},{2,6},{3,7},{4,0},{5,1},{6,2},{7,3},{16,20},{17,21},{1... | collective-permute-start | bytes 786440 | tf_op jit(solution)/shard_map/ppermute | solution.py:29
  32.8 8.7 %copy-start = (bf16[512,256]{1,0:T(8,128)(2,1)S(1)}, bf16[512,256]{1,0:T(8,128)(2,1)}, u32[]{:S(2)}) copy-start(bf16[512,256]{1,0:T(8,128)(2,1)} %grads.1) | copy-start | bytes 786436
  32.8 8.7 %copy-start.2 = (bf16[256,64]{0,1:T(8,128)(2,1)S(1)}, bf16[256,64]{0,1:T(8,128)(2,1)}, u32[]{:S(2)}) copy-start(bf16[256,64]{0,1:T(8,128)(2,1)} %param.11) | copy-start | bytes 98308
  32.8 8.7 %collective-permute-start.10 = (bf16[512,256]{1,0:T(8,128)(2,1)S(1)}, bf16[512,256]{1,0:T(8,128)(2,1)S(1)}, u32[]{:S(2)}, u32[]{:S(2)}) collective-permute-start(bf16[512,256]{1,0:T(8,128)(2,1)S(1)} %collective-permute-done.refs_0_), channel_id=1, source_target_pairs={{0,1},{1,0},{2,3},{3,2},{4,5},{5,4},{6,7},{7,6},{16,17},{17,16},{1... | collective-permute-start | bytes 786440 | tf_op jit(solution)/shard_map/ppermute | solution.py:29
  33.6 7.9 %collective-permute-start.12 = (bf16[512,256]{1,0:T(8,128)(2,1)S(1)}, bf16[512,256]{1,0:T(8,128)(2,1)S(1)}, u32[]{:S(2)}, u32[]{:S(2)}) collective-permute-start(bf16[512,256]{1,0:T(8,128)(2,1)S(1)} %collective-permute-done.11.refs_2_), channel_id=1, source_target_pairs={{0,1},{1,0},{2,3},{3,2},{4,5},{5,4},{6,7},{7,6},{16,17},{17,16},{1... | collective-permute-start | bytes 786440 | tf_op jit(solution)/shard_map/ppermute | solution.py:29
  33.7 7.8 %collective-permute-start.14 = (bf16[512,256]{1,0:T(8,128)(2,1)S(1)}, bf16[512,256]{1,0:T(8,128)(2,1)S(1)}, u32[]{:S(2)}, u32[]{:S(2)}) collective-permute-start(bf16[512,256]{1,0:T(8,128)(2,1)S(1)} %collective-permute-done.13.refs_4_), channel_id=1, source_target_pairs={{0,1},{1,0},{2,3},{3,2},{4,5},{5,4},{6,7},{7,6},{16,17},{17,16},{1... | collective-permute-start | bytes 786440 | tf_op jit(solution)/shard_map/ppermute | solution.py:29
  40.2 3.8 %collective-permute-start.9 = (bf16[512,256]{1,0:T(8,128)(2,1)S(1)}, bf16[512,256]{1,0:T(8,128)(2,1)S(1)}, u32[]{:S(2)}, u32[]{:S(2)}) collective-permute-start(bf16[512,256]{1,0:T(8,128)(2,1)S(1)} %collective-permute-done.2.first), channel_id=1, source_target_pairs={{0,1},{1,0},{2,3},{3,2},{4,5},{5,4},{6,7},{7,6},{16,17},{17,16},{1... | collective-permute-start | bytes 786440 | tf_op jit(solution)/shard_map/ppermute | solution.py:29
  41.5 2.4 %copy-start.1 = (bf16[688,64]{0,1:T(8,128)(2,1)S(1)}, bf16[688,64]{0,1:T(8,128)(2,1)}, u32[]{:S(2)}) copy-start(bf16[688,64]{0,1:T(8,128)(2,1)} %param.10) | copy-start | bytes 264196
  85.1 6.2 %collective-permute-start.15 = (bf16[128,4096]{1,0:T(8,128)(2,1)S(1)}, bf16[128,4096]{1,0:T(8,128)(2,1)S(1)}, u32[]{:S(2)}, u32[]{:S(2)}) collective-permute-start(bf16[128,4096]{1,0:T(8,128)(2,1)S(1)} %bitcast.18), channel_id=1, source_target_pairs={{0,1},{1,0},{2,3},{3,2},{4,5},{5,4},{6,7},{7,6},{16,17},{17,16},{1... | collective-permute-start | bytes 3145736 | tf_op jit(solution)/shard_map/ppermute | solution.py:29

commit v6 on v5

--- a/solution.py
+++ b/solution.py
@@ -208,7 +208,7 @@
     part = jnp.broadcast_to(part.astype(jnp.bfloat16), (8, *part.shape))
     along = lax.all_to_all(part, BOTH, 0, 0, axis_index_groups=LINES).astype(jnp.float32)
     total = (along[:4] + along[4:]).reshape(8, SEQ, 128)
-    outer = jnp.einsum("eta,etb->eab", total[..., :64], total[..., 64:], precision=lax.Precision.HIGHEST)
+    outer = jnp.einsum("eta,etb->eab", total[..., :64], total[..., 64:], precision=lax.Precision.HIGH)
     feats = outer.reshape(8, 4096) / jnp.sqrt(jnp.float32(SEQ))
     features = lax.dynamic_slice_in_dim(feats, ex // 4 * 2 + par // 8, 1, 0)
 

time: 94.2 us -> 94 us (level)
  no operation moved by 1% of the time
where the time goes in v6:
time: 94 us; the launch traced here: 93.8 us
  blocking collectives  38.6 us (41%)
  starting transfers between devices  25.2 us (27%)
  Pallas kernels  12.5 us (13%)
  waiting for transfers between devices  12.2 us (13%)
  matrix products  3.22 us (3%)
  local copies, waits for them, and re-layouts  0.95 us (1%)
    ppermute x16, starting transfers between devices, send(): return lax.ppermute(value, BOTH, pairs(move))  25.2 us
    all_to_all x1, blocking collectives, on_device(): lax.all_to_all(feats, BOTH, 0, 0, axis_index_groups=PLANES)  18.2 us
    all_to_all x1, blocking collectives, on_device(): lax.all_to_all(part, BOTH, 0, 0, axis_index_groups=LINES)  12.7 us
    pallas_call x5, Pallas kernels, call(): pl.pallas_call(kernel, out_shape=[VMEM(shape, dtype) for shape, dtype in...  12.5 us
    ppermute x16, waiting for transfers between devices, send(): return lax.ppermute(value, BOTH, pairs(move))  12.2 us
    all_to_all x1, blocking collectives, on_device(): shares = lax.all_to_all(shares, BOTH, 0, 0, axis_index_groups=SQUARES)  7.67 us
    dot_general x1, matrix products, on_device(): jnp.dot(mine.T, feats, preferred_element_type=jnp.float32) * (1.0 / 256)  2.77 us
  transfers between devices with their start and end apart: 16, of which 4 were waited for; matrix products, arithmetic and copies ran while one was open for 1% of the time, Pallas kernels for 12%

profile of v6, /device:TPU:1, one launch (start us, length us, event | category | flops | bytes accessed | tf_op | source)
XLA Modules:
  0.0 93.8 jit_solution(10536695286699133539)
XLA Ops:
  0.6 3.3 %collective-permute-start.1 = (bf16[512,256]{1,0:T(8,128)(2,1)}, bf16[512,256]{1,0:T(8,128)(2,1)S(1)}, u32[]{:S(2)}, u32[]{:S(2)}) collective-permute-start(bf16[512,256]{1,0:T(8,128)(2,1)} %inputs.1), channel_id=1, source_target_pairs={{0,1},{1,0},{2,3},{3,2},{4,5},{5,4},{6,7},{7,6},{16,17},{17,16},{1... | collective-permute-start | bytes 786440 | tf_op jit(solution)/shard_map/ppermute | solution.py:29
  4.0 5.2 %collective-permute-start = (bf16[512,256]{1,0:T(8,128)(2,1)}, bf16[512,256]{1,0:T(8,128)(2,1)S(1)}, u32[]{:S(2)}, u32[]{:S(2)}) collective-permute-start(bf16[512,256]{1,0:T(8,128)(2,1)} %inputs.1), channel_id=1, source_target_pairs={{0,8},{1,9},{2,10},{3,11},{4,12},{5,13},{6,14},{7,15},{16,24},{17,... | collective-permute-start | bytes 786440 | tf_op jit(solution)/shard_map/ppermute | solution.py:29
  9.2 0.1 add_multiply_fusion
  9.2 0.1 add_multiply_fusion.1
  9.3 0.1 broadcast_add_fusion.1
  9.4 0.0 collective-permute-done.1.second
  9.4 1.2 %collective-permute-start.3 = (bf16[512,256]{1,0:T(8,128)(2,1)}, bf16[512,256]{1,0:T(8,128)(2,1)S(1)}, u32[]{:S(2)}, u32[]{:S(2)}) collective-permute-start(bf16[512,256]{1,0:T(8,128)(2,1)} %inputs.1), channel_id=1, source_target_pairs={{0,2},{1,3},{2,4},{3,5},{4,6},{5,7},{6,0},{7,1},{16,18},{17,19},{1... | collective-permute-start | bytes 786440 | tf_op jit(solution)/shard_map/ppermute | solution.py:29
  10.6 1.5 %collective-permute-start.4 = (bf16[512,256]{1,0:T(8,128)(2,1)}, bf16[512,256]{1,0:T(8,128)(2,1)S(1)}, u32[]{:S(2)}, u32[]{:S(2)}) collective-permute-start(bf16[512,256]{1,0:T(8,128)(2,1)} %inputs.1), channel_id=1, source_target_pairs={{0,6},{1,7},{2,0},{3,1},{4,2},{5,3},{6,4},{7,5},{16,22},{17,23},{1... | collective-permute-start | bytes 786440 | tf_op jit(solution)/shard_map/ppermute | solution.py:29
  12.1 1.5 %collective-permute-start.5 = (bf16[512,256]{1,0:T(8,128)(2,1)}, bf16[512,256]{1,0:T(8,128)(2,1)S(1)}, u32[]{:S(2)}, u32[]{:S(2)}) collective-permute-start(bf16[512,256]{1,0:T(8,128)(2,1)} %inputs.1), channel_id=1, source_target_pairs={{0,4},{1,5},{2,6},{3,7},{4,0},{5,1},{6,2},{7,3},{16,20},{17,21},{1... | collective-permute-start | bytes 786440 | tf_op jit(solution)/shard_map/ppermute | solution.py:29
  13.6 0.1 broadcast_add_fusion
  13.7 0.1 add.90
  13.8 0.1 pad_add_fusion.starts
  13.8 5.3 %stage.1 = (bf16[512,256]{1,0:T(8,128)(2,1)S(1)}, bf16[1376,512]{1,0:T(8,128)(2,1)S(1)}, bf16[1376,1536]{1,0:T(8,128)(2,1)S(1)}, bf16[1376,1536]{1,0:T(8,128)(2,1)S(1)}, bf16[1376,512]{1,0:T(8,128)(2,1)S(1)}) custom-call(s32[18]{0:T(128)S(1)} %pad_add_fusion.starts, bf16[512,256]{1,0:T(8,128)(2,1)} %inputs.1, bf16[688,4096]{1,0:T(8,128)(2,1)} %bitcast.20, ...), custom_call_target="tpu_custom_call" | custom-call | tf_op jit(solution)/shard_map/stage/pallas_call | solution.py:118
  19.1 0.4 collective-permute-start.11
  19.5 2.4 %collective-permute-start.13 = (bf16[512,256]{1,0:T(8,128)(2,1)S(1)}, bf16[512,256]{1,0:T(8,128)(2,1)S(1)}, u32[]{:S(2)}, u32[]{:S(2)}) collective-permute-start(bf16[512,256]{1,0:T(8,128)(2,1)S(1)} %collective-permute-done.refs_0_), channel_id=1, source_target_pairs={{0,6},{1,7},{2,0},{3,1},{4,2},{5,3},{6,4},{7,5},{16,22},{17,23},{1... | collective-permute-start | bytes 786440 | tf_op jit(solution)/shard_map/ppermute | solution.py:29
  21.9 3.1 %collective-permute-done.5.refs_4_ = bf16[512,256]{1,0:T(8,128)(2,1)S(1)} collective-permute-done((bf16[512,256]{1,0:T(8,128)(2,1)}, bf16[512,256]{1,0:T(8,128)(2,1)S(1)}, u32[]{:S(2)}, u32[]{:S(2)}) %collective-permute-start.5) | collective-permute-done | bytes 262176 | tf_op jit(solution)/shard_map/ppermute | solution.py:29
  25.0 2.0 %collective-permute-start.6 = (bf16[512,256]{1,0:T(8,128)(2,1)S(1)}, bf16[512,256]{1,0:T(8,128)(2,1)S(1)}, u32[]{:S(2)}, u32[]{:S(2)}) collective-permute-start(bf16[512,256]{1,0:T(8,128)(2,1)S(1)} %collective-permute-done.3.refs_0_), channel_id=1, source_target_pairs={{0,1},{1,0},{2,3},{3,2},{4,5},{5,4},{6,7},{7,6},{16,17},{17,16},{1... | collective-permute-start | bytes 786440 | tf_op jit(solution)/shard_map/ppermute | solution.py:29
  27.0 0.0 collective-permute-start.7
  27.0 0.5 collective-permute-start.8
  27.5 3.8 %collective-permute-done.11.refs_2_ = bf16[512,256]{1,0:T(8,128)(2,1)S(1)} collective-permute-done((bf16[512,256]{1,0:T(8,128)(2,1)S(1)}, bf16[512,256]{1,0:T(8,128)(2,1)S(1)}, u32[]{:S(2)}, u32[]{:S(2)}) %collective-permute-start.11) | collective-permute-done | bytes 262176 | tf_op jit(solution)/shard_map/ppermute | solution.py:29
  31.3 0.6 collective-permute-start.2
  31.8 0.9 own.1.refs_7_
  32.8 0.0 copy-start
  32.8 0.0 copy-start.2
  32.8 0.0 collective-permute-done.13.refs_4_
  32.8 0.8 collective-permute-start.10
  33.6 0.1 collective-permute-start.12
  33.7 0.0 collective-permute-done.7.refs_3_
  33.7 0.4 collective-permute-start.14
  34.2 2.4 %near.1.refs_7_ = f32[1376,512]{1,0:T(8,128)S(1)} custom-call(bf16[512,256]{1,0:T(8,128)(2,1)S(1)} %collective-permute-done.3.refs_0_, bf16[512,256]{1,0:T(8,128)(2,1)S(1)} %collective-permute-done.6.refs_1_, bf16[512,256]{1,0:T(8,128)(2,1)S(1)} %collective-permute-done.4.refs_2_, bf16[512,256]{1,0:T(8,128)(2,1)S(1)} %collective-permute-done.7.refs_3_, ...), custom_call_target="tpu_custom_call" | custom-call | flops 2164260864 | tf_op jit(solution)/shard_map/near/pallas_call | solution.py:118
  36.5 3.6 %collective-permute-done.2.first = bf16[512,256]{1,0:T(8,128)(2,1)S(1)} collective-permute-done((bf16[512,256]{1,0:T(8,128)(2,1)S(1)}, bf16[512,256]{1,0:T(8,128)(2,1)S(1)}, u32[]{:S(2)}, u32[]{:S(2)}) %collective-permute-start.2) | collective-permute-done | bytes 262176 | tf_op jit(solution)/shard_map/ppermute | solution.py:29
  40.2 1.3 %collective-permute-start.9 = (bf16[512,256]{1,0:T(8,128)(2,1)S(1)}, bf16[512,256]{1,0:T(8,128)(2,1)S(1)}, u32[]{:S(2)}, u32[]{:S(2)}) collective-permute-start(bf16[512,256]{1,0:T(8,128)(2,1)S(1)} %collective-permute-done.2.first), channel_id=1, source_target_pairs={{0,1},{1,0},{2,3},{3,2},{4,5},{5,4},{6,7},{7,6},{16,17},{17,16},{1... | collective-permute-start | bytes 786440 | tf_op jit(solution)/shard_map/ppermute | solution.py:29
  41.5 0.0 collective-permute-done.10.refs_1_
  41.5 0.0 collective-permute-done.12.refs_3_
  41.5 0.0 copy-start.1
  41.5 2.4 %middle.1 = (f32[1376,512]{1,0:T(8,128)S(1)}, f32[512,64]{1,0:T(8,128)S(1)}) custom-call(bf16[512,256]{1,0:T(8,128)(2,1)S(1)} %copy-done, bf16[64,256]{1,0:T(8,128)(2,1)S(1)} %bitcast.17, bf16[512,256]{1,0:T(8,128)(2,1)S(1)} %collective-permute-done.refs_0_, bf16[512,256]{1,0:T(8,128)(2,1)S(1)} %collective-permute-done.10.refs_1_, ...), custom_call_target="tpu_custom_call" | custom-call | flops 2164260864 | tf_op jit(solution)/shard_map/middle/pallas_call | solution.py:118
  43.9 0.0 collective-permute-done.9.second
  44.0 1.5 %last.1 = bf16[8,2,32,128]{3,2,1,0:T(8,128)(2,1)S(1)} custom-call(bf16[64,688]{1,0:T(8,128)(2,1)S(1)} %bitcast.16, bf16[512,256]{1,0:T(8,128)(2,1)S(1)} %collective-permute-done.2.first, bf16[512,256]{1,0:T(8,128)(2,1)S(1)} %collective-permute-done.9.second, bf16[1376,512]{1,0:T(8,128)(2,1)S(1)} %get-tuple-element.42.weights, ...), custom_call_target="tpu_custom_call" | custom-call | flops 721420288 | tf_op jit(solution)/shard_map/last/pallas_call | solution.py:118
  45.4 7.7 %all_to_all.15 = bf16[8,2,32,128]{3,2,1,0:T(8,128)(2,1)S(1)} all-to-all(bf16[8,2,32,128]{3,2,1,0:T(8,128)(2,1)S(1)} %last.1), channel_id=1, replica_groups={{0,1,2,3,4,5,6,7},{16,17,18,19,20,21,22,23},{32,33,34,35,36,37,38,39},{..., dimensions={0} | all-to-all | bytes 262144 | tf_op jit(solution)/shard_map/all_to_all | solution.py:205
  53.2 12.7 %all_to_all.16 = bf16[8,2,32,128]{3,2,1,0:T(8,128)(2,1)S(1)} all-to-all(bf16[8,2,32,128]{3,2,1,0:T(8,128)(2,1)S(1)} %broadcast_in_dim.4), channel_id=1, replica_groups={{0,64,128,192,8,72,136,200},{1,65,129,193,9,73,137,201},{2,66,130,194,1..., dimensions={0} | all-to-all | bytes 262144 | tf_op jit(solution)/shard_map/all_to_all | solution.py:209
  65.9 0.5 convolution_multiply_fusion.1
  66.4 0.1 div.45
  66.5 0.1 broadcast_in_dim.5
  66.6 18.2 %all_to_all.17 = bf16[16,8,4096]{2,1,0:T(8,128)(2,1)S(1)} all-to-all(bf16[16,8,4096]{2,1,0:T(8,128)(2,1)S(1)} %broadcast_in_dim.5), channel_id=1, replica_groups={{0,18,36,54,16,34,52,6,32,50,4,22,48,2,20,38},{1,19,37,55,17,35,53,7,33..., dimensions={0} | all-to-all | bytes 2097152 | tf_op jit(solution)/shard_map/all_to_all | solution.py:216
  84.8 3.9 %collective-permute-start.15 = (bf16[128,4096]{1,0:T(8,128)(2,1)S(1)}, bf16[128,4096]{1,0:T(8,128)(2,1)S(1)}, u32[]{:S(2)}, u32[]{:S(2)}) collective-permute-start(bf16[128,4096]{1,0:T(8,128)(2,1)S(1)} %bitcast.18), channel_id=1, source_target_pairs={{0,1},{1,0},{2,3},{3,2},{4,5},{5,4},{6,7},{7,6},{16,17},{17,16},{1... | collective-permute-start | bytes 3145736 | tf_op jit(solution)/shard_map/ppermute | solution.py:29
  88.7 0.6 constant_dynamic-slice_fusion
  89.4 1.7 %collective-permute-done.15 = bf16[128,4096]{1,0:T(8,128)(2,1)S(1)} collective-permute-done((bf16[128,4096]{1,0:T(8,128)(2,1)S(1)}, bf16[128,4096]{1,0:T(8,128)(2,1)S(1)}, u32[]{:S(2)}, u32[]{:S(2)}) %collective-permute-start.15) | collective-permute-done | bytes 1048608 | tf_op jit(solution)/shard_map/ppermute | solution.py:29
  91.0 2.8 %convolution_multiply_fusion = f32[256,4096]{1,0:T(8,128)} fusion(bf16[128,4096]{1,0:T(8,128)(2,1)S(1)} %collective-permute-done.15, bf16[128,4096]{1,0:T(8,128)(2,1)S(1)} %bitcast.19, s32[]{:T(128)S(6)} %select_n.52), kind=kOutput, calls=%fused_computation | convolution fusion | flops 542375936 | bytes 8388612 | tf_op jit(solution)/shard_map/dot_general | solution.py:219
  (14 shorter events, 0.1 us)
Async XLA Ops:
  0.6 8.8 %collective-permute-start.1 = (bf16[512,256]{1,0:T(8,128)(2,1)}, bf16[512,256]{1,0:T(8,128)(2,1)S(1)}, u32[]{:S(2)}, u32[]{:S(2)}) collective-permute-start(bf16[512,256]{1,0:T(8,128)(2,1)} %inputs.1), channel_id=1, source_target_pairs={{0,1},{1,0},{2,3},{3,2},{4,5},{5,4},{6,7},{7,6},{16,17},{17,16},{1... | collective-permute-start | bytes 786440 | tf_op jit(solution)/shard_map/ppermute | solution.py:29
  4.0 15.2 %collective-permute-start = (bf16[512,256]{1,0:T(8,128)(2,1)}, bf16[512,256]{1,0:T(8,128)(2,1)S(1)}, u32[]{:S(2)}, u32[]{:S(2)}) collective-permute-start(bf16[512,256]{1,0:T(8,128)(2,1)} %inputs.1), channel_id=1, source_target_pairs={{0,8},{1,9},{2,10},{3,11},{4,12},{5,13},{6,14},{7,15},{16,24},{17,... | collective-permute-start | bytes 786440 | tf_op jit(solution)/shard_map/ppermute | solution.py:29
  9.4 12.5 %collective-permute-start.3 = (bf16[512,256]{1,0:T(8,128)(2,1)}, bf16[512,256]{1,0:T(8,128)(2,1)S(1)}, u32[]{:S(2)}, u32[]{:S(2)}) collective-permute-start(bf16[512,256]{1,0:T(8,128)(2,1)} %inputs.1), channel_id=1, source_target_pairs={{0,2},{1,3},{2,4},{3,5},{4,6},{5,7},{6,0},{7,1},{16,18},{17,19},{1... | collective-permute-start | bytes 786440 | tf_op jit(solution)/shard_map/ppermute | solution.py:29
  10.6 11.3 %collective-permute-start.4 = (bf16[512,256]{1,0:T(8,128)(2,1)}, bf16[512,256]{1,0:T(8,128)(2,1)S(1)}, u32[]{:S(2)}, u32[]{:S(2)}) collective-permute-start(bf16[512,256]{1,0:T(8,128)(2,1)} %inputs.1), channel_id=1, source_target_pairs={{0,6},{1,7},{2,0},{3,1},{4,2},{5,3},{6,4},{7,5},{16,22},{17,23},{1... | collective-permute-start | bytes 786440 | tf_op jit(solution)/shard_map/ppermute | solution.py:29
  12.1 12.9 %collective-permute-start.5 = (bf16[512,256]{1,0:T(8,128)(2,1)}, bf16[512,256]{1,0:T(8,128)(2,1)S(1)}, u32[]{:S(2)}, u32[]{:S(2)}) collective-permute-start(bf16[512,256]{1,0:T(8,128)(2,1)} %inputs.1), channel_id=1, source_target_pairs={{0,4},{1,5},{2,6},{3,7},{4,0},{5,1},{6,2},{7,3},{16,20},{17,21},{1... | collective-permute-start | bytes 786440 | tf_op jit(solution)/shard_map/ppermute | solution.py:29
  19.1 12.1 %collective-permute-start.11 = (bf16[512,256]{1,0:T(8,128)(2,1)S(1)}, bf16[512,256]{1,0:T(8,128)(2,1)S(1)}, u32[]{:S(2)}, u32[]{:S(2)}) collective-permute-start(bf16[512,256]{1,0:T(8,128)(2,1)S(1)} %collective-permute-done.refs_0_), channel_id=1, source_target_pairs={{0,2},{1,3},{2,4},{3,5},{4,6},{5,7},{6,0},{7,1},{16,18},{17,19},{1... | collective-permute-start | bytes 786440 | tf_op jit(solution)/shard_map/ppermute | solution.py:29
  19.5 13.3 %collective-permute-start.13 = (bf16[512,256]{1,0:T(8,128)(2,1)S(1)}, bf16[512,256]{1,0:T(8,128)(2,1)S(1)}, u32[]{:S(2)}, u32[]{:S(2)}) collective-permute-start(bf16[512,256]{1,0:T(8,128)(2,1)S(1)} %collective-permute-done.refs_0_), channel_id=1, source_target_pairs={{0,6},{1,7},{2,0},{3,1},{4,2},{5,3},{6,4},{7,5},{16,22},{17,23},{1... | collective-permute-start | bytes 786440 | tf_op jit(solution)/shard_map/ppermute | solution.py:29
  25.0 8.7 %collective-permute-start.6 = (bf16[512,256]{1,0:T(8,128)(2,1)S(1)}, bf16[512,256]{1,0:T(8,128)(2,1)S(1)}, u32[]{:S(2)}, u32[]{:S(2)}) collective-permute-start(bf16[512,256]{1,0:T(8,128)(2,1)S(1)} %collective-permute-done.3.refs_0_), channel_id=1, source_target_pairs={{0,1},{1,0},{2,3},{3,2},{4,5},{5,4},{6,7},{7,6},{16,17},{17,16},{1... | collective-permute-start | bytes 786440 | tf_op jit(solution)/shard_map/ppermute | solution.py:29
  27.0 6.8 %collective-permute-start.7 = (bf16[512,256]{1,0:T(8,128)(2,1)S(1)}, bf16[512,256]{1,0:T(8,128)(2,1)S(1)}, u32[]{:S(2)}, u32[]{:S(2)}) collective-permute-start(bf16[512,256]{1,0:T(8,128)(2,1)S(1)} %collective-permute-done.4.refs_2_), channel_id=1, source_target_pairs={{0,1},{1,0},{2,3},{3,2},{4,5},{5,4},{6,7},{7,6},{16,17},{17,16},{1... | collective-permute-start | bytes 786440 | tf_op jit(solution)/shard_map/ppermute | solution.py:29
  27.0 7.2 %collective-permute-start.8 = (bf16[512,256]{1,0:T(8,128)(2,1)S(1)}, bf16[512,256]{1,0:T(8,128)(2,1)S(1)}, u32[]{:S(2)}, u32[]{:S(2)}) collective-permute-start(bf16[512,256]{1,0:T(8,128)(2,1)S(1)} %collective-permute-done.5.refs_4_), channel_id=1, source_target_pairs={{0,1},{1,0},{2,3},{3,2},{4,5},{5,4},{6,7},{7,6},{16,17},{17,16},{1... | collective-permute-start | bytes 786440 | tf_op jit(solution)/shard_map/ppermute | solution.py:29
  31.3 8.9 %collective-permute-start.2 = (bf16[512,256]{1,0:T(8,128)(2,1)S(1)}, bf16[512,256]{1,0:T(8,128)(2,1)S(1)}, u32[]{:S(2)}, u32[]{:S(2)}) collective-permute-start(bf16[512,256]{1,0:T(8,128)(2,1)S(1)} %collective-permute-done.refs_0_), channel_id=1, source_target_pairs={{0,4},{1,5},{2,6},{3,7},{4,0},{5,1},{6,2},{7,3},{16,20},{17,21},{1... | collective-permute-start | bytes 786440 | tf_op jit(solution)/shard_map/ppermute | solution.py:29
  32.8 8.7 %copy-start = (bf16[512,256]{1,0:T(8,128)(2,1)S(1)}, bf16[512,256]{1,0:T(8,128)(2,1)}, u32[]{:S(2)}) copy-start(bf16[512,256]{1,0:T(8,128)(2,1)} %grads.1) | copy-start | bytes 786436
  32.8 8.7 %copy-start.2 = (bf16[256,64]{0,1:T(8,128)(2,1)S(1)}, bf16[256,64]{0,1:T(8,128)(2,1)}, u32[]{:S(2)}) copy-start(bf16[256,64]{0,1:T(8,128)(2,1)} %param.11) | copy-start | bytes 98308
  32.8 8.7 %collective-permute-start.10 = (bf16[512,256]{1,0:T(8,128)(2,1)S(1)}, bf16[512,256]{1,0:T(8,128)(2,1)S(1)}, u32[]{:S(2)}, u32[]{:S(2)}) collective-permute-start(bf16[512,256]{1,0:T(8,128)(2,1)S(1)} %collective-permute-done.refs_0_), channel_id=1, source_target_pairs={{0,1},{1,0},{2,3},{3,2},{4,5},{5,4},{6,7},{7,6},{16,17},{17,16},{1... | collective-permute-start | bytes 786440 | tf_op jit(solution)/shard_map/ppermute | solution.py:29
  33.6 7.9 %collective-permute-start.12 = (bf16[512,256]{1,0:T(8,128)(2,1)S(1)}, bf16[512,256]{1,0:T(8,128)(2,1)S(1)}, u32[]{:S(2)}, u32[]{:S(2)}) collective-permute-start(bf16[512,256]{1,0:T(8,128)(2,1)S(1)} %collective-permute-done.11.refs_2_), channel_id=1, source_target_pairs={{0,1},{1,0},{2,3},{3,2},{4,5},{5,4},{6,7},{7,6},{16,17},{17,16},{1... | collective-permute-start | bytes 786440 | tf_op jit(solution)/shard_map/ppermute | solution.py:29
  33.7 7.8 %collective-permute-start.14 = (bf16[512,256]{1,0:T(8,128)(2,1)S(1)}, bf16[512,256]{1,0:T(8,128)(2,1)S(1)}, u32[]{:S(2)}, u32[]{:S(2)}) collective-permute-start(bf16[512,256]{1,0:T(8,128)(2,1)S(1)} %collective-permute-done.13.refs_4_), channel_id=1, source_target_pairs={{0,1},{1,0},{2,3},{3,2},{4,5},{5,4},{6,7},{7,6},{16,17},{17,16},{1... | collective-permute-start | bytes 786440 | tf_op jit(solution)/shard_map/ppermute | solution.py:29
  40.2 3.8 %collective-permute-start.9 = (bf16[512,256]{1,0:T(8,128)(2,1)S(1)}, bf16[512,256]{1,0:T(8,128)(2,1)S(1)}, u32[]{:S(2)}, u32[]{:S(2)}) collective-permute-start(bf16[512,256]{1,0:T(8,128)(2,1)S(1)} %collective-permute-done.2.first), channel_id=1, source_target_pairs={{0,1},{1,0},{2,3},{3,2},{4,5},{5,4},{6,7},{7,6},{16,17},{17,16},{1... | collective-permute-start | bytes 786440 | tf_op jit(solution)/shard_map/ppermute | solution.py:29
  41.5 2.4 %copy-start.1 = (bf16[688,64]{0,1:T(8,128)(2,1)S(1)}, bf16[688,64]{0,1:T(8,128)(2,1)}, u32[]{:S(2)}) copy-start(bf16[688,64]{0,1:T(8,128)(2,1)} %param.10) | copy-start | bytes 264196
  84.8 6.2 %collective-permute-start.15 = (bf16[128,4096]{1,0:T(8,128)(2,1)S(1)}, bf16[128,4096]{1,0:T(8,128)(2,1)S(1)}, u32[]{:S(2)}, u32[]{:S(2)}) collective-permute-start(bf16[128,4096]{1,0:T(8,128)(2,1)S(1)} %bitcast.18), channel_id=1, source_target_pairs={{0,1},{1,0},{2,3},{3,2},{4,5},{5,4},{6,7},{7,6},{16,17},{17,16},{1... | collective-permute-start | bytes 3145736 | tf_op jit(solution)/shard_map/ppermute | solution.py:29
